TPU v7x, 32 devices: a whole 2x2x4 slice. The times are simulated.
32 devices in a mesh: req: 8 (over z, y), mp: 4 (over x, core).
Axes of the slice: x: 2, y: 2, z: 4, core: 2. Of those that a mesh axis runs over, the one named last changes fastest.
Arguments:
- hidden_in: bfloat16 [4096, 2048], P(('req', 'mp')), may hold values from -48 to 48
- segment_ids: int32 [8, 512], replicated, may hold values from 0 to 2, never falling along the last dimension, each value on 1 to 256 neighbouring positions
- request_prompt: int32 [256], P('req'), may hold values from 0 to 23, as said below
- page_table: int32 [256, 16], P('req'), may hold values from 0 to 511, as said below
- ln_attn: bfloat16 [2048], replicated, may hold values from 0.5 to 1.5
- w_query: bfloat16 [2048, 2048], P(None, 'mp'), may hold values from -0.125 to 0.125
- w_key: bfloat16 [2048, 1024], P(None, 'mp'), may hold values from -0.125 to 0.125
- w_value: bfloat16 [2048, 1024], P(None, 'mp'), may hold values from -0.125 to 0.125
- q_gain: bfloat16 [128], replicated, may hold values from 0.5 to 1.5
- k_gain: bfloat16 [128], replicated, may hold values from 0.5 to 1.5
- w_out: bfloat16 [2048, 2048], P('mp'), may hold values from -0.125 to 0.125
- ln_mlp: bfloat16 [2048], replicated, may hold values from 0.5 to 1.5
- w_gate: bfloat16 [2048, 3072], P(None, 'mp'), may hold values from -0.125 to 0.125
- w_up: bfloat16 [2048, 3072], P(None, 'mp'), may hold values from -0.125 to 0.125
- w_down: bfloat16 [3072, 2048], P('mp'), may hold values from -0.109375 to 0.109375
Outputs:
- layer_out: bfloat16 [4096, 2048], P(('req', 'mp'))
- kv_pages: bfloat16 [4096, 16, 8, 256], P('req', None, 'mp')
Inputs may be any that keep to these rules, and one draw needn't show every extreme that they name: `request_prompt`: every prompt is continued by 8 to 16 requests, and some prompt by exactly 16. `page_table`: the 32 rows of one index of req name each of the 512 pages once.
All inputs are finite; a program needn't handle non-finite values.
Results may differ from a plain program's by a relative error of at most 0.0075.
Values may be sent and summed in bfloat16 or wider, within the bound.
No kernel may reach another device: no remote copies, remote signals or barrier semaphores. Data moves between devices by JAX's collectives and lax.ppermute only.
A program may use at most 128 MiB of HBM per device.

v0:
```python
import math

import jax
import jax.numpy as jnp
from jax import lax
from jax.sharding import PartitionSpec as P

HD = 128
PROMPTS_DEV = 3
PAGE = 16


EPS = 1e-06
THETA = 1000000.0


def rms_scale(values, gain):
    wide = values.astype(jnp.float32)
    return (
        wide
        * lax.rsqrt(jnp.mean(wide * wide, axis=-1, keepdims=True) + EPS)
        * gain.astype(jnp.float32)
    )


def segment_table(segment_row):
    member = (segment_row[:, None] == jnp.arange(PROMPTS_DEV, dtype=jnp.int32)[None, :]).astype(
        jnp.int32
    )
    lengths = jnp.sum(member, axis=0)
    starts = jnp.cumsum(lengths) - lengths
    index = jnp.arange(segment_row.shape[0], dtype=jnp.int32)
    position = index - jnp.sum(member * starts[None, :], axis=1)
    return (starts, lengths, position)


def rotate(values, position):
    half = HD // 2
    freq = THETA ** (-(jnp.arange(half, dtype=jnp.float32) * 2.0) / HD)
    angle = position.astype(jnp.float32)[:, None] * freq[None, :]
    cosine = jnp.cos(angle)[:, None, :]
    sine = jnp.sin(angle)[:, None, :]
    first = values[..., :half]
    second = values[..., half:]
    return jnp.concatenate(
        [first * cosine - second * sine, second * cosine + first * sine], axis=-1
    )


def body(
    hidden_in,
    segment_ids,
    request_prompt,
    page_table,
    ln_attn,
    w_query,
    w_key,
    w_value,
    q_gain,
    k_gain,
    w_out,
    ln_mlp,
    w_gate,
    w_up,
    w_down,
):
    parts = lax.axis_size("mp")
    owner_rows = hidden_in.shape[0]
    seq_rows = owner_rows * parts
    heads_here = w_query.shape[1] // HD
    kv_here = w_key.shape[1] // HD
    group = heads_here // kv_here
    group_index = lax.axis_index("req")
    segment_row = lax.dynamic_index_in_dim(segment_ids, group_index, 0, keepdims=False)
    unused_starts, unused_lengths, position = segment_table(segment_row)
    piece = lax.all_gather(hidden_in, "mp", axis=0, tiled=True)
    count = piece.shape[0]
    normed = rms_scale(piece, ln_attn).astype(jnp.bfloat16)
    query = jnp.dot(normed, w_query, preferred_element_type=jnp.float32).reshape(
        count, heads_here, HD
    )
    project_key = jnp.dot(normed, w_key, preferred_element_type=jnp.float32).reshape(
        count, kv_here, HD
    )
    project_value = jnp.dot(normed, w_value, preferred_element_type=jnp.float32).astype(
        jnp.bfloat16
    )
    query = (
        rotate(rms_scale(query, q_gain), position)
        .astype(jnp.bfloat16)
        .reshape(count, heads_here * HD)
    )
    project_key = (
        rotate(rms_scale(project_key, k_gain), position)
        .astype(jnp.bfloat16)
        .reshape(count, kv_here * HD)
    )
    joined = [query, project_key, project_value]
    projected = jnp.concatenate(joined, axis=1)
    query_width = heads_here * HD
    key_width = kv_here * HD
    query = projected[:, :query_width].reshape(seq_rows, kv_here, group, HD)
    key = projected[:, query_width : query_width + key_width].reshape(seq_rows, kv_here, HD)
    value = projected[:, query_width + key_width : query_width + 2 * key_width].reshape(
        seq_rows, kv_here, HD
    )
    block = min(512, seq_rows)
    blocks = seq_rows // block
    key_index = jnp.arange(seq_rows, dtype=jnp.int32)

    def attend_block(inputs):
        query_block, first = inputs
        scores = jnp.einsum(
            "qcgd,kcd->cgqk", query_block, key, preferred_element_type=jnp.float32
        ) / math.sqrt(HD)
        row_index = first + jnp.arange(block, dtype=jnp.int32)
        allowed = (segment_row[:, None] == segment_row[None, :]) & (
            key_index[None, :] <= row_index[:, None]
        )
        raised = jnp.where(allowed[None, None], jnp.exp(scores), 0.0)
        weights = (raised / jnp.sum(raised, axis=-1, keepdims=True)).astype(jnp.bfloat16)
        mixed = jnp.einsum("cgqk,kcd->qcgd", weights, value, preferred_element_type=jnp.float32)
        return mixed.astype(jnp.bfloat16).reshape(block, query_width)

    attended = lax.map(
        attend_block,
        (
            query.reshape(blocks, block, kv_here, group, HD),
            jnp.arange(blocks, dtype=jnp.int32) * block,
        ),
    )
    attended = attended.reshape(seq_rows, query_width)
    own_sum = lax.psum_scatter(
        jnp.dot(attended, w_out, preferred_element_type=jnp.float32).astype(jnp.bfloat16),
        "mp",
        scatter_dimension=0,
        tiled=True,
    ).astype(jnp.float32)
    after = (hidden_in.astype(jnp.float32) + own_sum).astype(jnp.bfloat16)
    normed_mlp = rms_scale(lax.all_gather(after, "mp", axis=0, tiled=True), ln_mlp).astype(
        jnp.bfloat16
    )
    gate = jnp.dot(normed_mlp, w_gate, preferred_element_type=jnp.float32)
    upper = jnp.dot(normed_mlp, w_up, preferred_element_type=jnp.float32)
    hidden = (jax.nn.silu(gate) * upper).astype(jnp.bfloat16)
    result = (
        after.astype(jnp.float32)
        + lax.psum_scatter(
            jnp.dot(hidden, w_down, preferred_element_type=jnp.float32).astype(jnp.bfloat16),
            "mp",
            scatter_dimension=0,
            tiled=True,
        ).astype(jnp.float32)
    ).astype(jnp.bfloat16)
    pairs = jnp.concatenate([key, value], axis=-1)
    all_starts, all_lengths, unused = jax.vmap(segment_table)(segment_ids)
    prompts = segment_ids.shape[0] * PROMPTS_DEV
    catalog = jnp.arange(prompts, dtype=jnp.int32)
    most_pages = page_table.shape[1]
    pool_pages = page_table.shape[0] * most_pages
    owner = (
        jnp.zeros((pool_pages,), jnp.int32)
        .at[page_table.reshape(-1)]
        .set(jnp.arange(pool_pages, dtype=jnp.int32))
    )
    request = owner // most_pages
    page = owner % most_pages
    picks = (request_prompt[:, None] == catalog[None, :]).astype(jnp.int32)
    request_begin = request_prompt // PROMPTS_DEV * seq_rows + jnp.sum(
        picks * all_starts.reshape(-1)[None, :], axis=1
    )
    request_length = jnp.sum(picks * all_lengths.reshape(-1)[None, :], axis=1)
    begin = request_begin[request]
    length = request_length[request]
    offset = page[:, None] * PAGE + jnp.arange(PAGE, dtype=jnp.int32)[None, :]
    valid = offset < length[:, None]
    source = jnp.where(valid, begin[:, None] + offset, 0)
    everything = lax.all_gather(pairs, "req", axis=0, tiled=True)
    taken = everything[source]
    cache = jnp.where(valid[:, :, None, None], taken, jnp.zeros((), jnp.bfloat16))
    return (result, cache)


def solution(mesh):
    return jax.shard_map(
        body,
        mesh=mesh,
        in_specs=(
            P(("req", "mp"), None),
            P(),
            P("req"),
            P("req", None),
            P(),
            P(None, "mp"),
            P(None, "mp"),
            P(None, "mp"),
            P(),
            P(),
            P("mp", None),
            P(),
            P(None, "mp"),
            P(None, "mp"),
            P("mp", None),
        ),
        out_specs=(P(("req", "mp"), None), P("req", None, "mp", None)),
        check_vma=False,
    )
```

profile of v0, /device:TPU:0, one launch (start us, length us, event | category | flops | bytes accessed | tf_op | source)
XLA Modules:
  0.0 282.0 jit_solution(9156071753110858922)
XLA Ops:
  7.2 0.7 all-gather.4.cloned.1.call-update
  8.0 0.8 convert_element_type.91
  8.8 0.7 convert_element_type.88
  9.4 0.7 constant_dynamic-slice_fusion
  10.2 0.1 convert_reduce_fusion.1
  10.3 0.2 reduce-window.8
  10.5 0.7 convert_element_type.85
  11.2 0.1 select_reduce_fusion.2
  11.3 0.5 multiply_cosine_fusion
  11.8 0.8 copy.59
  12.6 0.9 copy.60
  13.5 0.9 fusion.9
  14.4 20.5 %all-gather.4.cloned.1.call-done = bf16[512,2048]{1,0:T(8,128)(2,1)} async-done(((bf16[128,2048]{1,0:T(8,128)(2,1)}), bf16[512,2048]{1,0:T(8,128)(2,1)}) %all-gather.4.cloned.1.call-update) | async-done | bytes 2097168 | tf_op jit(solution)/shard_map/all_gather | solution.py:76
  34.9 2.1 fusion
  37.0 3.6 %multiply_reduce_fusion = (f32[512,4]{0,1:T(4,128)S(1)}, f32[512,512]{0,1:T(8,128)S(1)}) fusion(bf16[2048,512]{1,0:T(8,128)(2,1)} %param.20, bf16[512,2048]{1,0:T(8,128)(2,1)} %all-gather.4.cloned.1.call-done, f32[2048]{0:T(1024)S(1)} %convert_element_type.85, f32[512]{0:T(512)S(1)} %add_rsqrt_fusion.3), kind=kOutput, calls=%fused_computation.25 | convolution fusion | flops 1078458368 | bytes 5261312 | tf_op jit(solution)/shard_map/dot_general | solution.py:79
  40.6 0.2 multiply_multiply_fusion
  40.8 1.0 subtract_convert_fusion
  41.8 0.6 copy-done.1
  42.4 0.3 copy-done.15
  42.7 1.8 multiply_reduce_fusion.1
  44.4 2.0 copy.58
  46.5 2.0 copy.61
  48.4 1.0 copy.62
  49.4 1.3 multiply_multiply_fusion.1
  50.8 1.3 subtract_convert_fusion.1
  52.0 0.7 copy-done.4
  52.8 1.6 fusion.6
  54.4 0.3 copy-done.16
  54.7 0.9 convolution_convert_fusion.2
  55.7 1.3 fusion.8
  57.0 0.3 copy-done.14
  57.3 2.6 convolution_convert_fusion.1
  60.0 31.5 %reduce-scatter.3.cloned.1.call-done = bf16[128,2048]{1,0:T(8,128)(2,1)} async-done(((bf16[512,2048]{1,0:T(8,128)(2,1)}), bf16[128,2048]{1,0:T(8,128)(2,1)}) %reduce-scatter.3.cloned.1.call-update) | async-done | bytes 524304 | tf_op jit(solution)/shard_map/reduce_scatter | solution.py:133
  91.5 2.1 add_convert_fusion.1
  93.7 0.2 all-gather.8.cloned.1.call-start
  93.9 1.2 copy.66
  95.1 1.9 copy.67
  97.1 1.8 copy.68
  98.9 3.1 %pad_maximum_fusion = bf16[512,2,256]{2,1,0:T(2,128)(2,1)} fusion(bf16[512,2,128]{2,1,0:T(2,128)(2,1)} %copy.68, bf16[512,2,64]{2,1,0:T(2,128)(2,1)} %copy.67, bf16[512,2,64]{2,1,0:T(2,128)(2,1)S(1)} %copy.66), kind=kLoop, calls=%fused_computation.34 | loop fusion | flops 1572864 | bytes 1048576 | tf_op jit(solution)/shard_map/concatenate | solution.py:155
  102.1 0.1 reshape.378
  102.2 14.2 %all-gather.6.cloned.1.call-done = bf16[512,2048]{1,0:T(8,128)(2,1)} async-done(((bf16[128,2048]{1,0:T(8,128)(2,1)}), bf16[512,2048]{1,0:T(8,128)(2,1)}) %all-gather.6.cloned.1.call-update) | async-done | bytes 2097168 | tf_op jit(solution)/shard_map/all_gather | solution.py:140
  116.4 2.1 fusion.3
  118.5 5.5 %fusion.12 = f32[512,768]{1,0:T(8,128)} fusion(bf16[2048,768]{1,0:T(8,128)(2,1)} %param.27, bf16[512,2048]{1,0:T(8,128)(2,1)} %all-gather.6.cloned.1.call-done, f32[2048]{0:T(1024)S(1)} %convert_element_type.100, f32[512]{0:T(512)S(1)} %add_rsqrt_fusion.2), kind=kOutput, calls=%fused_computation.29 | convolution fusion | flops 1614807040 | bytes 6825984 | tf_op jit(solution)/shard_map/dot_general | solution.py:143
  124.0 8.7 %convolution_convert_fusion = bf16[512,2048]{1,0:T(8,128)(2,1)} fusion(bf16[768,2048]{1,0:T(8,128)(2,1)S(1)} %copy-done, f32[512,768]{1,0:T(8,128)} %fusion.12, bf16[2048,768]{1,0:T(8,128)(2,1)} %param.28, bf16[512,2048]{1,0:T(8,128)(2,1)} %all-gather.6.cloned.1.call-done, f32[2048]{0:T(1024)S(1)} %convert_element_type.100, f32[512]{0:T(512)S(1)} %add_rsqrt_fusion.2), kind=kOutput, calls=%fused_computation.16 | convolution fusion | flops 3228827648 | bytes 12068864 | tf_op jit(solution)/shard_map/dot_general | solution.py:149
  132.7 0.1 convert_reduce_fusion
  132.9 0.1 copy.65
  133.0 0.1 mul.252
  133.1 0.1 copy.69
  133.2 0.1 reduce_window_sum.21
  133.3 2.4 scatter_custom_fusion
  135.7 0.1 select_reduce_fusion.1
  135.8 0.7 fusion.35
  136.5 0.7 fusion.37
  137.2 0.7 fusion.36
  137.9 0.7 fusion.34
  138.7 20.2 %select_select_fusion.1 = (s32[512]{0:T(512)S(1)}, pred[512]{0:T(512)(128)(4,1)S(1)}, pred[512]{0:T(512)(128)(4,1)S(1)}, pred[512]{0:T(512)(128)(4,1)S(1)}, pred...) fusion(s32[]{:T(128)} %bitcast.16, s32[]{:T(128)} %bitcast.17, ...), kind=kLoop, calls=%fused_computation.69 | loop fusion | flops 31744 | bytes 20096 | tf_op jit(solution)/shard_map/gather | solution.py:174
  158.9 20.1 %select_select_fusion = s32[512]{0:T(512)S(1)} fusion(pred[512]{0:T(512)(128)(4,1)S(1)} %get-tuple-element.56, pred[512]{0:T(512)(128)(4,1)S(1)} %get-tuple-element.55, pred[512]{0:T(512)(128)(4,1)S(1)} %get-tuple-element.54, pred[512]{0:T(512)(128)(4,1)S(1)} %get-tuple-element.53, pred[512]{0:T(512)(128)(4,1)S(1)} %get-tuple-element.52, ...), kind=kLoop, calls=%fused_computation.68 | loop fusion | flops 15872 | bytes 18048 | tf_op jit(solution)/shard_map/gather | solution.py:173
  178.9 0.3 compare_select_fusion
  179.2 0.1 reshape.459
  179.4 0.2 add_compare_fusion
  179.6 12.5 %all-gather.8.cloned.1.call-done = bf16[4096,2,256]{2,1,0:T(2,128)(2,1)} async-done(((bf16[512,2,256]{2,1,0:T(2,128)(2,1)}), bf16[4096,2,256]{2,1,0:T(2,128)(2,1)}) %all-gather.8.cloned.1.call-update) | async-done | bytes 4194320 | tf_op jit(solution)/shard_map/all_gather | solution.py:178
  192.1 66.7 %gather_fusion = bf16[8192,2,256]{2,1,0:T(2,128)(2,1)} fusion(bf16[4096,2,256]{2,1,0:T(2,128)(2,1)} %all-gather.8.cloned.1.call-done, s32[8192]{0:T(1024)S(1)} %broadcast_clamp_fusion), kind=kCustom, calls=%fused_computation | custom fusion | bytes 16809984 | tf_op jit(solution)/shard_map/gather | solution.py:179
  258.8 14.5 %broadcast_select_fusion = bf16[512,16,2,256]{3,2,1,0:T(2,128)(2,1)} fusion(bf16[512,16,2,256]{3,2,1,0:T(2,128)(2,1)} %bitcast.113, pred[512,16]{1,0:T(8,128)(4,1)S(1)} %add_compare_fusion), kind=kLoop, calls=%fused_computation.2 | loop fusion | flops 4194304 | bytes 16785408 | tf_op jit(solution)/shard_map/jit(_where)/select_n | solution.py:180
  273.3 2.1 add_convert_fusion
  (54 shorter events, 0.6 us)
Async XLA Ops:
  7.2 116.9 %copy-start = (bf16[768,2048]{1,0:T(8,128)(2,1)S(1)}, bf16[768,2048]{1,0:T(8,128)(2,1)}, u32[]{:S(2)}) copy-start(bf16[768,2048]{1,0:T(8,128)(2,1)} %param.29) | copy-start | bytes 9437188
  7.2 27.7 %all-gather.4.cloned.1.call-start = ((), (), s32[]{:S(2)}) async-start(), calls=%async_computation.2 | async-start | bytes 2621440 | tf_op jit(solution)/shard_map/all_gather | solution.py:76
  7.9 83.6 %reduce-scatter.3.cloned.1.call-start = ((), (), s32[]{:S(2)}) async-start(), calls=%async_computation.3 | async-start | bytes 2621440 | tf_op jit(solution)/shard_map/reduce_scatter | solution.py:133
  40.6 1.8 copy-start.1
  40.6 2.0 copy-start.15
  42.7 5.8 %copy-start.3 = (bf16[512,4,64]{0,2,1:T(8,128)(2,1)S(1)}, bf16[512,4,64]{0,2,1:T(8,128)(2,1)}, u32[]{:S(2)}) copy-start(bf16[512,4,64]{0,2,1:T(8,128)(2,1)} %get-tuple-element.58) | copy-start | bytes 786436
  49.4 3.4 %copy-start.6 = (bf16[512,4,64]{2,0,1:T(8,128)(2,1)S(1)}, bf16[512,4,64]{2,0,1:T(8,128)(2,1)}, u32[]{:S(2)}) copy-start(bf16[512,4,64]{2,0,1:T(8,128)(2,1)} %copy.61) | copy-start | bytes 786436
  49.4 3.4 %copy-start.7 = (bf16[512,4,64]{2,0,1:T(8,128)(2,1)S(1)}, bf16[512,4,64]{2,0,1:T(8,128)(2,1)}, u32[]{:S(2)}) copy-start(bf16[512,4,64]{2,0,1:T(8,128)(2,1)} %copy.62) | copy-start | bytes 786436
  49.4 3.4 %copy-start.8 = (pred[512,512]{0,1:T(8,128)(4,1)S(1)}, pred[512,512]{0,1:T(8,128)(4,1)}, u32[]{:S(2)}) copy-start(pred[512,512]{0,1:T(8,128)(4,1)} %fusion.9) | copy-start | bytes 786436
  52.0 0.7 copy-start.4
  52.0 0.8 copy-start.5
  52.8 1.6 copy-start.2
  52.8 1.9 copy-start.16
  55.6 1.4 copy-start.9
  55.7 1.7 copy-start.14
  60.0 42.1 %copy-start.12 = (bf16[2048]{0:T(1024)(128)(2,1)S(1)}, bf16[2048]{0:T(1024)(128)(2,1)}, u32[]{:S(2)}) copy-start(bf16[2048]{0:T(1024)(128)(2,1)} %param.26) | copy-start | bytes 12292
  60.0 42.1 %copy-start.11 = (s32[32,16]{0,1:T(8,128)S(1)}, s32[32,16]{0,1:T(8,128)}, u32[]{:S(2)}) copy-start(s32[32,16]{0,1:T(8,128)} %param.18) | copy-start | bytes 6148
  60.0 56.4 %all-gather.6.cloned.1.call-start = ((), (), s32[]{:S(2)}) async-start(), calls=%async_computation.4 | async-start | bytes 2621440 | tf_op jit(solution)/shard_map/all_gather | solution.py:140
  93.7 98.4 %all-gather.8.cloned.1.call-start = ((), (), s32[]{:S(2)}) async-start(), calls=%async_computation.6 | async-start | bytes 4718592 | tf_op jit(solution)/shard_map/all_gather | solution.py:178
  102.0 171.3 %reduce-scatter.5.cloned.1.call-start = ((), (), s32[]{:S(2)}) async-start(), calls=%async_computation.5 | async-start | bytes 2621440 | tf_op jit(solution)/shard_map/reduce_scatter | solution.py:148
  124.0 8.7 %copy-start.10 = (s32[8,512]{1,0:T(8,128)S(1)}, s32[8,512]{1,0:T(8,128)}, u32[]{:S(2)}) copy-start(s32[8,512]{1,0:T(8,128)} %param.16) | copy-start | bytes 49156
  124.0 11.7 %copy-start.13 = (s32[32]{0:T(128)S(1)}, s32[32]{0:T(128)}, u32[]{:S(2)}) copy-start(s32[32]{0:T(128)} %param.17) | copy-start | bytes 388
Sparse Core Ops, SparseCore 0:
  9.6 25.2 all-gather.3
  60.1 31.4 reduce-scatter.2
  93.8 22.5 all-gather.5
  118.6 73.3 all-gather.7
  194.6 29.6 reduce-scatter.4
where the time goes:
time: 283 us; the launch traced here: 282 us
  local copies, waits for them, and re-layouts  87.2 us (31%)
  waiting for transfers between devices  79.5 us (28%)
  other arithmetic  74.8 us (26%)
  matrix products  26 us (9%)
  between operations  14.1 us (5%)
    gather x1, local copies, waits for them, and re-layouts, body(): taken = everything[source]  66.7 us
    reduce_scatter x1, waiting for transfers between devices, body(): lax.psum_scatter(jnp.dot(attended, w_out, preferred_element_type=jnp.floa...  31.5 us
    all_gather x1, waiting for transfers between devices, body(): piece = lax.all_gather(hidden_in, 'mp', axis=0, tiled=True)  20.5 us
    gather x1, other arithmetic, body(): length = request_length[request]  20.2 us
    gather x1, other arithmetic, body(): begin = request_begin[request]  20.1 us
    select_n x1, other arithmetic, body(): jnp.where(valid[:, :, None, None], taken, jnp.zeros((), jnp.bfloat16))  14.5 us
    all_gather x1, waiting for transfers between devices, body(): lax.all_gather(after, 'mp', axis=0, tiled=True)  14.2 us
    all_gather x1, waiting for transfers between devices, body(): everything = lax.all_gather(pairs, 'req', axis=0, tiled=True)  12.5 us
  transfers between devices with their start and end apart: 5, of which 4 were waited for; matrix products, arithmetic and copies ran while one was open for 56% of the time, Pallas kernels for 0%

commit v1 on v0

--- a/solution.py
+++ b/solution.py
@@ -1,8 +1,11 @@
+import functools
 import math
 
 import jax
 import jax.numpy as jnp
 from jax import lax
+from jax.experimental import pallas as pl
+from jax.experimental.pallas import tpu as pltpu
 from jax.sharding import PartitionSpec as P
 
 HD = 128
@@ -45,6 +48,99 @@
     return jnp.concatenate(
         [first * cosine - second * sine, second * cosine + first * sine], axis=-1
     )
+
+
+def segment_bounds(segment_ids):
+    limits = jnp.arange(PROMPTS_DEV + 1, dtype=jnp.int32)
+    below = segment_ids[:, None, :] < limits[None, :, None]
+    return jnp.sum(below.astype(jnp.int32), axis=2).reshape(-1)
+
+
+def page_kernel(rows, requests, entries, bounds, prompts, table, source, out, blank, sems):
+    blank[...] = jnp.zeros_like(blank)
+
+    def pieces(amount, first, start):
+        for size in (8, 4, 2, 1):
+            skipped = amount - amount % (2 * size)
+
+            @pl.when((amount // size) % 2 == 1)
+            def _():
+                start(first + skipped, size)
+
+    def issue(r, carry):
+        prompt = prompts[r]
+        g = prompt // PROMPTS_DEV
+        slot = g * (PROMPTS_DEV + 1) + prompt - g * PROMPTS_DEV
+        begin = bounds[slot]
+        length = bounds[slot + 1] - begin
+        begin = g * rows + begin
+        full = length // PAGE
+        rest = length - full * PAGE
+
+        def copy_page(e, c):
+            pltpu.make_async_copy(
+                source.at[pl.ds(begin + e * PAGE, PAGE)], out.at[table[r, e]], sems.at[r]
+            ).start()
+            return c
+
+        lax.fori_loop(0, full, copy_page, 0)
+
+        @pl.when(rest > 0)
+        def _():
+            page = table[r, full]
+            base = begin + full * PAGE
+
+            def kept(at, size):
+                pltpu.make_async_copy(
+                    source.at[pl.ds(base + at, size)], out.at[page, pl.ds(at, size)], sems.at[r]
+                ).start()
+
+            def blanked(at, size):
+                pltpu.make_async_copy(
+                    blank.at[pl.ds(0, size)], out.at[page, pl.ds(at, size)], sems.at[r]
+                ).start()
+
+            pieces(rest, 0, kept)
+            pieces(PAGE - rest, rest, blanked)
+
+        def clear_page(e, c):
+            pltpu.make_async_copy(blank, out.at[table[r, e]], sems.at[r]).start()
+            return c
+
+        lax.fori_loop((length + PAGE - 1) // PAGE, entries, clear_page, 0)
+        return carry
+
+    lax.fori_loop(0, requests, issue, 0)
+
+    def finish(r, carry):
+        pltpu.make_async_copy(
+            out.at[pl.ds(0, entries)], out.at[pl.ds(0, entries)], sems.at[r]
+        ).wait()
+        return carry
+
+    lax.fori_loop(0, requests, finish, 0)
+
+
+def fill_pages(bounds, request_prompt, page_table, everything, rows):
+    requests, entries = page_table.shape
+    row_shape = everything.shape[1:]
+    scalars = pl.BlockSpec(memory_space=pltpu.SMEM)
+    return pl.pallas_call(
+        functools.partial(page_kernel, rows, requests, entries),
+        out_shape=jax.ShapeDtypeStruct(
+            (requests * entries, PAGE) + row_shape, everything.dtype
+        ),
+        in_specs=[scalars, scalars, scalars, pl.BlockSpec(memory_space=pltpu.VMEM)],
+        out_specs=pl.BlockSpec(memory_space=pl.ANY),
+        scratch_shapes=[
+            pltpu.VMEM((PAGE,) + row_shape, everything.dtype),
+            pltpu.SemaphoreType.DMA((requests,)),
+        ],
+        compiler_params=pltpu.CompilerParams(
+            vmem_limit_bytes=everything.size * 2 + (8 << 20)
+        ),
+        name="fill_pages",
+    )(bounds, request_prompt, page_table, everything)
 
 
 def body(
@@ -153,31 +249,8 @@
         ).astype(jnp.float32)
     ).astype(jnp.bfloat16)
     pairs = jnp.concatenate([key, value], axis=-1)
-    all_starts, all_lengths, unused = jax.vmap(segment_table)(segment_ids)
-    prompts = segment_ids.shape[0] * PROMPTS_DEV
-    catalog = jnp.arange(prompts, dtype=jnp.int32)
-    most_pages = page_table.shape[1]
-    pool_pages = page_table.shape[0] * most_pages
-    owner = (
-        jnp.zeros((pool_pages,), jnp.int32)
-        .at[page_table.reshape(-1)]
-        .set(jnp.arange(pool_pages, dtype=jnp.int32))
-    )
-    request = owner // most_pages
-    page = owner % most_pages
-    picks = (request_prompt[:, None] == catalog[None, :]).astype(jnp.int32)
-    request_begin = request_prompt // PROMPTS_DEV * seq_rows + jnp.sum(
-        picks * all_starts.reshape(-1)[None, :], axis=1
-    )
-    request_length = jnp.sum(picks * all_lengths.reshape(-1)[None, :], axis=1)
-    begin = request_begin[request]
-    length = request_length[request]
-    offset = page[:, None] * PAGE + jnp.arange(PAGE, dtype=jnp.int32)[None, :]
-    valid = offset < length[:, None]
-    source = jnp.where(valid, begin[:, None] + offset, 0)
     everything = lax.all_gather(pairs, "req", axis=0, tiled=True)
-    taken = everything[source]
-    cache = jnp.where(valid[:, :, None, None], taken, jnp.zeros((), jnp.bfloat16))
+    cache = fill_pages(segment_bounds(segment_ids), request_prompt, page_table, everything, seq_rows)
     return (result, cache)
 
 

time: 283 us -> 234 us (0.83)
  local copies, waits for them, and re-layouts: 87.2 us -> 17.1 us
  waiting for transfers between devices: 79.5 us -> 147 us
  other arithmetic: 74.8 us -> 19.4 us
  Pallas kernels: 0 us -> 8.59 us
    gather x5 -> x0, local copies, waits for them, and re-layouts: 69.5 us -> none  [the longest x1 66.7 us: body(): taken = everything[source]]
    all_gather x1, waiting for transfers between devices: 12.5 us -> 58.9 us  [body(): everything = lax.all_gather(pairs, 'req', axis=0, tiled=True)]
    gather x3 -> x0, other arithmetic: 40.2 us -> none  [the longest x1 20.2 us: body(): length = request_length[request]]
    reduce_scatter x1, waiting for transfers between devices: 0.01 us -> 21.4 us  [body(): lax.psum_scatter(jnp.dot(hidden, w_down, preferred_element_type=jnp.float...]
    select_n x3 -> x0, other arithmetic: 14.8 us -> none  [the longest x1 14.5 us: body(): jnp.where(valid[:, :, None, None], taken, jnp.zeros((), jnp.bfloat16))]
    pallas_call x0 -> x1, Pallas kernels: none -> 8.59 us  [fill_pages(): pl.pallas_call(functools.partial(page_kernel, rows, requests, entries), o...]
    another operation x6 -> x4, local copies, waits for them, and re-layouts: 6.25 us -> 6.1 us
  transfers between devices with their start and end apart: 5 -> 5, of which waited for: 4 -> 5; matrix products, arithmetic and copies ran while one was open for 56% -> 13% of each run, Pallas kernels for 0% -> 4%
where the time goes in v1:
time: 234 us; the launch traced here: 233 us
  waiting for transfers between devices  147 us (63%)
  matrix products  26 us (11%)
  other arithmetic  19.4 us (8%)
  local copies, waits for them, and re-layouts  17.1 us (7%)
  between operations  14 us (6%)
  Pallas kernels  8.59 us (4%)
    all_gather x1, waiting for transfers between devices, body(): everything = lax.all_gather(pairs, 'req', axis=0, tiled=True)  58.9 us
    reduce_scatter x1, waiting for transfers between devices, body(): lax.psum_scatter(jnp.dot(attended, w_out, preferred_element_type=jnp.floa...  31.5 us
    reduce_scatter x1, waiting for transfers between devices, body(): lax.psum_scatter(jnp.dot(hidden, w_down, preferred_element_type=jnp.float...  21.4 us
    all_gather x1, waiting for transfers between devices, body(): piece = lax.all_gather(hidden_in, 'mp', axis=0, tiled=True)  20.5 us
    all_gather x1, waiting for transfers between devices, body(): lax.all_gather(after, 'mp', axis=0, tiled=True)  14.4 us
    dot_general x1, matrix products, body(): jnp.dot(hidden, w_down, preferred_element_type=jnp.float32)  8.71 us
    pallas_call x1, Pallas kernels, fill_pages(): pl.pallas_call(functools.partial(page_kernel, rows, requests, entries), o...  8.59 us
    another operation x4, local copies, waits for them, and re-layouts  6.1 us
  transfers between devices with their start and end apart: 5, of which 5 were waited for; matrix products, arithmetic and copies ran while one was open for 13% of the time, Pallas kernels for 4%

profile of v1, /device:TPU:0, one launch (start us, length us, event | category | flops | bytes accessed | tf_op | source)
XLA Modules:
  0.0 233.0 jit_solution(10904523622917965237)
XLA Ops:
  7.2 0.0 copy-start
  7.2 0.0 all-gather.4.cloned.1.call-start
  7.2 0.7 all-gather.4.cloned.1.call-update
  7.9 0.0 reduce-scatter.3.cloned.1.call-start
  8.0 0.8 convert_element_type.90
  8.8 0.7 convert_element_type.87
  9.4 0.7 constant_dynamic-slice_fusion
  10.2 0.1 convert_reduce_fusion.1
  10.3 0.2 reduce-window.8
  10.5 0.7 convert_element_type.84
  11.2 0.1 select_reduce_fusion
  11.3 0.5 multiply_cosine_fusion
  11.8 0.8 copy.59
  12.6 0.9 copy.60
  13.5 0.9 fusion.9
  14.4 20.5 %all-gather.4.cloned.1.call-done = bf16[512,2048]{1,0:T(8,128)(2,1)} async-done(((bf16[128,2048]{1,0:T(8,128)(2,1)}), bf16[512,2048]{1,0:T(8,128)(2,1)}) %all-gather.4.cloned.1.call-update) | async-done | bytes 2097168 | tf_op jit(solution)/shard_map/all_gather | solution.py:172
  34.9 2.1 fusion
  37.0 3.6 %multiply_reduce_fusion = (f32[512,4]{0,1:T(4,128)S(1)}, f32[512,512]{0,1:T(8,128)S(1)}) fusion(bf16[2048,512]{1,0:T(8,128)(2,1)} %param.20, bf16[512,2048]{1,0:T(8,128)(2,1)} %all-gather.4.cloned.1.call-done, f32[2048]{0:T(1024)S(1)} %convert_element_type.84, f32[512]{0:T(512)S(1)} %add_rsqrt_fusion.3), kind=kOutput, calls=%fused_computation.22 | convolution fusion | flops 1078458368 | bytes 5261312 | tf_op jit(solution)/shard_map/dot_general | solution.py:175
  40.6 0.0 copy-start.16
  40.6 0.2 multiply_multiply_fusion
  40.8 1.0 subtract_convert_fusion
  41.8 0.6 copy-done.3
  42.4 0.3 copy-done.16
  42.7 1.8 multiply_reduce_fusion.1
  44.4 2.0 copy.58
  46.5 2.0 copy.61
  48.4 1.0 copy.62
  49.4 1.3 multiply_multiply_fusion.1
  50.8 1.3 subtract_convert_fusion.1
  52.1 0.7 copy-done.6
  52.7 0.1 copy-done.7
  52.9 1.6 fusion.6
  54.4 0.0 copy-done.4
  54.4 0.3 copy-done.17
  54.7 0.9 convolution_convert_fusion.2
  55.7 1.3 fusion.8
  57.0 0.3 copy-done.15
  57.4 2.6 %convolution_convert_fusion.1 = bf16[512,2048]{1,0:T(8,128)(2,1)} fusion(bf16[512,512]{0,1:T(8,128)(2,1)S(1)} %bitcast.53, bf16[512,2048]{1,0:T(8,128)(2,1)S(1)} %copy-done.15), kind=kOutput, calls=%fused_computation.14 | convolution fusion | flops 1074790400 | bytes 4718592 | tf_op jit(solution)/shard_map/dot_general | solution.py:230
  60.0 0.0 reduce-scatter.3.cloned.1.call-update
  60.0 0.0 all-gather.6.cloned.1.call-start
  60.1 31.5 %reduce-scatter.3.cloned.1.call-done = bf16[128,2048]{1,0:T(8,128)(2,1)} async-done(((bf16[512,2048]{1,0:T(8,128)(2,1)}), bf16[128,2048]{1,0:T(8,128)(2,1)}) %reduce-scatter.3.cloned.1.call-update) | async-done | bytes 524304 | tf_op jit(solution)/shard_map/reduce_scatter | solution.py:229
  91.6 2.1 add_convert_fusion.1
  93.7 0.0 all-gather.6.cloned.1.call-update
  93.7 0.2 all-gather.8.cloned.1.call-start
  94.0 1.2 copy.65
  95.2 1.9 copy.66
  97.1 1.8 copy.67
  98.9 3.1 %pad_maximum_fusion = bf16[512,2,256]{2,1,0:T(2,128)(2,1)} fusion(bf16[512,2,128]{2,1,0:T(2,128)(2,1)} %copy.67, bf16[512,2,64]{2,1,0:T(2,128)(2,1)} %copy.66, bf16[512,2,64]{2,1,0:T(2,128)(2,1)S(1)} %copy.65), kind=kLoop, calls=%fused_computation.30 | loop fusion | flops 1572864 | bytes 1048576 | tf_op jit(solution)/shard_map/concatenate | solution.py:251
  102.0 0.0 all-gather.8.cloned.1.call-update
  102.0 0.0 reduce-scatter.5.cloned.1.call-start
  102.1 14.4 %all-gather.6.cloned.1.call-done = bf16[512,2048]{1,0:T(8,128)(2,1)} async-done(((bf16[128,2048]{1,0:T(8,128)(2,1)}), bf16[512,2048]{1,0:T(8,128)(2,1)}) %all-gather.6.cloned.1.call-update) | async-done | bytes 2097168 | tf_op jit(solution)/shard_map/all_gather | solution.py:236
  116.5 2.1 fusion.3
  118.5 5.5 %fusion.12 = f32[512,768]{1,0:T(8,128)} fusion(bf16[2048,768]{1,0:T(8,128)(2,1)} %param.27, bf16[512,2048]{1,0:T(8,128)(2,1)} %all-gather.6.cloned.1.call-done, f32[2048]{0:T(1024)S(1)} %convert_element_type.99, f32[512]{0:T(512)S(1)} %add_rsqrt_fusion.2), kind=kOutput, calls=%fused_computation.25 | convolution fusion | flops 1614807040 | bytes 6825984 | tf_op jit(solution)/shard_map/dot_general | solution.py:239
  124.1 8.7 %convolution_convert_fusion = bf16[512,2048]{1,0:T(8,128)(2,1)} fusion(bf16[768,2048]{1,0:T(8,128)(2,1)S(1)} %copy-done, f32[512,768]{1,0:T(8,128)} %fusion.12, bf16[2048,768]{1,0:T(8,128)(2,1)} %param.28, bf16[512,2048]{1,0:T(8,128)(2,1)} %all-gather.6.cloned.1.call-done, f32[2048]{0:T(1024)S(1)} %convert_element_type.99, f32[512]{0:T(512)S(1)} %add_rsqrt_fusion.2), kind=kOutput, calls=%fused_computation.13 | convolution fusion | flops 3228827648 | bytes 12068864 | tf_op jit(solution)/shard_map/dot_general | solution.py:245
  132.8 0.0 reduce-scatter.5.cloned.1.call-update
  132.8 0.1 convert_reduce_fusion
  133.0 0.1 copy.64
  133.1 0.1 reshape.212.bounds
  133.1 0.1 copy.68.table
  133.2 58.9 %all-gather.8.cloned.1.call-done.source = bf16[4096,2,256]{2,1,0:T(2,128)(2,1)} async-done(((bf16[512,2,256]{2,1,0:T(2,128)(2,1)}), bf16[4096,2,256]{2,1,0:T(2,128)(2,1)}) %all-gather.8.cloned.1.call-update) | async-done | bytes 4194320 | tf_op jit(solution)/shard_map/all_gather | solution.py:252
  192.1 2.2 copy-done.1
  194.3 8.6 %fill_pages.1 = bf16[512,16,2,256]{3,2,1,0:T(2,128)(2,1)} custom-call(s32[32]{0:T(128)S(1)} %reshape.212.bounds, s32[32]{0:T(128)S(1)} %copy-done.2, s32[32,16]{1,0:T(8,128)S(1)} %copy.68.table, bf16[4096,2,256]{2,1,0:T(2,128)(2,1)S(1)} %copy-done.1), custom_call_target="tpu_custom_call" | custom-call | tf_op jit(solution)/shard_map/fill_pages/pallas_call | solution.py:128
  202.9 21.4 %reduce-scatter.5.cloned.1.call-done = bf16[128,2048]{1,0:T(8,128)(2,1)} async-done(((bf16[512,2048]{1,0:T(8,128)(2,1)}), bf16[128,2048]{1,0:T(8,128)(2,1)}) %reduce-scatter.5.cloned.1.call-update) | async-done | bytes 524304 | tf_op jit(solution)/shard_map/reduce_scatter | solution.py:244
  224.3 2.1 add_convert_fusion
  (34 shorter events, 0.1 us)
Async XLA Ops:
  7.2 116.9 %copy-start = (bf16[768,2048]{1,0:T(8,128)(2,1)S(1)}, bf16[768,2048]{1,0:T(8,128)(2,1)}, u32[]{:S(2)}) copy-start(bf16[768,2048]{1,0:T(8,128)(2,1)} %param.29) | copy-start | bytes 9437188
  7.2 27.7 %all-gather.4.cloned.1.call-start = ((), (), s32[]{:S(2)}) async-start(), calls=%async_computation.2 | async-start | bytes 2621440 | tf_op jit(solution)/shard_map/all_gather | solution.py:172
  7.9 83.7 %reduce-scatter.3.cloned.1.call-start = ((), (), s32[]{:S(2)}) async-start(), calls=%async_computation.3 | async-start | bytes 2621440 | tf_op jit(solution)/shard_map/reduce_scatter | solution.py:229
  40.6 1.8 copy-start.3
  40.6 2.0 copy-start.16
  42.7 5.8 %copy-start.5 = (bf16[512,4,64]{0,2,1:T(8,128)(2,1)S(1)}, bf16[512,4,64]{0,2,1:T(8,128)(2,1)}, u32[]{:S(2)}) copy-start(bf16[512,4,64]{0,2,1:T(8,128)(2,1)} %get-tuple-element.17) | copy-start | bytes 786436
  49.4 3.4 %copy-start.8 = (bf16[512,4,64]{2,0,1:T(8,128)(2,1)S(1)}, bf16[512,4,64]{2,0,1:T(8,128)(2,1)}, u32[]{:S(2)}) copy-start(bf16[512,4,64]{2,0,1:T(8,128)(2,1)} %copy.61) | copy-start | bytes 786436
  49.4 3.4 %copy-start.9 = (bf16[512,4,64]{2,0,1:T(8,128)(2,1)S(1)}, bf16[512,4,64]{2,0,1:T(8,128)(2,1)}, u32[]{:S(2)}) copy-start(bf16[512,4,64]{2,0,1:T(8,128)(2,1)} %copy.62) | copy-start | bytes 786436
  49.4 3.4 %copy-start.10 = (pred[512,512]{0,1:T(8,128)(4,1)S(1)}, pred[512,512]{0,1:T(8,128)(4,1)}, u32[]{:S(2)}) copy-start(pred[512,512]{0,1:T(8,128)(4,1)} %fusion.9) | copy-start | bytes 786436
  52.0 0.7 copy-start.6
  52.0 0.8 copy-start.7
  52.9 1.6 copy-start.4
  52.9 1.9 copy-start.17
  55.7 1.4 copy-start.11
  55.7 1.7 copy-start.15
  60.0 42.1 %copy-start.14 = (bf16[2048]{0:T(1024)(128)(2,1)S(1)}, bf16[2048]{0:T(1024)(128)(2,1)}, u32[]{:S(2)}) copy-start(bf16[2048]{0:T(1024)(128)(2,1)} %param.26) | copy-start | bytes 12292
  60.0 56.5 %all-gather.6.cloned.1.call-start = ((), (), s32[]{:S(2)}) async-start(), calls=%async_computation.4 | async-start | bytes 2621440 | tf_op jit(solution)/shard_map/all_gather | solution.py:236
  93.7 98.4 %all-gather.8.cloned.1.call-start = ((), (), s32[]{:S(2)}) async-start(), calls=%async_computation.6 | async-start | bytes 4718592 | tf_op jit(solution)/shard_map/all_gather | solution.py:252
  102.0 122.3 %reduce-scatter.5.cloned.1.call-start = ((), (), s32[]{:S(2)}) async-start(), calls=%async_computation.5 | async-start | bytes 2621440 | tf_op jit(solution)/shard_map/reduce_scatter | solution.py:244
  124.1 8.7 %copy-start.12 = (s32[8,512]{1,0:T(8,128)S(1)}, s32[8,512]{1,0:T(8,128)}, u32[]{:S(2)}) copy-start(s32[8,512]{1,0:T(8,128)} %param.16) | copy-start | bytes 49156
  124.1 9.1 %copy-start.13 = (s32[32,16]{0,1:T(8,128)S(1)}, s32[32,16]{0,1:T(8,128)}, u32[]{:S(2)}) copy-start(s32[32,16]{0,1:T(8,128)} %param.18) | copy-start | bytes 6148
  124.1 68.0 %copy-start.2 = (s32[32]{0:T(128)S(1)}, s32[32]{0:T(128)}, u32[]{:S(2)}) copy-start(s32[32]{0:T(128)} %prompts.1) | copy-start | bytes 388
  192.1 2.2 copy-start.1
Sparse Core Ops, SparseCore 0:
  9.6 25.2 all-gather.3
  60.1 31.4 reduce-scatter.2
  93.8 22.5 all-gather.5
  118.7 73.3 all-gather.7
  194.6 29.6 reduce-scatter.4

commit v2 on v1

v2 whole, which is shorter than its diff:
```python
import functools
import math

import jax
import jax.numpy as jnp
from jax import lax
from jax.experimental import pallas as pl
from jax.experimental.pallas import tpu as pltpu
from jax.sharding import PartitionSpec as P

HD = 128
PROMPTS_DEV = 3
PAGE = 16
EPS = 1e-06
THETA = 1000000.0
SMEM = pl.BlockSpec(memory_space=pltpu.SMEM)
VMEM = pl.BlockSpec(memory_space=pltpu.VMEM)
ANY = pl.BlockSpec(memory_space=pl.ANY)


def dot(a, b):
    return jnp.dot(a, b, preferred_element_type=jnp.float32)


def normalized(wide, gain):
    return wide * lax.rsqrt(jnp.mean(wide * wide, axis=-1, keepdims=True) + EPS) * gain


def segment_bounds(segment_ids):
    limits = jnp.arange(PROMPTS_DEV + 1, dtype=jnp.int32)
    below = segment_ids[:, None, :] < limits[None, :, None]
    return jnp.sum(below.astype(jnp.int32), axis=2).reshape(-1)


def rotation(bounds, req, first, rows):
    own = lax.dynamic_slice_in_dim(bounds, req * (PROMPTS_DEV + 1), PROMPTS_DEV, 0)
    token = (lax.iota(jnp.int32, rows) + first) % rows
    start = jnp.max(jnp.where(token[:, None] >= own[None, :], own[None, :], 0), axis=1)
    half = HD // 2
    freq = THETA ** (-(jnp.arange(half, dtype=jnp.float32) * 2.0) / HD)
    angle = (token - start).astype(jnp.float32)[:, None] * freq[None, :]
    cosine, sine = jnp.cos(angle), jnp.sin(angle)
    return (
        jnp.concatenate([cosine, cosine], axis=1),
        jnp.concatenate([-sine, sine], axis=1),
    )


def project_kernel(place, own, other, ln, wq, wk, wv, qg, kg, cos, sin, q, k, v, pairs, normed):
    core = place[2]
    count = own.shape[0]
    gain = ln[...].astype(jnp.float32)
    for ref, at in ((own, core * count), (other, (1 - core) * count)):
        normed[pl.ds(pl.multiple_of(at, count), count), :] = normalized(
            ref[...].astype(jnp.float32), gain
        ).astype(jnp.bfloat16)
    rows = normed[...]
    cosine, sine = cos[...], sin[...]

    def heads(weight, gain_ref, out):
        wide = dot(rows, weight[...])
        gain = gain_ref[...].astype(jnp.float32)
        for h in range(weight.shape[1] // HD):
            one = normalized(wide[:, h * HD : (h + 1) * HD], gain)
            turned = one * cosine + pltpu.roll(one, HD // 2, 1) * sine
            out[:, h * HD : (h + 1) * HD] = turned.astype(jnp.bfloat16)

    heads(wk, kg, k)
    v[...] = dot(rows, wv[...]).astype(jnp.bfloat16)
    shape = (rows.shape[0], k.shape[1] // HD, HD)
    pairs[...] = jnp.concatenate([k[...].reshape(shape), v[...].reshape(shape)], axis=-1)
    heads(wq, qg, q)


def project(place, own, other, ln, wq, wk, wv, qg, kg, cos, sin, chunk):
    count, width = 2 * own.shape[0], own.shape[1]
    kv_here = wk.shape[1] // HD
    bf = jnp.bfloat16
    table = pl.BlockSpec((count, HD), lambda i: (chunk, 0))

    def full(a):
        return pl.BlockSpec(a.shape, lambda i: (0,) * a.ndim, pipeline_mode=pl.Buffered(1))

    outs = [
        jax.ShapeDtypeStruct((count, wq.shape[1]), bf),
        jax.ShapeDtypeStruct((count, wk.shape[1]), bf),
        jax.ShapeDtypeStruct((count, wv.shape[1]), bf),
        jax.ShapeDtypeStruct((count, kv_here, 2 * HD), bf),
    ]
    return pl.pallas_call(
        project_kernel,
        grid=(1,),
        out_shape=outs,
        in_specs=[SMEM] + [full(a) for a in (own, other, ln, wq, wk, wv, qg, kg)] + [table, table],
        out_specs=[full(o) for o in outs],
        scratch_shapes=[pltpu.VMEM((count, width), bf)],
        compiler_params=pltpu.CompilerParams(vmem_limit_bytes=24 << 20),
        cost_estimate=pl.CostEstimate(
            flops=2 * count * width * (wq.shape[1] + 2 * wk.shape[1]),
            bytes_accessed=8 << 20,
            transcendentals=0,
        ),
        name="project",
    )(place, own, other, ln, wq, wk, wv, qg, kg, cos, sin)


def attend_kernel(place, bounds, qa, qb, ka, kb, va, vb, keep_a, send_a, keep_b, send_b):
    req, side, core = place[0], place[1], place[2]
    half = qa.shape[0]
    count = half // 2
    rows = 2 * half
    kv_here = ka.shape[1] // HD
    group = qa.shape[1] // ka.shape[1]
    slot = req * (PROMPTS_DEV + 1)
    scale = 1.0 / math.sqrt(HD)
    first_a = side * half
    first_b = rows - half - first_a
    column = lax.broadcasted_iota(jnp.int32, (count, half), 1)
    line = lax.broadcasted_iota(jnp.int32, (count, half), 0)
    for q, out, first, part in (
        (qb, send_b, first_b, 1 - core),
        (qb, keep_b, first_b, core),
        (qa, send_a, first_a, 1 - core),
        (qa, keep_a, first_a, core),
    ):
        at = pl.multiple_of(part * count, count)
        token = first + at + line
        start = jnp.zeros_like(token)
        for s in range(1, PROMPTS_DEV):
            begin = bounds[slot + s]
            start = jnp.where(token >= begin, begin, start)
        allowed = [
            (column + base <= token) & (column + base >= start) for base in (first_a, first_b)
        ]
        for j in range(kv_here):
            lanes = slice(j * HD, (j + 1) * HD)
            for h in range(j * group, (j + 1) * group):
                one = q[pl.ds(at, count), h * HD : (h + 1) * HD]
                raised = []
                for keys, mask in zip((ka, kb), allowed):
                    scores = lax.dot_general(
                        one,
                        keys[:, lanes],
                        (((1,), (1,)), ((), ())),
                        preferred_element_type=jnp.float32,
                    )
                    raised.append(jnp.where(mask, jnp.exp(scores * scale), 0.0))
                total = sum(jnp.sum(r, axis=-1, keepdims=True) for r in raised)
                share = 1.0 / total
                mixed = sum(
                    dot((r * share).astype(jnp.bfloat16), values[:, lanes])
                    for r, values in zip(raised, (va, vb))
                )
                out[:, h * HD : (h + 1) * HD] = mixed.astype(jnp.bfloat16)


def attend(place, bounds, qa, qb, ka, kb, va, vb):
    count, width = qa.shape[0] // 2, qa.shape[1]
    out = jax.ShapeDtypeStruct((count, width), jnp.bfloat16)
    return pl.pallas_call(
        attend_kernel,
        out_shape=[out] * 4,
        in_specs=[SMEM, SMEM] + [VMEM] * 6,
        out_specs=[VMEM] * 4,
        compiler_params=pltpu.CompilerParams(vmem_limit_bytes=24 << 20),
        cost_estimate=pl.CostEstimate(
            flops=64 * count * count * width, bytes_accessed=4 << 20, transcendentals=1 << 20
        ),
        name="attend",
    )(place, bounds, qa, qb, ka, kb, va, vb)


def mlp_kernel(first, second, ln, wg, wu, keep, send, normed):
    count = first.shape[0]

    @pl.when(pl.program_id(0) == 0)
    def _():
        gain = ln[...].astype(jnp.float32)
        for ref, at in ((first, 0), (second, count)):
            normed[at : at + count, :] = normalized(
                ref[...].astype(jnp.float32), gain
            ).astype(jnp.bfloat16)

    rows = normed[...]
    gate = dot(rows, wg[...])
    upper = dot(rows, wu[...])
    hidden = (gate / (1.0 + jnp.exp(-gate)) * upper).astype(jnp.bfloat16)
    keep[...] = hidden[:count]
    send[...] = hidden[count:]


def mlp(first, second, ln, wg, wu):
    count, width = first.shape
    units = wg.shape[1]
    step = 256
    whole = pl.BlockSpec((count, width), lambda i: (0, 0), pipeline_mode=pl.Buffered(1))
    weight = pl.BlockSpec((width, step), lambda i: (0, i))
    out = jax.ShapeDtypeStruct((count, units), jnp.bfloat16)
    return pl.pallas_call(
        mlp_kernel,
        grid=(units // step,),
        out_shape=[out] * 2,
        in_specs=[whole, whole, pl.BlockSpec((1, width), lambda i: (0, 0)), weight, weight],
        out_specs=[pl.BlockSpec((count, step), lambda i: (0, i))] * 2,
        scratch_shapes=[pltpu.VMEM((2 * count, width), jnp.bfloat16)],
        compiler_params=pltpu.CompilerParams(vmem_limit_bytes=24 << 20),
        cost_estimate=pl.CostEstimate(
            flops=8 * count * width * units, bytes_accessed=8 << 20, transcendentals=1 << 18
        ),
        name="gate_up",
    )(first, second, ln, wg, wu)


def page_kernel(rows, requests, entries, blocks, *refs):
    place, bounds, prompts, table = refs[:4]
    arrived = refs[4 : 4 + blocks]
    out, held, blank, load_sems, sems = refs[4 + blocks :]
    half = rows // 2
    for i in range(blocks):
        pltpu.make_async_copy(
            arrived[i],
            held.at[pl.ds(pl.multiple_of(place[3 + i] * half, half), half)],
            load_sems.at[i],
        ).start()
    blank[...] = jnp.zeros_like(blank)
    for i in range(blocks):
        pltpu.make_async_copy(
            arrived[i],
            held.at[pl.ds(pl.multiple_of(place[3 + i] * half, half), half)],
            load_sems.at[i],
        ).wait()

    def pieces(amount, first, start):
        for size in (8, 4, 2, 1):
            skipped = amount - amount % (2 * size)

            @pl.when((amount // size) % 2 == 1)
            def _():
                start(first + skipped, size)

    def issue(r, carry):
        prompt = prompts[r]
        g = prompt // PROMPTS_DEV
        slot = g * (PROMPTS_DEV + 1) + prompt - g * PROMPTS_DEV
        begin = bounds[slot]
        length = bounds[slot + 1] - begin
        begin = g * rows + begin
        full = length // PAGE
        rest = length - full * PAGE

        def copy_page(e, c):
            pltpu.make_async_copy(
                held.at[pl.ds(begin + e * PAGE, PAGE)], out.at[table[r, e]], sems.at[r]
            ).start()
            return c

        lax.fori_loop(0, full, copy_page, 0)

        @pl.when(rest > 0)
        def _():
            page = table[r, full]
            base = begin + full * PAGE

            def kept(at, size):
                pltpu.make_async_copy(
                    held.at[pl.ds(base + at, size)], out.at[page, pl.ds(at, size)], sems.at[r]
                ).start()

            def blanked(at, size):
                pltpu.make_async_copy(
                    blank.at[pl.ds(0, size)], out.at[page, pl.ds(at, size)], sems.at[r]
                ).start()

            pieces(rest, 0, kept)
            pieces(PAGE - rest, rest, blanked)

        def clear_page(e, c):
            pltpu.make_async_copy(blank, out.at[table[r, e]], sems.at[r]).start()
            return c

        lax.fori_loop((length + PAGE - 1) // PAGE, entries, clear_page, 0)
        return carry

    lax.fori_loop(0, requests, issue, 0)

    def finish(r, carry):
        pltpu.make_async_copy(
            out.at[pl.ds(0, entries)], out.at[pl.ds(0, entries)], sems.at[r]
        ).wait()
        return carry

    lax.fori_loop(0, requests, finish, 0)


def fill_pages(place, bounds, request_prompt, page_table, arrived, rows):
    requests, entries = page_table.shape
    row_shape = arrived[0].shape[1:]
    dtype = arrived[0].dtype
    blocks = len(arrived)
    held = (blocks * arrived[0].shape[0],) + row_shape
    return pl.pallas_call(
        functools.partial(page_kernel, rows, requests, entries, blocks),
        out_shape=jax.ShapeDtypeStruct((requests * entries, PAGE) + row_shape, dtype),
        in_specs=[SMEM] * 4 + [ANY] * blocks,
        out_specs=ANY,
        scratch_shapes=[
            pltpu.VMEM(held, dtype),
            pltpu.VMEM((PAGE,) + row_shape, dtype),
            pltpu.SemaphoreType.DMA((blocks,)),
            pltpu.SemaphoreType.DMA((requests,)),
        ],
        compiler_params=pltpu.CompilerParams(
            vmem_limit_bytes=math.prod(held) * 2 + (4 << 20)
        ),
        cost_estimate=pl.CostEstimate(flops=0, bytes_accessed=12 << 20, transcendentals=0),
        name="fill_pages",
    )(place, bounds, request_prompt, page_table, *arrived)


def body(
    hidden_in,
    segment_ids,
    request_prompt,
    page_table,
    ln_attn,
    w_query,
    w_key,
    w_value,
    q_gain,
    k_gain,
    w_out,
    ln_mlp,
    w_gate,
    w_up,
    w_down,
):
    parts = lax.axis_size("mp")
    groups = lax.axis_size("req")
    rows = hidden_in.shape[0] * parts
    half = rows // 2
    req = lax.axis_index("req")
    mine = lax.axis_index("mp")
    side, core = mine // 2, mine % 2
    to_core = [(i, i ^ 1) for i in range(parts)]
    to_side = [(i, i ^ 2) for i in range(parts)]
    to_pair = [(i, i ^ 1) for i in range(groups)]
    to_next = [(i, (i + 2) % groups) for i in range(groups)]

    def by_core(a):
        return lax.ppermute(a, "mp", to_core)

    def by_side(a):
        return lax.ppermute(a, "mp", to_side)

    here_x = by_side(hidden_in)
    here_c = by_core(hidden_in)
    bounds = segment_bounds(segment_ids)
    homes = []
    for step in range(groups // 2):
        for flip in (0, 1):
            for part in (0, 1):
                home = ((req ^ flip) - 2 * step) % groups
                homes.append(2 * home + (side ^ part))
    place = jnp.stack([req, side, core] + homes).astype(jnp.int32)
    cos, sin = rotation(bounds, req, side * half, rows)
    ln = ln_attn.reshape(1, -1)
    qg, kg = q_gain.reshape(1, -1), k_gain.reshape(1, -1)
    weights = (ln, w_query, w_key, w_value, qg, kg, cos, sin)
    qa, ka, va, pairs_a = project(place, hidden_in, here_c, *weights, 0)
    out_other = by_core(w_out)
    here_xc = by_core(here_x)
    qb, kb, vb, pairs_b = project(place, here_x, here_xc, *weights, 1)

    arrived = []
    moving = [pairs_a, pairs_b]
    for step in range(groups // 2):
        if step:
            moving = [lax.ppermute(a, "req", to_next) for a in moving]
        arrived += moving + [lax.ppermute(a, "req", to_pair) for a in moving]

    keep_a, send_a, keep_b, send_b = attend(place, bounds, qa, qb, ka, kb, va, vb)
    got_b = by_core(send_b)
    got_a = by_core(send_a)
    part_b = (dot(keep_b, w_out) + dot(got_b, out_other)).astype(jnp.bfloat16)
    back = by_side(part_b)
    part_a = dot(keep_a, w_out) + dot(got_a, out_other)
    after = (hidden_in.astype(jnp.float32) + part_a + back.astype(jnp.float32)).astype(
        jnp.bfloat16
    )
    down_other = by_core(w_down)

    after_x = by_side(after)
    after_c = by_core(after)
    ln2 = ln_mlp.reshape(1, -1)
    keep_a, send_a = mlp(after, after_c, ln2, w_gate, w_up)
    got_a = by_core(send_a)
    down_a = dot(keep_a, w_down) + dot(got_a, down_other)
    after_xc = by_core(after_x)
    keep_b, send_b = mlp(after_x, after_xc, ln2, w_gate, w_up)
    got_b = by_core(send_b)
    down_b = (dot(keep_b, w_down) + dot(got_b, down_other)).astype(jnp.bfloat16)
    back = by_side(down_b)
    result = (after.astype(jnp.float32) + down_a + back.astype(jnp.float32)).astype(jnp.bfloat16)
    cache = fill_pages(place, bounds, request_prompt, page_table, arrived, rows)
    return (result, cache)


def solution(mesh):
    return jax.shard_map(
        body,
        mesh=mesh,
        in_specs=(
            P(("req", "mp"), None),
            P(),
            P("req"),
            P("req", None),
            P(),
            P(None, "mp"),
            P(None, "mp"),
            P(None, "mp"),
            P(),
            P(),
            P("mp", None),
            P(),
            P(None, "mp"),
            P(None, "mp"),
            P("mp", None),
        ),
        out_specs=(P(("req", "mp"), None), P("req", None, "mp", None)),
        check_vma=False,
    )
```

time: 234 us -> 152 us (0.65)
  waiting for transfers between devices: 147 us -> 57.7 us
  starting transfers between devices: 0.38 us -> 23.5 us
  Pallas kernels: 8.59 us -> 28.8 us
  other arithmetic: 19.4 us -> 4.21 us
  matrix products: 26 us -> 12.5 us
  between operations: 14 us -> 1.17 us
  local copies, waits for them, and re-layouts: 17.1 us -> 23 us
    all_gather x3 -> x0, waiting for transfers between devices: 93.8 us -> none  [the longest x1 58.9 us: body(): everything = lax.all_gather(pairs, 'req', axis=0, tiled=True)]
    ppermute x0 -> x28, waiting for transfers between devices: none -> 57.7 us  [the longest x4 28.6 us: by_side(): return lax.ppermute(a, 'mp', to_side)]
    reduce_scatter x2 -> x0, waiting for transfers between devices: 53 us -> none  [the longest x1 31.5 us: body(): lax.psum_scatter(jnp.dot(attended, w_out, preferred_element_type=jnp.floa...]
    ppermute x0 -> x28, starting transfers between devices: none -> 23.5 us  [the longest x8 10.6 us: body(): arrived += moving + [lax.ppermute(a, 'req', to_pair) for a in moving]]
    pallas_call x1 -> x6, Pallas kernels: 8.59 us -> 28.8 us  [the longest x1 10 us: fill_pages(): pl.pallas_call(functools.partial(page_kernel, rows, requests, entries, bl...]
    unnamed x37 -> x79, local copies, waits for them, and re-layouts: 4.57 us -> 21.9 us
    dot_general x8, matrix products: 26 us -> 12.5 us  [dot(): return jnp.dot(a, b, preferred_element_type=jnp.float32)]
    another operation x4 -> x1, local copies, waits for them, and re-layouts: 6.1 us -> 0.09 us  [body(): place = jnp.stack([req, side, core] + homes).astype(jnp.int32)]
  transfers between devices with their start and end apart: 5 -> 28, of which waited for: 5 -> 15; matrix products, arithmetic and copies ran while one was open for 13% -> 10% of each run, Pallas kernels for 4% -> 19%
where the time goes in v2:
time: 152 us; the launch traced here: 151 us
  waiting for transfers between devices  57.7 us (38%)
  Pallas kernels  28.8 us (19%)
  starting transfers between devices  23.5 us (15%)
  local copies, waits for them, and re-layouts  23 us (15%)
  matrix products  12.5 us (8%)
  other arithmetic  4.21 us (3%)
    ppermute x4, waiting for transfers between devices, by_side(): return lax.ppermute(a, 'mp', to_side)  28.6 us
    unnamed x79, local copies, waits for them, and re-layouts  21.9 us
    ppermute x6, waiting for transfers between devices, body(): moving = [lax.ppermute(a, 'req', to_next) for a in moving]  14.3 us
    ppermute x8, waiting for transfers between devices, body(): arrived += moving + [lax.ppermute(a, 'req', to_pair) for a in moving]  13.8 us
    dot_general x8, matrix products, dot(): return jnp.dot(a, b, preferred_element_type=jnp.float32)  12.5 us
    ppermute x8, starting transfers between devices, body(): arrived += moving + [lax.ppermute(a, 'req', to_pair) for a in moving]  10.6 us
    pallas_call x1, Pallas kernels, fill_pages(): pl.pallas_call(functools.partial(page_kernel, rows, requests, entries, bl...  10 us
    pallas_call x2, Pallas kernels, mlp(): pl.pallas_call(mlp_kernel, grid=(units // step,), out_shape=[out] * 2, in...  7.91 us
  transfers between devices with their start and end apart: 28, of which 15 were waited for; matrix products, arithmetic and copies ran while one was open for 10% of the time, Pallas kernels for 19%

profile of v2, /device:TPU:0, one launch (start us, length us, event | category | flops | bytes accessed | tf_op | source)
XLA Modules:
  0.0 150.9 jit_solution(3101046601279677097)
XLA Ops:
  1.2 2.9 %collective-permute-start.1 = (bf16[128,2048]{1,0:T(8,128)(2,1)}, bf16[128,2048]{1,0:T(8,128)(2,1)S(1)}, u32[]{:S(2)}, u32[]{:S(2)}) collective-permute-start(bf16[128,2048]{1,0:T(8,128)(2,1)} %own.1), channel_id=1, source_target_pairs={{0,2},{1,3},{2,0},{3,1},{4,6},{5,7},{6,4},{7,5},{8,10},{9,11},{10,... | collective-permute-start | bytes 1572872 | tf_op jit(solution)/shard_map/ppermute | solution.py:353
  4.2 0.9 convert_reduce_fusion
  5.4 11.1 %collective-permute-done.1.own = bf16[128,2048]{1,0:T(8,128)(2,1)S(1)} collective-permute-done((bf16[128,2048]{1,0:T(8,128)(2,1)}, bf16[128,2048]{1,0:T(8,128)(2,1)S(1)}, u32[]{:S(2)}, u32[]{:S(2)}) %collective-permute-start.1) | collective-permute-done | bytes 524320 | tf_op jit(solution)/shard_map/ppermute | solution.py:353
  16.7 0.7 reshape.50.ln
  17.5 1.0 fusion.5
  18.8 1.2 copy-done.4
  20.0 1.2 copy-done.5
  21.2 1.0 copy-done.6
  22.2 0.7 copy-done.32
  23.6 2.7 %project.2 = (bf16[256,512]{1,0:T(8,128)(2,1)S(1)}, bf16[256,256]{1,0:T(8,128)(2,1)S(1)}, bf16[256,256]{1,0:T(8,128)(2,1)S(1)}, bf16[256,2,256]{2,1,0:T(2,128)(2,1)S(1)}) custom-call(s32[19]{0:T(128)S(1)} %stack.79.place.refs_0_, bf16[128,2048]{1,0:T(8,128)(2,1)S(1)} %copy-done.6, bf16[128,2048]{1,0:T(8,128)(2,1)S(1)} %collective-permute-done.other, ...), custom_call_target="tpu_custom_call" | custom-call | flops 1073741824 | bytes 8388608 | tf_op jit(solution)/shard_map/project/pallas_call | solution.py:90
  26.2 3.2 %project.3 = (bf16[256,512]{1,0:T(8,128)(2,1)S(1)}, bf16[256,256]{1,0:T(8,128)(2,1)S(1)}, bf16[256,256]{1,0:T(8,128)(2,1)S(1)}, bf16[256,2,256]{2,1,0:T(2,128)(2,1)S(1)}) custom-call(s32[19]{0:T(128)S(1)} %stack.79.place.refs_0_, bf16[128,2048]{1,0:T(8,128)(2,1)S(1)} %collective-permute-done.1.own, bf16[128,2048]{1,0:T(8,128)(2,1)} %collective-permute-done.2.other, ...), custom_call_target="tpu_custom_call" | custom-call | flops 1073741824 | bytes 8388608 | tf_op jit(solution)/shard_map/project/pallas_call | solution.py:90
  29.4 5.1 %attend.1 = (bf16[128,512]{1,0:T(8,128)(2,1)S(1)}, bf16[128,512]{1,0:T(8,128)(2,1)S(1)}, bf16[128,512]{1,0:T(8,128)(2,1)S(1)}, bf16[128,512]{1,0:T(8,128)(2,1)S(1)}) custom-call(s32[19]{0:T(128)S(1)} %stack.79.place.refs_0_, s32[32]{0:T(128)S(1)} %reshape.49.bounds.refs_1_, bf16[256,512]{1,0:T(8,128)(2,1)S(1)} %get-tuple-element.18.qa, ...), custom_call_target="tpu_custom_call" | custom-call | flops 536870912 | bytes 4194304 | tf_op jit(solution)/shard_map/attend/pallas_call | solution.py:160
  34.9 1.0 collective-permute-done.5
  35.9 2.0 %fusion.8 = f32[128,2048]{1,0:T(8,128)S(1)} fusion(bf16[128,512]{1,0:T(8,128)(2,1)S(1)} %collective-permute-done.5, bf16[512,2048]{1,0:T(8,128)(2,1)} %collective-permute-done.4), kind=kOutput, calls=%fused_computation.25 | convolution fusion | flops 268435456 | bytes 3276800 | tf_op jit(solution)/shard_map/dot_general | solution.py:22
  38.5 1.8 %collective-permute-start.6 = (bf16[128,2048]{1,0:T(8,128)(2,1)S(1)}, bf16[128,2048]{1,0:T(8,128)(2,1)S(1)}, u32[]{:S(2)}, u32[]{:S(2)}) collective-permute-start(bf16[128,2048]{1,0:T(8,128)(2,1)S(1)} %fusion.3), channel_id=1, source_target_pairs={{0,2},{1,3},{2,0},{3,1},{4,6},{5,7},{6,4},{7,5},{8,10},{9,11},{10,... | collective-permute-start | bytes 1572872 | tf_op jit(solution)/shard_map/ppermute | solution.py:353
  40.3 1.6 %collective-permute-start.16 = (bf16[256,2,256]{2,1,0:T(2,128)(2,1)S(1)}, bf16[256,2,256]{2,1,0:T(2,128)(2,1)S(1)}, u32[]{:S(2)}, u32[]{:S(2)}) collective-permute-start(bf16[256,2,256]{2,1,0:T(2,128)(2,1)S(1)} %get-tuple-element.32.refs_4_), channel_id=1, source_target_pairs={{0,8},{4,12},{8,16},{12,20},{16,24},{20,28},{24,0},{28,4},{1,9},{5... | collective-permute-start | bytes 786440 | tf_op jit(solution)/shard_map/ppermute | solution.py:378
  41.9 1.5 %collective-permute-start.14 = (bf16[256,2,256]{2,1,0:T(2,128)(2,1)S(1)}, bf16[256,2,256]{2,1,0:T(2,128)(2,1)S(1)}, u32[]{:S(2)}, u32[]{:S(2)}) collective-permute-start(bf16[256,2,256]{2,1,0:T(2,128)(2,1)S(1)} %get-tuple-element.32.refs_4_), channel_id=1, source_target_pairs={{0,4},{4,0},{8,12},{12,8},{16,20},{20,16},{24,28},{28,24},{1,5},{5... | collective-permute-start | bytes 786440 | tf_op jit(solution)/shard_map/ppermute | solution.py:379
  43.4 2.2 %fusion.7 = f32[128,2048]{1,0:T(8,128)S(1)} fusion(bf16[128,512]{1,0:T(8,128)(2,1)S(1)} %collective-permute-done.3, bf16[512,2048]{1,0:T(8,128)(2,1)} %collective-permute-done.4), kind=kOutput, calls=%fused_computation.24 | convolution fusion | flops 268435456 | bytes 3276800 | tf_op jit(solution)/shard_map/dot_general | solution.py:22
  45.7 7.1 %collective-permute-done.6 = bf16[128,2048]{1,0:T(8,128)(2,1)S(1)} collective-permute-done((bf16[128,2048]{1,0:T(8,128)(2,1)S(1)}, bf16[128,2048]{1,0:T(8,128)(2,1)S(1)}, u32[]{:S(2)}, u32[]{:S(2)}) %collective-permute-start.6) | collective-permute-done | bytes 524320 | tf_op jit(solution)/shard_map/ppermute | solution.py:353
  52.7 1.4 fusion.2.first
  54.1 1.7 %collective-permute-start.10 = (bf16[128,2048]{1,0:T(8,128)(2,1)}, bf16[128,2048]{1,0:T(8,128)(2,1)S(1)}, u32[]{:S(2)}, u32[]{:S(2)}) collective-permute-start(bf16[128,2048]{1,0:T(8,128)(2,1)} %fusion.2.first), channel_id=1, source_target_pairs={{0,2},{1,3},{2,0},{3,1},{4,6},{5,7},{6,4},{7,5},{8,10},{9,11},{10,... | collective-permute-start | bytes 1572872 | tf_op jit(solution)/shard_map/ppermute | solution.py:353
  55.9 1.6 %collective-permute-start.20 = (bf16[256,2,256]{2,1,0:T(2,128)(2,1)S(1)}, bf16[256,2,256]{2,1,0:T(2,128)(2,1)S(1)}, u32[]{:S(2)}, u32[]{:S(2)}) collective-permute-start(bf16[256,2,256]{2,1,0:T(2,128)(2,1)S(1)} %collective-permute-done.16.refs_8_), channel_id=1, source_target_pairs={{0,8},{4,12},{8,16},{12,20},{16,24},{20,28},{24,0},{28,4},{1,9},{5... | collective-permute-start | bytes 786440 | tf_op jit(solution)/shard_map/ppermute | solution.py:378
  57.5 1.5 %collective-permute-start.18 = (bf16[256,2,256]{2,1,0:T(2,128)(2,1)S(1)}, bf16[256,2,256]{2,1,0:T(2,128)(2,1)S(1)}, u32[]{:S(2)}, u32[]{:S(2)}) collective-permute-start(bf16[256,2,256]{2,1,0:T(2,128)(2,1)S(1)} %collective-permute-done.16.refs_8_), channel_id=1, source_target_pairs={{0,4},{4,0},{8,12},{12,8},{16,20},{20,16},{24,28},{28,24},{1,5},{5... | collective-permute-start | bytes 786440 | tf_op jit(solution)/shard_map/ppermute | solution.py:379
  59.0 0.7 copy-done.10
  59.7 0.7 copy-done.12
  60.4 1.6 %collective-permute-start.17 = (bf16[256,2,256]{2,1,0:T(2,128)(2,1)S(1)}, bf16[256,2,256]{2,1,0:T(2,128)(2,1)S(1)}, u32[]{:S(2)}, u32[]{:S(2)}) collective-permute-start(bf16[256,2,256]{2,1,0:T(2,128)(2,1)S(1)} %get-tuple-element.33.refs_5_), channel_id=1, source_target_pairs={{0,8},{4,12},{8,16},{12,20},{16,24},{20,28},{24,0},{28,4},{1,9},{5... | collective-permute-start | bytes 786440 | tf_op jit(solution)/shard_map/ppermute | solution.py:378
  61.9 4.9 %collective-permute-done.20.refs_12_ = bf16[256,2,256]{2,1,0:T(2,128)(2,1)S(1)} collective-permute-done((bf16[256,2,256]{2,1,0:T(2,128)(2,1)S(1)}, bf16[256,2,256]{2,1,0:T(2,128)(2,1)S(1)}, u32[]{:S(2)}, u32[]{:S(2)}) %collective-permute-start.20) | collective-permute-done | bytes 262176 | tf_op jit(solution)/shard_map/ppermute | solution.py:378
  66.8 1.6 %collective-permute-start.15 = (bf16[256,2,256]{2,1,0:T(2,128)(2,1)S(1)}, bf16[256,2,256]{2,1,0:T(2,128)(2,1)S(1)}, u32[]{:S(2)}, u32[]{:S(2)}) collective-permute-start(bf16[256,2,256]{2,1,0:T(2,128)(2,1)S(1)} %get-tuple-element.33.refs_5_), channel_id=1, source_target_pairs={{0,4},{4,0},{8,12},{12,8},{16,20},{20,16},{24,28},{28,24},{1,5},{5... | collective-permute-start | bytes 786440 | tf_op jit(solution)/shard_map/ppermute | solution.py:379
  68.5 3.9 %collective-permute-done.17.refs_9_ = bf16[256,2,256]{2,1,0:T(2,128)(2,1)S(1)} collective-permute-done((bf16[256,2,256]{2,1,0:T(2,128)(2,1)S(1)}, bf16[256,2,256]{2,1,0:T(2,128)(2,1)S(1)}, u32[]{:S(2)}, u32[]{:S(2)}) %collective-permute-start.17) | collective-permute-done | bytes 262176 | tf_op jit(solution)/shard_map/ppermute | solution.py:378
  72.4 0.8 collective-permute-done.15.refs_7_
  73.2 0.7 copy-done.20
  73.9 1.6 %collective-permute-start.22 = (bf16[256,2,256]{2,1,0:T(2,128)(2,1)S(1)}, bf16[256,2,256]{2,1,0:T(2,128)(2,1)S(1)}, u32[]{:S(2)}, u32[]{:S(2)}) collective-permute-start(bf16[256,2,256]{2,1,0:T(2,128)(2,1)S(1)} %collective-permute-done.20.refs_12_), channel_id=1, source_target_pairs={{0,4},{4,0},{8,12},{12,8},{16,20},{20,16},{24,28},{28,24},{1,5},{5... | collective-permute-start | bytes 786440 | tf_op jit(solution)/shard_map/ppermute | solution.py:379
  75.5 3.7 %collective-permute-done.24.refs_16_ = bf16[256,2,256]{2,1,0:T(2,128)(2,1)S(1)} collective-permute-done((bf16[256,2,256]{2,1,0:T(2,128)(2,1)S(1)}, bf16[256,2,256]{2,1,0:T(2,128)(2,1)S(1)}, u32[]{:S(2)}, u32[]{:S(2)}) %collective-permute-start.24) | collective-permute-done | bytes 262176 | tf_op jit(solution)/shard_map/ppermute | solution.py:378
  79.9 0.7 copy-done.18
  80.6 1.6 %collective-permute-done.21.refs_13_ = bf16[256,2,256]{2,1,0:T(2,128)(2,1)} collective-permute-done((bf16[256,2,256]{2,1,0:T(2,128)(2,1)S(1)}, bf16[256,2,256]{2,1,0:T(2,128)(2,1)}, u32[]{:S(2)}, u32[]{:S(2)}) %collective-permute-start.21) | collective-permute-done | bytes 262176 | tf_op jit(solution)/shard_map/ppermute | solution.py:378
  82.2 0.9 collective-permute-done.22.refs_14_
  83.1 0.7 copy-done.24
  83.9 3.6 %collective-permute-done.19.refs_11_ = bf16[256,2,256]{2,1,0:T(2,128)(2,1)S(1)} collective-permute-done((bf16[256,2,256]{2,1,0:T(2,128)(2,1)S(1)}, bf16[256,2,256]{2,1,0:T(2,128)(2,1)S(1)}, u32[]{:S(2)}, u32[]{:S(2)}) %collective-permute-start.19) | collective-permute-done | bytes 262176 | tf_op jit(solution)/shard_map/ppermute | solution.py:379
  87.4 0.7 copy-done.26
  88.1 1.7 %collective-permute-start.26 = (bf16[256,2,256]{2,1,0:T(2,128)(2,1)S(1)}, bf16[256,2,256]{2,1,0:T(2,128)(2,1)S(1)}, u32[]{:S(2)}, u32[]{:S(2)}) collective-permute-start(bf16[256,2,256]{2,1,0:T(2,128)(2,1)S(1)} %collective-permute-done.24.refs_16_), channel_id=1, source_target_pairs={{0,4},{4,0},{8,12},{12,8},{16,20},{20,16},{24,28},{28,24},{1,5},{5... | collective-permute-start | bytes 786440 | tf_op jit(solution)/shard_map/ppermute | solution.py:379
  89.8 0.7 copy-done.22
  90.7 1.5 collective-permute-start.23
  92.8 3.7 %gate_up.3 = (bf16[128,768]{1,0:T(8,128)(2,1)S(1)}, bf16[128,768]{1,0:T(8,128)(2,1)}) custom-call(bf16[128,2048]{1,0:T(8,128)(2,1)S(1)} %collective-permute-done.10.first, bf16[128,2048]{1,0:T(8,128)(2,1)S(1)} %collective-permute-done.11.second, bf16[1,2048]{1,0:T(2,128)(2,1)S(1)} %reshape.53.ln, bf16[2048,768]{1,0:T(8,128)(2,1)S(1)} %copy-done, ...), custom_call_target="tpu_custom_call" | custom-call | flops 1610612736 | bytes 8388608 | tf_op jit(solution)/shard_map/gate_up/pallas_call | solution.py:199
  96.5 0.7 copy-done.30
  97.4 0.7 copy-done.28
  98.2 4.9 %collective-permute-done.23.refs_15_ = bf16[256,2,256]{2,1,0:T(2,128)(2,1)} collective-permute-done((bf16[256,2,256]{2,1,0:T(2,128)(2,1)}, bf16[256,2,256]{2,1,0:T(2,128)(2,1)}, u32[]{:S(2)}, u32[]{:S(2)}) %collective-permute-start.23) | collective-permute-done | bytes 262176 | tf_op jit(solution)/shard_map/ppermute | solution.py:379
  103.1 3.4 %collective-permute-done.27.refs_19_ = bf16[256,2,256]{2,1,0:T(2,128)(2,1)} collective-permute-done((bf16[256,2,256]{2,1,0:T(2,128)(2,1)}, bf16[256,2,256]{2,1,0:T(2,128)(2,1)}, u32[]{:S(2)}, u32[]{:S(2)}) %collective-permute-start.27) | collective-permute-done | bytes 262176 | tf_op jit(solution)/shard_map/ppermute | solution.py:379
  106.5 0.9 copy-done.9
  107.5 0.9 copy-done.11
  108.4 0.9 copy-done.13
  109.4 0.9 copy-done.15
  110.3 0.9 copy-done.17
  111.3 0.9 copy-done.19
  112.2 0.9 copy-done.21
  113.2 0.9 copy-done.23
  114.1 0.9 copy-done.25
  115.1 0.9 copy-done.27
  116.0 0.9 copy-done.29
  117.0 10.0 %fill_pages.1 = bf16[512,16,2,256]{3,2,1,0:T(2,128)(2,1)} custom-call(s32[19]{0:T(128)S(1)} %stack.79.place.refs_0_, s32[32]{0:T(128)S(1)} %reshape.49.bounds.refs_1_, s32[32]{0:T(128)S(1)} %copy-done.34, s32[32,16]{1,0:T(8,128)S(1)} %copy.20.refs_3_, bf16[256,2,256]{2,1,0:T(2,128)(2,1)S(1)} %get-tuple-element.32.refs_4_, ...), custom_call_target="tpu_custom_call" | custom-call | bytes 12582912 | tf_op jit(solution)/shard_map/fill_pages/pallas_call | solution.py:301
  127.0 4.2 %gate_up.2 = (bf16[128,768]{1,0:T(8,128)(2,1)S(1)}, bf16[128,768]{1,0:T(8,128)(2,1)S(1)}) custom-call(bf16[128,2048]{1,0:T(8,128)(2,1)} %fusion.2.first, bf16[128,2048]{1,0:T(8,128)(2,1)} %collective-permute-done.7.second, bf16[1,2048]{1,0:T(2,128)(2,1)S(1)} %reshape.53.ln, bf16[2048,768]{1,0:T(8,128)(2,1)S(1)} %copy-done, bf16[2048,768]{1,0:T(8,128)(2,1)S(1)} %copy-done.2), custom_call_target="tpu_custom_call" | custom-call | flops 1610612736 | bytes 8388608 | tf_op jit(solution)/shard_map/gate_up/pallas_call | solution.py:199
  131.3 2.7 %fusion.10 = f32[128,2048]{1,0:T(8,128)S(1)} fusion(bf16[128,768]{1,0:T(8,128)(2,1)} %collective-permute-done.12, bf16[768,2048]{1,0:T(8,128)(2,1)} %collective-permute-done.9), kind=kOutput, calls=%fused_computation.27 | convolution fusion | flops 402653184 | bytes 4390912 | tf_op jit(solution)/shard_map/dot_general | solution.py:22
  135.4 2.5 %fusion.9 = f32[128,2048]{1,0:T(8,128)S(1)} fusion(bf16[128,768]{1,0:T(8,128)(2,1)S(1)} %collective-permute-done.8, bf16[768,2048]{1,0:T(8,128)(2,1)} %collective-permute-done.9), kind=kOutput, calls=%fused_computation.26 | convolution fusion | flops 402653184 | bytes 4390912 | tf_op jit(solution)/shard_map/dot_general | solution.py:22
  138.5 10.4 %collective-permute-done.13 = bf16[128,2048]{1,0:T(8,128)(2,1)S(1)} collective-permute-done((bf16[128,2048]{1,0:T(8,128)(2,1)S(1)}, bf16[128,2048]{1,0:T(8,128)(2,1)S(1)}, u32[]{:S(2)}, u32[]{:S(2)}) %collective-permute-start.13) | collective-permute-done | bytes 524320 | tf_op jit(solution)/shard_map/ppermute | solution.py:353
  148.9 2.0 %add_convert_fusion = bf16[128,2048]{1,0:T(8,128)(2,1)} fusion(bf16[128,2048]{1,0:T(8,128)(2,1)S(1)} %collective-permute-done.13, f32[128,2048]{1,0:T(8,128)S(1)} %convolution_add_fusion.1, bf16[128,2048]{1,0:T(8,128)(2,1)} %fusion.2.first), kind=kLoop, calls=%fused_computation.9 | loop fusion | flops 1310720 | bytes 2621440 | tf_op jit(solution)/shard_map/convert_element_type | solution.py:403
  (99 shorter events, 6.7 us)
Async XLA Ops:
  0.6 18.1 %copy-start.3 = (bf16[2048,512]{1,0:T(8,128)(2,1)S(1)}, bf16[2048,512]{1,0:T(8,128)(2,1)}, u32[]{:S(2)}) copy-start(bf16[2048,512]{1,0:T(8,128)(2,1)} %wq.3) | copy-start | bytes 6291460
  0.6 35.3 %collective-permute-start.4 = (bf16[512,2048]{1,0:T(8,128)(2,1)}, bf16[512,2048]{1,0:T(8,128)(2,1)}, u32[]{:S(2)}, u32[]{:S(2)}) collective-permute-start(bf16[512,2048]{1,0:T(8,128)(2,1)} %param.25), channel_id=1, source_target_pairs={{0,1},{1,0},{2,3},{3,2},{4,5},{5,4},{6,7},{7,6},{8,9},{9,8},{10,11... | collective-permute-start | bytes 6291464 | tf_op jit(solution)/shard_map/ppermute | solution.py:350
  1.2 17.6 %collective-permute-start = (bf16[128,2048]{1,0:T(8,128)(2,1)}, bf16[128,2048]{1,0:T(8,128)(2,1)S(1)}, u32[]{:S(2)}, u32[]{:S(2)}) collective-permute-start(bf16[128,2048]{1,0:T(8,128)(2,1)} %own.1), channel_id=1, source_target_pairs={{0,1},{1,0},{2,3},{3,2},{4,5},{5,4},{6,7},{7,6},{8,9},{9,8},{10,11... | collective-permute-start | bytes 1572872 | tf_op jit(solution)/shard_map/ppermute | solution.py:350
  1.2 15.3 %collective-permute-start.1 = (bf16[128,2048]{1,0:T(8,128)(2,1)}, bf16[128,2048]{1,0:T(8,128)(2,1)S(1)}, u32[]{:S(2)}, u32[]{:S(2)}) collective-permute-start(bf16[128,2048]{1,0:T(8,128)(2,1)} %own.1), channel_id=1, source_target_pairs={{0,2},{1,3},{2,0},{3,1},{4,6},{5,7},{6,4},{7,5},{8,10},{9,11},{10,... | collective-permute-start | bytes 1572872 | tf_op jit(solution)/shard_map/ppermute | solution.py:353
  4.2 127.1 %collective-permute-start.9 = (bf16[768,2048]{1,0:T(8,128)(2,1)}, bf16[768,2048]{1,0:T(8,128)(2,1)}, u32[]{:S(2)}, u32[]{:S(2)}) collective-permute-start(bf16[768,2048]{1,0:T(8,128)(2,1)} %param.29), channel_id=1, source_target_pairs={{0,1},{1,0},{2,3},{3,2},{4,5},{5,4},{6,7},{7,6},{8,9},{9,8},{10,11... | collective-permute-start | bytes 9437192 | tf_op jit(solution)/shard_map/ppermute | solution.py:350
  16.5 9.7 %collective-permute-start.2 = (bf16[128,2048]{1,0:T(8,128)(2,1)S(1)}, bf16[128,2048]{1,0:T(8,128)(2,1)}, u32[]{:S(2)}, u32[]{:S(2)}) collective-permute-start(bf16[128,2048]{1,0:T(8,128)(2,1)S(1)} %collective-permute-done.1.own), channel_id=1, source_target_pairs={{0,1},{1,0},{2,3},{3,2},{4,5},{5,4},{6,7},{7,6},{8,9},{9,8},{10,11... | collective-permute-start | bytes 1572872 | tf_op jit(solution)/shard_map/ppermute | solution.py:350
  18.7 1.2 copy-start.4
  20.0 1.2 copy-start.5
  21.2 1.0 copy-start.6
  29.4 37.4 %copy-start.8 = (bf16[256,2,256]{2,1,0:T(2,128)(2,1)}, bf16[256,2,256]{2,1,0:T(2,128)(2,1)S(1)}, u32[]{:S(2)}) copy-start(bf16[256,2,256]{2,1,0:T(2,128)(2,1)S(1)} %get-tuple-element.33.refs_5_) | copy-start | bytes 786436
  29.4 8.6 %copy-start.36 = (bf16[512,2048]{1,0:T(8,128)(2,1)S(1)}, bf16[512,2048]{1,0:T(8,128)(2,1)}, u32[]{:S(2)}) copy-start(bf16[512,2048]{1,0:T(8,128)(2,1)} %param.25) | copy-start | bytes 6291460
  34.5 1.4 collective-permute-start.5
  38.0 14.7 %copy-start.7 = (bf16[128,2048]{1,0:T(8,128)(2,1)S(1)}, bf16[128,2048]{1,0:T(8,128)(2,1)}, u32[]{:S(2)}) copy-start(bf16[128,2048]{1,0:T(8,128)(2,1)} %own.1) | copy-start | bytes 1572868
  38.5 14.2 %collective-permute-start.6 = (bf16[128,2048]{1,0:T(8,128)(2,1)S(1)}, bf16[128,2048]{1,0:T(8,128)(2,1)S(1)}, u32[]{:S(2)}, u32[]{:S(2)}) collective-permute-start(bf16[128,2048]{1,0:T(8,128)(2,1)S(1)} %fusion.3), channel_id=1, source_target_pairs={{0,2},{1,3},{2,0},{3,1},{4,6},{5,7},{6,4},{7,5},{8,10},{9,11},{10,... | collective-permute-start | bytes 1572872 | tf_op jit(solution)/shard_map/ppermute | solution.py:353
  40.3 3.2 %collective-permute-start.3 = (bf16[128,512]{1,0:T(8,128)(2,1)S(1)}, bf16[128,512]{1,0:T(8,128)(2,1)S(1)}, u32[]{:S(2)}, u32[]{:S(2)}) collective-permute-start(bf16[128,512]{1,0:T(8,128)(2,1)S(1)} %get-tuple-element.25), channel_id=1, source_target_pairs={{0,1},{1,0},{2,3},{3,2},{4,5},{5,4},{6,7},{7,6},{8,9},{9,8},{10,11... | collective-permute-start | bytes 393224 | tf_op jit(solution)/shard_map/ppermute | solution.py:350
  40.3 15.5 %collective-permute-start.16 = (bf16[256,2,256]{2,1,0:T(2,128)(2,1)S(1)}, bf16[256,2,256]{2,1,0:T(2,128)(2,1)S(1)}, u32[]{:S(2)}, u32[]{:S(2)}) collective-permute-start(bf16[256,2,256]{2,1,0:T(2,128)(2,1)S(1)} %get-tuple-element.32.refs_4_), channel_id=1, source_target_pairs={{0,8},{4,12},{8,16},{12,20},{16,24},{20,28},{24,0},{28,4},{1,9},{5... | collective-permute-start | bytes 786440 | tf_op jit(solution)/shard_map/ppermute | solution.py:378
  41.9 17.8 %collective-permute-start.14 = (bf16[256,2,256]{2,1,0:T(2,128)(2,1)S(1)}, bf16[256,2,256]{2,1,0:T(2,128)(2,1)S(1)}, u32[]{:S(2)}, u32[]{:S(2)}) collective-permute-start(bf16[256,2,256]{2,1,0:T(2,128)(2,1)S(1)} %get-tuple-element.32.refs_4_), channel_id=1, source_target_pairs={{0,4},{4,0},{8,12},{12,8},{16,20},{20,16},{24,28},{28,24},{1,5},{5... | collective-permute-start | bytes 786440 | tf_op jit(solution)/shard_map/ppermute | solution.py:379
  43.4 49.3 %copy-start.1 = (bf16[2048,768]{1,0:T(8,128)(2,1)S(1)}, bf16[2048,768]{1,0:T(8,128)(2,1)}, u32[]{:S(2)}) copy-start(bf16[2048,768]{1,0:T(8,128)(2,1)} %wu.3) | copy-start | bytes 9437188
  45.6 47.1 %copy-start.38 = (bf16[2048]{0:T(1024)(128)(2,1)S(1)}, bf16[2048]{0:T(1024)(128)(2,1)}, u32[]{:S(2)}) copy-start(bf16[2048]{0:T(1024)(128)(2,1)} %param.26) | copy-start | bytes 12292
  45.6 47.1 %copy-start = (bf16[2048,768]{1,0:T(8,128)(2,1)S(1)}, bf16[2048,768]{1,0:T(8,128)(2,1)}, u32[]{:S(2)}) copy-start(bf16[2048,768]{1,0:T(8,128)(2,1)} %wg.3) | copy-start | bytes 9437188
  54.1 18.2 %collective-permute-start.10 = (bf16[128,2048]{1,0:T(8,128)(2,1)}, bf16[128,2048]{1,0:T(8,128)(2,1)S(1)}, u32[]{:S(2)}, u32[]{:S(2)}) collective-permute-start(bf16[128,2048]{1,0:T(8,128)(2,1)} %fusion.2.first), channel_id=1, source_target_pairs={{0,2},{1,3},{2,0},{3,1},{4,6},{5,7},{6,4},{7,5},{8,10},{9,11},{10,... | collective-permute-start | bytes 1572872 | tf_op jit(solution)/shard_map/ppermute | solution.py:353
  55.9 11.0 %collective-permute-start.20 = (bf16[256,2,256]{2,1,0:T(2,128)(2,1)S(1)}, bf16[256,2,256]{2,1,0:T(2,128)(2,1)S(1)}, u32[]{:S(2)}, u32[]{:S(2)}) collective-permute-start(bf16[256,2,256]{2,1,0:T(2,128)(2,1)S(1)} %collective-permute-done.16.refs_8_), channel_id=1, source_target_pairs={{0,8},{4,12},{8,16},{12,20},{16,24},{20,28},{24,0},{28,4},{1,9},{5... | collective-permute-start | bytes 786440 | tf_op jit(solution)/shard_map/ppermute | solution.py:378
  57.5 11.0 %collective-permute-start.18 = (bf16[256,2,256]{2,1,0:T(2,128)(2,1)S(1)}, bf16[256,2,256]{2,1,0:T(2,128)(2,1)S(1)}, u32[]{:S(2)}, u32[]{:S(2)}) collective-permute-start(bf16[256,2,256]{2,1,0:T(2,128)(2,1)S(1)} %collective-permute-done.16.refs_8_), channel_id=1, source_target_pairs={{0,4},{4,0},{8,12},{12,8},{16,20},{20,16},{24,28},{28,24},{1,5},{5... | collective-permute-start | bytes 786440 | tf_op jit(solution)/shard_map/ppermute | solution.py:379
  59.0 0.7 copy-start.10
  60.4 12.0 %collective-permute-start.17 = (bf16[256,2,256]{2,1,0:T(2,128)(2,1)S(1)}, bf16[256,2,256]{2,1,0:T(2,128)(2,1)S(1)}, u32[]{:S(2)}, u32[]{:S(2)}) collective-permute-start(bf16[256,2,256]{2,1,0:T(2,128)(2,1)S(1)} %get-tuple-element.33.refs_5_), channel_id=1, source_target_pairs={{0,8},{4,12},{8,16},{12,20},{16,24},{20,28},{24,0},{28,4},{1,9},{5... | collective-permute-start | bytes 786440 | tf_op jit(solution)/shard_map/ppermute | solution.py:378
  66.8 29.7 %copy-start.14 = (bf16[256,2,256]{2,1,0:T(2,128)(2,1)}, bf16[256,2,256]{2,1,0:T(2,128)(2,1)S(1)}, u32[]{:S(2)}) copy-start(bf16[256,2,256]{2,1,0:T(2,128)(2,1)S(1)} %collective-permute-done.20.refs_12_) | copy-start | bytes 786436
  66.8 6.4 %collective-permute-start.15 = (bf16[256,2,256]{2,1,0:T(2,128)(2,1)S(1)}, bf16[256,2,256]{2,1,0:T(2,128)(2,1)S(1)}, u32[]{:S(2)}, u32[]{:S(2)}) collective-permute-start(bf16[256,2,256]{2,1,0:T(2,128)(2,1)S(1)} %get-tuple-element.33.refs_5_), channel_id=1, source_target_pairs={{0,4},{4,0},{8,12},{12,8},{16,20},{20,16},{24,28},{28,24},{1,5},{5... | collective-permute-start | bytes 786440 | tf_op jit(solution)/shard_map/ppermute | solution.py:379
  68.5 28.1 %copy-start.16 = (bf16[256,2,256]{2,1,0:T(2,128)(2,1)}, bf16[256,2,256]{2,1,0:T(2,128)(2,1)S(1)}, u32[]{:S(2)}) copy-start(bf16[256,2,256]{2,1,0:T(2,128)(2,1)S(1)} %collective-permute-done.18.refs_10_) | copy-start | bytes 786436
  68.5 10.8 %collective-permute-start.24 = (bf16[256,2,256]{2,1,0:T(2,128)(2,1)S(1)}, bf16[256,2,256]{2,1,0:T(2,128)(2,1)S(1)}, u32[]{:S(2)}, u32[]{:S(2)}) collective-permute-start(bf16[256,2,256]{2,1,0:T(2,128)(2,1)S(1)} %collective-permute-done.20.refs_12_), channel_id=1, source_target_pairs={{0,8},{4,12},{8,16},{12,20},{16,24},{20,28},{24,0},{28,4},{1,9},{5... | collective-permute-start | bytes 786440 | tf_op jit(solution)/shard_map/ppermute | solution.py:378
  72.4 9.8 %collective-permute-start.21 = (bf16[256,2,256]{2,1,0:T(2,128)(2,1)S(1)}, bf16[256,2,256]{2,1,0:T(2,128)(2,1)}, u32[]{:S(2)}, u32[]{:S(2)}) collective-permute-start(bf16[256,2,256]{2,1,0:T(2,128)(2,1)S(1)} %collective-permute-done.17.refs_9_), channel_id=1, source_target_pairs={{0,8},{4,12},{8,16},{12,20},{16,24},{20,28},{24,0},{28,4},{1,9},{5... | collective-permute-start | bytes 786440 | tf_op jit(solution)/shard_map/ppermute | solution.py:378
  72.4 19.8 %collective-permute-start.11 = (bf16[128,2048]{1,0:T(8,128)(2,1)S(1)}, bf16[128,2048]{1,0:T(8,128)(2,1)S(1)}, u32[]{:S(2)}, u32[]{:S(2)}) collective-permute-start(bf16[128,2048]{1,0:T(8,128)(2,1)S(1)} %collective-permute-done.10.first), channel_id=1, source_target_pairs={{0,1},{1,0},{2,3},{3,2},{4,5},{5,4},{6,7},{7,6},{8,9},{9,8},{10,11... | collective-permute-start | bytes 1572872 | tf_op jit(solution)/shard_map/ppermute | solution.py:350
  73.2 0.7 copy-start.20
  73.9 9.2 %collective-permute-start.22 = (bf16[256,2,256]{2,1,0:T(2,128)(2,1)S(1)}, bf16[256,2,256]{2,1,0:T(2,128)(2,1)S(1)}, u32[]{:S(2)}, u32[]{:S(2)}) collective-permute-start(bf16[256,2,256]{2,1,0:T(2,128)(2,1)S(1)} %collective-permute-done.20.refs_12_), channel_id=1, source_target_pairs={{0,4},{4,0},{8,12},{12,8},{16,20},{20,16},{24,28},{28,24},{1,5},{5... | collective-permute-start | bytes 786440 | tf_op jit(solution)/shard_map/ppermute | solution.py:379
  79.3 8.1 %collective-permute-start.19 = (bf16[256,2,256]{2,1,0:T(2,128)(2,1)S(1)}, bf16[256,2,256]{2,1,0:T(2,128)(2,1)S(1)}, u32[]{:S(2)}, u32[]{:S(2)}) collective-permute-start(bf16[256,2,256]{2,1,0:T(2,128)(2,1)S(1)} %collective-permute-done.17.refs_9_), channel_id=1, source_target_pairs={{0,4},{4,0},{8,12},{12,8},{16,20},{20,16},{24,28},{28,24},{1,5},{5... | collective-permute-start | bytes 786440 | tf_op jit(solution)/shard_map/ppermute | solution.py:379
  79.9 0.7 copy-start.18
  82.2 8.5 %collective-permute-start.25 = (bf16[256,2,256]{2,1,0:T(2,128)(2,1)}, bf16[256,2,256]{2,1,0:T(2,128)(2,1)}, u32[]{:S(2)}, u32[]{:S(2)}) collective-permute-start(bf16[256,2,256]{2,1,0:T(2,128)(2,1)} %collective-permute-done.21.refs_13_), channel_id=1, source_target_pairs={{0,8},{4,12},{8,16},{12,20},{16,24},{20,28},{24,0},{28,4},{1,9},{5... | collective-permute-start | bytes 786440 | tf_op jit(solution)/shard_map/ppermute | solution.py:378
  83.1 0.7 copy-start.24
  83.9 43.1 %collective-permute-start.7 = (bf16[128,2048]{1,0:T(8,128)(2,1)}, bf16[128,2048]{1,0:T(8,128)(2,1)}, u32[]{:S(2)}, u32[]{:S(2)}) collective-permute-start(bf16[128,2048]{1,0:T(8,128)(2,1)} %fusion.2.first), channel_id=1, source_target_pairs={{0,1},{1,0},{2,3},{3,2},{4,5},{5,4},{6,7},{7,6},{8,9},{9,8},{10,11... | collective-permute-start | bytes 1572872 | tf_op jit(solution)/shard_map/ppermute | solution.py:350
  87.4 0.7 copy-start.26
  88.1 9.2 %collective-permute-start.26 = (bf16[256,2,256]{2,1,0:T(2,128)(2,1)S(1)}, bf16[256,2,256]{2,1,0:T(2,128)(2,1)S(1)}, u32[]{:S(2)}, u32[]{:S(2)}) collective-permute-start(bf16[256,2,256]{2,1,0:T(2,128)(2,1)S(1)} %collective-permute-done.24.refs_16_), channel_id=1, source_target_pairs={{0,4},{4,0},{8,12},{12,8},{16,20},{20,16},{24,28},{28,24},{1,5},{5... | collective-permute-start | bytes 786440 | tf_op jit(solution)/shard_map/ppermute | solution.py:379
  89.8 0.7 copy-start.22
  90.7 12.4 %collective-permute-start.23 = (bf16[256,2,256]{2,1,0:T(2,128)(2,1)}, bf16[256,2,256]{2,1,0:T(2,128)(2,1)}, u32[]{:S(2)}, u32[]{:S(2)}) collective-permute-start(bf16[256,2,256]{2,1,0:T(2,128)(2,1)} %collective-permute-done.21.refs_13_), channel_id=1, source_target_pairs={{0,4},{4,0},{8,12},{12,8},{16,20},{20,16},{24,28},{28,24},{1,5},{5... | collective-permute-start | bytes 786440 | tf_op jit(solution)/shard_map/ppermute | solution.py:379
  92.1 14.4 %collective-permute-start.27 = (bf16[256,2,256]{2,1,0:T(2,128)(2,1)}, bf16[256,2,256]{2,1,0:T(2,128)(2,1)}, u32[]{:S(2)}, u32[]{:S(2)}) collective-permute-start(bf16[256,2,256]{2,1,0:T(2,128)(2,1)} %collective-permute-done.25.refs_17_), channel_id=1, source_target_pairs={{0,4},{4,0},{8,12},{12,8},{16,20},{20,16},{24,28},{28,24},{1,5},{5... | collective-permute-start | bytes 786440 | tf_op jit(solution)/shard_map/ppermute | solution.py:379
  92.7 5.4 %copy-start.37 = (s32[32,16]{0,1:T(8,128)S(1)}, s32[32,16]{0,1:T(8,128)}, u32[]{:S(2)}) copy-start(s32[32,16]{0,1:T(8,128)} %param.18) | copy-start | bytes 6148
  92.8 13.8 %copy-start.34 = (s32[32]{0:T(128)S(1)}, s32[32]{0:T(128)}, u32[]{:S(2)}) copy-start(s32[32]{0:T(128)} %refs_2_.1) | copy-start | bytes 388
  96.5 0.7 copy-start.30
  97.4 0.7 copy-start.28
  98.1 33.2 %collective-permute-start.12 = (bf16[128,768]{1,0:T(8,128)(2,1)}, bf16[128,768]{1,0:T(8,128)(2,1)}, u32[]{:S(2)}, u32[]{:S(2)}) collective-permute-start(bf16[128,768]{1,0:T(8,128)(2,1)} %get-tuple-element.31), channel_id=1, source_target_pairs={{0,1},{1,0},{2,3},{3,2},{4,5},{5,4},{6,7},{7,6},{8,9},{9,8},{10,11... | collective-permute-start | bytes 589832 | tf_op jit(solution)/shard_map/ppermute | solution.py:350
  98.2 28.8 %copy-start.2 = (bf16[2048,768]{1,0:T(8,128)(2,1)S(1)}, bf16[2048,768]{1,0:T(8,128)(2,1)}, u32[]{:S(2)}) copy-start(bf16[2048,768]{1,0:T(8,128)(2,1)} %wu.3) | copy-start | bytes 9437188
  106.5 1.0 copy-start.9
  107.5 0.9 copy-start.11
  108.4 0.9 copy-start.13
  109.4 0.9 copy-start.15
  110.3 0.9 copy-start.17
  111.3 0.9 copy-start.19
  112.2 0.9 copy-start.21
  113.2 0.9 copy-start.23
  114.1 0.9 copy-start.25
  115.1 0.9 copy-start.27
  116.0 0.9 copy-start.29
  131.2 2.8 %copy-start.31 = (bf16[128,768]{1,0:T(8,128)(2,1)S(1)}, bf16[128,768]{1,0:T(8,128)(2,1)}, u32[]{:S(2)}) copy-start(bf16[128,768]{1,0:T(8,128)(2,1)} %copy-done.30) | copy-start | bytes 589828
  131.2 3.0 %copy-start.35 = (bf16[768,2048]{1,0:T(8,128)(2,1)S(1)}, bf16[768,2048]{1,0:T(8,128)(2,1)}, u32[]{:S(2)}) copy-start(bf16[768,2048]{1,0:T(8,128)(2,1)} %param.29) | copy-start | bytes 9437188
  131.2 4.2 %collective-permute-start.8 = (bf16[128,768]{1,0:T(8,128)(2,1)S(1)}, bf16[128,768]{1,0:T(8,128)(2,1)S(1)}, u32[]{:S(2)}, u32[]{:S(2)}) collective-permute-start(bf16[128,768]{1,0:T(8,128)(2,1)S(1)} %get-tuple-element.29), channel_id=1, source_target_pairs={{0,1},{1,0},{2,3},{3,2},{4,5},{5,4},{6,7},{7,6},{8,9},{9,8},{10,11... | collective-permute-start | bytes 589832 | tf_op jit(solution)/shard_map/ppermute | solution.py:350
  134.8 14.1 %collective-permute-start.13 = (bf16[128,2048]{1,0:T(8,128)(2,1)S(1)}, bf16[128,2048]{1,0:T(8,128)(2,1)S(1)}, u32[]{:S(2)}, u32[]{:S(2)}) collective-permute-start(bf16[128,2048]{1,0:T(8,128)(2,1)S(1)} %fusion.4), channel_id=1, source_target_pairs={{0,2},{1,3},{2,0},{3,1},{4,6},{5,7},{6,4},{7,5},{8,10},{9,11},{10,... | collective-permute-start | bytes 1572872 | tf_op jit(solution)/shard_map/ppermute | solution.py:353
  (3 other events, 2.0 us)

commit v3 on v2

v3 whole, which is shorter than its diff:
```python
import functools
import math

import jax
import jax.numpy as jnp
import numpy as np
from jax import lax
from jax.experimental import pallas as pl
from jax.experimental.pallas import tpu as pltpu
from jax.sharding import PartitionSpec as P

HD = 128
PROMPTS_DEV = 3
PAGE = 16
EPS = 1e-06
THETA = 1000000.0
SMEM = pl.BlockSpec(memory_space=pltpu.SMEM)
VMEM = pl.BlockSpec(memory_space=pltpu.VMEM)
ANY = pl.BlockSpec(memory_space=pl.ANY)
FAR = pl.BlockSpec(memory_space=pltpu.HBM)
MOST = 60 << 20
BRIEF = pl.CostEstimate(flops=1, bytes_accessed=1, transcendentals=0)


def dot(a, b):
    return jnp.dot(a, b, preferred_element_type=jnp.float32)


def ordered(value, *earlier):
    return lax.optimization_barrier((value,) + earlier)[0]


def normalized(wide, gain):
    return wide * lax.rsqrt(jnp.mean(wide * wide, axis=-1, keepdims=True) + EPS) * gain


def segment_bounds(segment_ids):
    limits = jnp.arange(PROMPTS_DEV + 1, dtype=jnp.int32)
    below = segment_ids[:, None, :] < limits[None, :, None]
    return jnp.sum(below.astype(jnp.int32), axis=2).reshape(-1)


def turns(rows):
    freq = THETA ** (-(np.arange(HD // 2) * 2.0) / HD)
    angle = np.arange(rows)[:, None] * np.concatenate([freq, freq])[None, :]
    return np.cos(angle).astype(np.float32), np.sin(angle).astype(np.float32)


def angles(ids, req, first, cos_rows, sin_rows):
    row = ids[pl.ds(req, 1), :]
    begins = [jnp.sum((row < s).astype(jnp.int32)) for s in range(1, PROMPTS_DEV)]
    line = lax.broadcasted_iota(jnp.int32, (8, HD), 0)
    lane = lax.broadcasted_iota(jnp.int32, (8, HD), 1)
    turn = jnp.where(lane < HD // 2, lane, lane - HD // 2).astype(jnp.float32)
    back = jnp.zeros((8, HD), jnp.float32)
    for s, begin in enumerate(begins):
        back = jnp.where(line == s + 1, begin.astype(jnp.float32), back)
    back = back * jnp.exp(turn * (-2.0 / HD * math.log(THETA)))
    back_cos, back_sin = jnp.cos(back), jnp.sin(back)
    token = first + lax.broadcasted_iota(jnp.int32, cos_rows.shape, 0)
    less_cos, less_sin = back_cos[0:1, :], back_sin[0:1, :]
    for s, begin in enumerate(begins):
        later = token >= begin
        less_cos = jnp.where(later, back_cos[s + 1 : s + 2, :], less_cos)
        less_sin = jnp.where(later, back_sin[s + 1 : s + 2, :], less_sin)
    cosine = cos_rows * less_cos + sin_rows * less_sin
    sine = sin_rows * less_cos - cos_rows * less_sin
    first_half = lax.broadcasted_iota(jnp.int32, cos_rows.shape, 1) < HD // 2
    return cosine, jnp.where(first_half, -sine, sine), begins


def turned_heads(wide, gain_ref, cosine, sine, out, at):
    gain = gain_ref[...].astype(jnp.float32)
    for h in range(wide.shape[1] // HD):
        one = normalized(wide[:, h * HD : (h + 1) * HD], gain)
        turned = one * cosine + pltpu.roll(one, HD // 2, 1) * sine
        out[at, h * HD : (h + 1) * HD] = turned.astype(jnp.bfloat16)


def joined_heads(k, v):
    shape = (k.shape[0], k.shape[1] // HD, HD)
    return jnp.concatenate([k.reshape(shape), v.reshape(shape)], axis=-1)


def split_copies(moves, sems):
    copies, used = [], 0
    for source, target, parts in moves:
        step = source.shape[0] // parts
        group = []
        for i in range(parts):
            cut = pl.ds(i * step, step)
            group.append(pltpu.make_async_copy(source.at[cut], target.at[cut], sems.at[used]))
            used += 1
        copies.append(group)
    for group in copies:
        for copy in group:
            copy.start()
    return copies


def wait_all(group):
    for copy in group:
        copy.wait()


def keys_kernel(pieces, swapped, place, ids, *refs):
    rows_far = refs[: 1 + pieces]
    ln, wk_far, wv_far, kg, cos, sin = refs[1 + pieces : 7 + pieces]
    k, v, pairs, normed = refs[7 + pieces : 11 + pieces]
    raw, wk, wv, cos_rows, sin_rows, sems = refs[11 + pieces :]
    req, side, core = place[0], place[1], place[2]
    if swapped:
        side = 1 - side
    half = raw.shape[0]
    count = half // 2
    here = pl.ds(pl.multiple_of(side * half, half), half)
    moves = []
    at = core * count
    for i, far in enumerate(rows_far):
        step = far.shape[0]
        moves.append((far, raw.at[pl.ds(pl.multiple_of(at, step), step)], 2 if i == 0 else 1))
        at = at + step if i else (1 - core) * count
    moves += [
        (cos.at[here], cos_rows, 1),
        (sin.at[here], sin_rows, 1),
        (wk_far, wk, 4),
        (wv_far, wv, 4),
    ]
    copies = split_copies(moves, sems)
    for group in copies[:-2]:
        wait_all(group)
    gain = ln[...].astype(jnp.float32)
    normed[...] = normalized(raw[...].astype(jnp.float32), gain).astype(jnp.bfloat16)
    cosine, sine, _ = angles(ids, req, side * half, cos_rows[...], sin_rows[...])
    wait_all(copies[-2])
    turned_heads(dot(normed[...], wk[...]), kg, cosine, sine, k, slice(None))
    wait_all(copies[-1])
    v[...] = dot(normed[...], wv[...]).astype(jnp.bfloat16)
    pairs[...] = joined_heads(k[...], v[...])


def keys_of(place, ids, own, others, ln, wk, wv, kg, cos, sin, swapped):
    half, width = 2 * own.shape[0], own.shape[1]
    kv = wk.shape[1]
    bf = jnp.bfloat16
    return pl.pallas_call(
        functools.partial(keys_kernel, len(others), swapped),
        out_shape=[
            jax.ShapeDtypeStruct((half, kv), bf),
            jax.ShapeDtypeStruct((half, kv), bf),
            jax.ShapeDtypeStruct((half, kv // HD, 2 * HD), bf),
            jax.ShapeDtypeStruct((half, width), bf),
        ],
        in_specs=[SMEM, VMEM]
        + [FAR] * (1 + len(others))
        + [VMEM, FAR, FAR, VMEM, FAR, FAR],
        out_specs=[VMEM] * 4,
        scratch_shapes=[
            pltpu.VMEM((half, width), bf),
            pltpu.VMEM(wk.shape, bf),
            pltpu.VMEM(wv.shape, bf),
            pltpu.VMEM((half, HD), jnp.float32),
            pltpu.VMEM((half, HD), jnp.float32),
            pltpu.SemaphoreType.DMA((12 + 2 * len(others),)),
        ],
        compiler_params=pltpu.CompilerParams(vmem_limit_bytes=MOST),
        cost_estimate=BRIEF,
        name="keys_of",
    )(place, ids, own, *others, ln, wk, wv, kg, cos, sin)


def attend_kernel(
    place, ids, near_far, far_far, wq_far, qg, cos, sin, ka, va, kb, vb, keep, send,
    normed, wq, cos_rows, sin_rows, q, k, v, sems,
):
    req, side, core = place[0], place[1], place[2]
    half = near_far.shape[0]
    count = half // 2
    near = pl.ds(pl.multiple_of(side * half, half), half)
    far = pl.ds(pl.multiple_of((1 - side) * half, half), half)
    copies = split_copies(
        (
            (wq_far, wq, 8),
            (near_far, normed.at[near], 4),
            (far_far, normed.at[far], 4),
            (cos, cos_rows, 1),
            (sin, sin_rows, 1),
            (ka, k.at[near], 1),
            (va, v.at[near], 1),
            (kb, k.at[far], 1),
            (vb, v.at[far], 1),
        ),
        sems,
    )
    for group in copies[3:]:
        wait_all(group)
    cosine, sine, begins = angles(ids, req, 0, cos_rows[...], sin_rows[...])
    for group in copies[:3]:
        wait_all(group)
    turned_heads(dot(normed[...], wq[...]), qg, cosine, sine, q, slice(None))

    kv_here = k.shape[1] // HD
    group = q.shape[1] // k.shape[1]
    scale = 1.0 / math.sqrt(HD)
    for block in range(4):
        seen = (block + 1) * count
        token = block * count + lax.broadcasted_iota(jnp.int32, (count, seen), 0)
        column = lax.broadcasted_iota(jnp.int32, (count, seen), 1)
        start = jnp.zeros_like(token)
        for begin in begins:
            start = jnp.where(token >= begin, begin, start)
        allowed = (column <= token) & (column >= start)
        mixed = []
        for j in range(kv_here):
            lanes = slice(j * HD, (j + 1) * HD)
            for h in range(j * group, (j + 1) * group):
                scores = lax.dot_general(
                    q[block * count : seen, h * HD : (h + 1) * HD],
                    k[:seen, lanes],
                    (((1,), (1,)), ((), ())),
                    preferred_element_type=jnp.float32,
                )
                raised = jnp.where(allowed, jnp.exp(scores * scale), 0.0)
                share = 1.0 / jnp.sum(raised, axis=-1, keepdims=True)
                mixed.append(
                    dot((raised * share).astype(jnp.bfloat16), v[:seen, lanes]).astype(
                        jnp.bfloat16
                    )
                )
        for distance in range(4):
            out = send if distance % 2 else keep
            at = slice(distance // 2 * count, (distance // 2 + 1) * count)

            @pl.when((block ^ (2 * side + core)) == distance)
            def _(out=out, at=at, mixed=tuple(mixed)):
                for h, one in enumerate(mixed):
                    out[at, h * HD : (h + 1) * HD] = one


def attend(place, ids, near, far, wq, qg, cos, sin, ka, va, kb, vb):
    half, width = near.shape
    rows = 2 * half
    kv = ka.shape[1]
    bf = jnp.bfloat16
    return pl.pallas_call(
        attend_kernel,
        out_shape=[jax.ShapeDtypeStruct((half, wq.shape[1]), bf)] * 2,
        in_specs=[SMEM, VMEM, FAR, FAR, FAR, VMEM] + [FAR] * 6,
        out_specs=[VMEM] * 2,
        scratch_shapes=[
            pltpu.VMEM((rows, width), bf),
            pltpu.VMEM(wq.shape, bf),
            pltpu.VMEM((rows, HD), jnp.float32),
            pltpu.VMEM((rows, HD), jnp.float32),
            pltpu.VMEM((rows, wq.shape[1]), bf),
            pltpu.VMEM((rows, kv), bf),
            pltpu.VMEM((rows, kv), bf),
            pltpu.SemaphoreType.DMA((22,)),
        ],
        compiler_params=pltpu.CompilerParams(vmem_limit_bytes=MOST),
        cost_estimate=BRIEF,
        name="attend",
    )(place, ids, near, far, wq, qg, cos, sin, ka, va, kb, vb)


def mlp_kernel(pieces, *refs):
    ln, wg, wu, keep, send, normed = refs[pieces:]
    count = keep.shape[0]
    gain = ln[...].astype(jnp.float32)
    at = 0
    for ref in refs[:pieces]:
        normed[at : at + ref.shape[0], :] = normalized(
            ref[...].astype(jnp.float32), gain
        ).astype(jnp.bfloat16)
        at += ref.shape[0]
    rows = normed[...]
    step = 256
    for at in range(0, wg.shape[1], step):
        lanes = slice(at, at + step)
        gate = dot(rows, wg[:, lanes])
        upper = dot(rows, wu[:, lanes])
        hidden = (gate / (1.0 + jnp.exp(-gate)) * upper).astype(jnp.bfloat16)
        keep[:, lanes] = hidden[:count]
        send[:, lanes] = hidden[count:]


def mlp(first, others, ln, wg, wu):
    count, width = first.shape
    out = jax.ShapeDtypeStruct((count, wg.shape[1]), jnp.bfloat16)
    return pl.pallas_call(
        functools.partial(mlp_kernel, 1 + len(others)),
        out_shape=[out] * 2,
        in_specs=[VMEM] * (4 + len(others)),
        out_specs=[VMEM] * 2,
        scratch_shapes=[pltpu.VMEM((2 * count, width), jnp.bfloat16)],
        compiler_params=pltpu.CompilerParams(vmem_limit_bytes=24 << 20),
        cost_estimate=BRIEF,
        name="gate_up",
    )(first, *others, ln, wg, wu)


def page_kernel(rows, requests, entries, blocks, *refs):
    place, bounds, prompts, table = refs[:4]
    arrived = refs[4 : 4 + blocks]
    out, held, blank, load_sems, sems = refs[4 + blocks :]
    half = rows // 2
    loads = [
        pltpu.make_async_copy(
            ref, held.at[pl.ds(pl.multiple_of(place[3 + i] * half, half), half)], load_sems.at[i]
        )
        for i, ref in enumerate(arrived)
    ]
    for load in loads:
        load.start()
    blank[...] = jnp.zeros_like(blank)
    for load in loads:
        load.wait()

    def pieces(amount, first, start):
        for size in (8, 4, 2, 1):
            skipped = amount - amount % (2 * size)

            @pl.when((amount // size) % 2 == 1)
            def _():
                start(first + skipped, size)

    def issue(r, carry):
        prompt = prompts[r]
        g = prompt // PROMPTS_DEV
        slot = g * (PROMPTS_DEV + 1) + prompt - g * PROMPTS_DEV
        begin = bounds[slot]
        length = bounds[slot + 1] - begin
        begin = g * rows + begin
        full = length // PAGE
        rest = length - full * PAGE

        def copy_page(e, c):
            pltpu.make_async_copy(
                held.at[pl.ds(begin + e * PAGE, PAGE)], out.at[table[r, e]], sems.at[r]
            ).start()
            return c

        lax.fori_loop(0, full, copy_page, 0)

        @pl.when(rest > 0)
        def _():
            page = table[r, full]
            base = begin + full * PAGE

            def kept(at, size):
                pltpu.make_async_copy(
                    held.at[pl.ds(base + at, size)], out.at[page, pl.ds(at, size)], sems.at[r]
                ).start()

            def blanked(at, size):
                pltpu.make_async_copy(
                    blank.at[pl.ds(0, size)], out.at[page, pl.ds(at, size)], sems.at[r]
                ).start()

            pieces(rest, 0, kept)
            pieces(PAGE - rest, rest, blanked)

        def clear_page(e, c):
            pltpu.make_async_copy(blank, out.at[table[r, e]], sems.at[r]).start()
            return c

        lax.fori_loop((length + PAGE - 1) // PAGE, entries, clear_page, 0)
        return carry

    lax.fori_loop(0, requests, issue, 0)

    def finish(r, carry):
        pltpu.make_async_copy(
            out.at[pl.ds(0, entries)], out.at[pl.ds(0, entries)], sems.at[r]
        ).wait()
        return carry

    lax.fori_loop(0, requests, finish, 0)


def fill_pages(place, bounds, request_prompt, page_table, arrived, rows):
    requests, entries = page_table.shape
    row_shape, dtype = arrived[0].shape[1:], arrived[0].dtype
    blocks = len(arrived)
    return pl.pallas_call(
        functools.partial(page_kernel, rows, requests, entries, blocks),
        out_shape=jax.ShapeDtypeStruct((requests * entries, PAGE) + row_shape, dtype),
        in_specs=[SMEM] * 4 + [FAR] * blocks,
        out_specs=ANY,
        scratch_shapes=[
            pltpu.VMEM((blocks * rows // 2,) + row_shape, dtype),
            pltpu.VMEM((PAGE,) + row_shape, dtype),
            pltpu.SemaphoreType.DMA((blocks,)),
            pltpu.SemaphoreType.DMA((requests,)),
        ],
        compiler_params=pltpu.CompilerParams(vmem_limit_bytes=MOST),
        cost_estimate=BRIEF,
        name="fill_pages",
    )(place, bounds, request_prompt, page_table, *arrived)


def body(
    hidden_in,
    segment_ids,
    request_prompt,
    page_table,
    ln_attn,
    w_query,
    w_key,
    w_value,
    q_gain,
    k_gain,
    w_out,
    ln_mlp,
    w_gate,
    w_up,
    w_down,
):
    parts = lax.axis_size("mp")
    groups = lax.axis_size("req")
    rows = hidden_in.shape[0] * parts
    half = rows // 2
    req = lax.axis_index("req")
    mine = lax.axis_index("mp")
    side, core = mine // 2, mine % 2
    to_core = [(i, i ^ 1) for i in range(parts)]
    to_side = [(i, i ^ 2) for i in range(parts)]
    to_pair = [(i, i ^ 1) for i in range(groups)]
    to_next = [(i, (i + 2) % groups) for i in range(groups)]

    def by_core(a):
        return lax.ppermute(a, "mp", to_core)

    def by_core_in_pieces(a):
        return [by_core(piece) for piece in jnp.split(a, 4)]

    def by_side(a):
        return lax.ppermute(a, "mp", to_side)

    def forward(a):
        return lax.ppermute(a, "req", to_next)

    def flipped(a):
        return lax.ppermute(a, "req", to_pair)

    here_x = by_side(hidden_in)
    here_c = by_core_in_pieces(hidden_in)
    steps = groups // 2
    homes = []
    for flip in (0, 1):
        for part in (0, 1):
            for step in range(steps):
                home = ((req ^ flip) - 2 * step) % groups
                homes.append(2 * home + (side ^ part))
    place = jnp.stack([req, side, core] + homes).astype(jnp.int32)
    ln = ln_attn.reshape(1, -1)
    qg, kg = q_gain.reshape(1, -1), k_gain.reshape(1, -1)
    cos, sin = turns(rows)
    tables = (ln, w_key, w_value, kg, cos, sin)
    ka, va, pairs_a, near = keys_of(place, segment_ids, hidden_in, here_c, *tables, False)
    line_a, flips_a = [pairs_a, forward(pairs_a)], [flipped(pairs_a)]
    bounds = segment_bounds(ordered(segment_ids, pairs_a))
    here_x = ordered(here_x, bounds, line_a[1], flips_a[0])
    here_xc = by_core(here_x)
    out_other = by_core(ordered(w_out, here_xc))
    kb, vb, pairs_b, far = keys_of(place, segment_ids, here_x, [here_xc], *tables, True)
    line_b, flips_b = [pairs_b, forward(pairs_b)], [flipped(pairs_b)]
    line_a.append(forward(line_a[1]))
    flips_a.append(flipped(line_a[1]))
    keep, send = attend(
        place, segment_ids, near, far, w_query, qg, cos, sin, ka, va, kb, vb
    )
    send = ordered(send, line_a[2], flips_a[1], line_b[1], flips_b[0])
    got = by_core(send)
    part_b = (dot(keep[half // 2 :], w_out) + dot(got[half // 2 :], out_other)).astype(
        jnp.bfloat16
    )
    back = by_side(part_b)
    keep, got = ordered(keep, part_b), ordered(got, part_b)
    part_a = dot(keep[: half // 2], w_out) + dot(got[: half // 2], out_other)
    line_a.append(forward(line_a[2]))
    line_b.append(forward(line_b[1]))
    flips_a.append(flipped(line_a[2]))
    flips_b.append(flipped(line_b[1]))
    back = ordered(back, part_a, line_a[3], flips_a[2], line_b[2], flips_b[1])
    after = (hidden_in.astype(jnp.float32) + part_a + back.astype(jnp.float32)).astype(
        jnp.bfloat16
    )

    after_x = by_side(after)
    after_c = by_core_in_pieces(after)
    ln2 = ln_mlp.reshape(1, -1)
    line_b.append(forward(line_b[2]))
    flips_a.append(flipped(line_a[3]))
    flips_b.append(flipped(line_b[2]))
    keep_a, send_a = mlp(after, after_c, ln2, w_gate, w_up)
    down_other = by_core(ordered(w_down, send_a))
    after_x = ordered(after_x, keep_a, line_b[3], flips_a[3], flips_b[2])
    after_xc = by_core(after_x)
    flips_b.append(flipped(line_b[3]))
    for step in range(4, steps):
        line_a.append(forward(line_a[step - 1]))
        line_b.append(forward(line_b[step - 1]))
        flips_a.append(flipped(line_a[step]))
        flips_b.append(flipped(line_b[step]))
    keep_b, send_b = mlp(after_x, [after_xc], ln2, w_gate, w_up)
    got_b = by_core(send_b)
    got_a = by_core(send_a)
    down_b = (dot(keep_b, w_down) + dot(got_b, down_other)).astype(jnp.bfloat16)
    back = by_side(down_b)
    got_a = ordered(got_a, down_b)
    down_a = dot(keep_a, w_down) + dot(got_a, down_other)
    arrived = line_a + line_b + flips_a + flips_b
    bounds = ordered(bounds, down_b)
    cache = fill_pages(place, bounds, request_prompt, page_table, arrived, rows)
    result = (after.astype(jnp.float32) + down_a + back.astype(jnp.float32)).astype(jnp.bfloat16)
    return (result, cache)


def solution(mesh):
    return jax.shard_map(
        body,
        mesh=mesh,
        in_specs=(
            P(("req", "mp"), None),
            P(),
            P("req"),
            P("req", None),
            P(),
            P(None, "mp"),
            P(None, "mp"),
            P(None, "mp"),
            P(),
            P(),
            P("mp", None),
            P(),
            P(None, "mp"),
            P(None, "mp"),
            P("mp", None),
        ),
        out_specs=(P(("req", "mp"), None), P("req", None, "mp", None)),
        check_vma=False,
    )
```

time: 152 us -> 119 us (0.78)
  waiting for transfers between devices: 57.7 us -> 40.4 us
  local copies, waits for them, and re-layouts: 23 us -> 7.31 us
  Pallas kernels: 28.8 us -> 35.5 us
  other arithmetic: 4.21 us -> 0.33 us
    ppermute x4, waiting for transfers between devices: 28.6 us -> 5.96 us  [by_side(): return lax.ppermute(a, 'mp', to_side)]
    unnamed x79 -> x61, local copies, waits for them, and re-layouts: 21.9 us -> 2.91 us
    pallas_call x5, Pallas kernels: 18.8 us -> 24.7 us  [the longest x1 10.3 us: attend(): pl.pallas_call(attend_kernel, out_shape=[jax.ShapeDtypeStruct((half, wq.s...]
    ppermute x10 -> x15, waiting for transfers between devices: 1.04 us -> 5.5 us  [by_core(): return lax.ppermute(a, 'mp', to_core)]
    ppermute x14, starting transfers between devices: 15.4 us -> 13.2 us  [the longest x8 8.2 us: flipped(): return lax.ppermute(a, 'req', to_pair)]
    ppermute x10 -> x15, starting transfers between devices: 1.15 us -> 3.12 us  [by_core(): return lax.ppermute(a, 'mp', to_core)]
    convert_element_type x2 -> x1, other arithmetic: 2.04 us -> 0.19 us  [body(): (hidden_in.astype(jnp.float32) + part_a + back.astype(jnp.float32)).astyp...]
    split x0 -> x2, local copies, waits for them, and re-layouts: none -> 1.84 us  [by_core_in_pieces(): return [by_core(piece) for piece in jnp.split(a, 4)]]
  transfers between devices with their start and end apart: 28 -> 33, of which waited for: 15 -> 15; matrix products, arithmetic and copies ran while one was open for 10% -> 13% of each run, Pallas kernels for 19% -> 28%
where the time goes in v3:
time: 119 us; the launch traced here: 118 us
  waiting for transfers between devices  40.4 us (34%)
  Pallas kernels  35.5 us (30%)
  starting transfers between devices  22 us (18%)
  matrix products  11.5 us (10%)
  local copies, waits for them, and re-layouts  7.31 us (6%)
    ppermute x8, waiting for transfers between devices, flipped(): return lax.ppermute(a, 'req', to_pair)  19.5 us
    dot_general x8, matrix products, dot(): return jnp.dot(a, b, preferred_element_type=jnp.float32)  11.5 us
    pallas_call x1, Pallas kernels, fill_pages(): pl.pallas_call(functools.partial(page_kernel, rows, requests, entries, bl...  10.7 us
    pallas_call x1, Pallas kernels, attend(): pl.pallas_call(attend_kernel, out_shape=[jax.ShapeDtypeStruct((half, wq.s...  10.3 us
    pallas_call x2, Pallas kernels, keys_of(): pl.pallas_call(functools.partial(keys_kernel, len(others), swapped), out_...  10.3 us
    ppermute x6, waiting for transfers between devices, forward(): return lax.ppermute(a, 'req', to_next)  9.46 us
    ppermute x8, starting transfers between devices, flipped(): return lax.ppermute(a, 'req', to_pair)  8.2 us
    ppermute x4, waiting for transfers between devices, by_side(): return lax.ppermute(a, 'mp', to_side)  5.96 us
  transfers between devices with their start and end apart: 33, of which 15 were waited for; matrix products, arithmetic and copies ran while one was open for 13% of the time, Pallas kernels for 28%

profile of v3, /device:TPU:0, one launch (start us, length us, event | category | flops | bytes accessed | tf_op | source)
XLA Modules:
  0.0 118.1 jit_solution(38026566473666972)
XLA Ops:
  0.7 3.0 %collective-permute-start.4 = (bf16[128,2048]{1,0:T(8,128)(2,1)}, bf16[128,2048]{1,0:T(8,128)(2,1)S(1)}, u32[]{:S(2)}, u32[]{:S(2)}) collective-permute-start(bf16[128,2048]{1,0:T(8,128)(2,1)} %refs_0_.1), channel_id=1, source_target_pairs={{0,2},{1,3},{2,0},{3,1},{4,6},{5,7},{6,4},{7,5},{8,10},{9,11},{10,... | collective-permute-start | bytes 1572872 | tf_op jit(solution)/shard_map/ppermute | solution.py:438
  3.7 1.8 %fusion.12 = (bf16[32,2048]{1,0:T(8,128)(2,1)}, bf16[32,2048]{1,0:T(8,128)(2,1)S(1)}, bf16[32,2048]{1,0:T(8,128)(2,1)S(1)}, bf16[32,2048]{1,0:T(8,128)(2,1)S(1)}) fusion(bf16[128,2048]{1,0:T(8,128)(2,1)} %refs_0_.1), kind=kLoop, calls=%fused_computation.19 | loop fusion | bytes 1048576 | tf_op jit(solution)/shard_map/split | solution.py:435
  5.5 0.5 collective-permute-start.2
  6.0 0.5 collective-permute-start
  6.5 1.3 %reshape.20.refs_5_.refs_2_ = bf16[1,2048]{1,0:T(2,128)(2,1)} reshape(bf16[2048]{0:T(1024)(128)(2,1)} %param.21) | data formatting | bytes 8192 | tf_op jit(solution)/shard_map/reshape | solution.py:456
  7.8 0.6 stack.79.place.refs_0_
  8.4 0.6 copy-done.24
  9.1 5.2 %keys_of.2 = (bf16[256,256]{1,0:T(8,128)(2,1)}, bf16[256,256]{1,0:T(8,128)(2,1)}, bf16[256,2,256]{2,1,0:T(2,128)(2,1)}, bf16[256,2048]{1,0:T(8,128)(2,1)}) custom-call(s32[19]{0:T(128)} %stack.79.place.refs_0_, s32[8,512]{1,0:T(8,128)} %ids.5, bf16[128,2048]{1,0:T(8,128)(2,1)} %refs_0_.1, bf16[32,2048]{1,0:T(8,128)(2,1)} %copy-done.27, ...), custom_call_target="tpu_custom_call" | custom-call | flops 1 | bytes 1 | tf_op jit(solution)/shard_map/keys_of/pallas_call | solution.py:146
  14.3 1.6 %collective-permute-start.6 = (bf16[256,2,256]{2,1,0:T(2,128)(2,1)}, bf16[256,2,256]{2,1,0:T(2,128)(2,1)S(1)}, u32[]{:S(2)}, u32[]{:S(2)}) collective-permute-start(bf16[256,2,256]{2,1,0:T(2,128)(2,1)} %get-tuple-element.28.refs_4_), channel_id=1, source_target_pairs={{0,4},{4,0},{8,12},{12,8},{16,20},{20,16},{24,28},{28,24},{1,5},{5... | collective-permute-start | bytes 786440 | tf_op jit(solution)/shard_map/ppermute | solution.py:444
  15.9 1.6 %collective-permute-start.5 = (bf16[256,2,256]{2,1,0:T(2,128)(2,1)}, bf16[256,2,256]{2,1,0:T(2,128)(2,1)S(1)}, u32[]{:S(2)}, u32[]{:S(2)}) collective-permute-start(bf16[256,2,256]{2,1,0:T(2,128)(2,1)} %get-tuple-element.28.refs_4_), channel_id=1, source_target_pairs={{0,8},{4,12},{8,16},{12,20},{16,24},{20,28},{24,0},{28,4},{1,9},{5... | collective-permute-start | bytes 786440 | tf_op jit(solution)/shard_map/ppermute | solution.py:441
  17.5 0.1 convert_reduce_fusion
  17.7 0.6 reshape.22.refs_1_
  18.3 4.5 %collective-permute-done.6.refs_12_ = bf16[256,2,256]{2,1,0:T(2,128)(2,1)S(1)} collective-permute-done((bf16[256,2,256]{2,1,0:T(2,128)(2,1)}, bf16[256,2,256]{2,1,0:T(2,128)(2,1)S(1)}, u32[]{:S(2)}, u32[]{:S(2)}) %collective-permute-start.6) | collective-permute-done | bytes 262176 | tf_op jit(solution)/shard_map/ppermute | solution.py:444
  22.8 3.1 %collective-permute-done.5.refs_5_ = bf16[256,2,256]{2,1,0:T(2,128)(2,1)S(1)} collective-permute-done((bf16[256,2,256]{2,1,0:T(2,128)(2,1)}, bf16[256,2,256]{2,1,0:T(2,128)(2,1)S(1)}, u32[]{:S(2)}, u32[]{:S(2)}) %collective-permute-start.5) | collective-permute-done | bytes 262176 | tf_op jit(solution)/shard_map/ppermute | solution.py:441
  26.0 1.9 %collective-permute-done.7.refs_1_ = bf16[128,2048]{1,0:T(8,128)(2,1)S(1)} collective-permute-done((bf16[128,2048]{1,0:T(8,128)(2,1)S(1)}, bf16[128,2048]{1,0:T(8,128)(2,1)S(1)}, u32[]{:S(2)}, u32[]{:S(2)}) %collective-permute-start.7) | collective-permute-done | bytes 524320 | tf_op jit(solution)/shard_map/ppermute | solution.py:432
  27.9 0.1 collective-permute-start.13
  28.1 0.5 collective-permute-start.9
  28.6 0.1 copy-done.8
  28.7 5.1 %keys_of.3 = (bf16[256,256]{1,0:T(8,128)(2,1)}, bf16[256,256]{1,0:T(8,128)(2,1)}, bf16[256,2,256]{2,1,0:T(2,128)(2,1)}, bf16[256,2048]{1,0:T(8,128)(2,1)}) custom-call(s32[19]{0:T(128)} %stack.79.place.refs_0_, s32[8,512]{1,0:T(8,128)} %ids.5, bf16[128,2048]{1,0:T(8,128)(2,1)} %copy-done.7, bf16[128,2048]{1,0:T(8,128)(2,1)} %copy-done.8, ...), custom_call_target="tpu_custom_call" | custom-call | flops 1 | bytes 1 | tf_op jit(solution)/shard_map/keys_of/pallas_call | solution.py:146
  33.9 1.4 %collective-permute-start.11 = (bf16[256,2,256]{2,1,0:T(2,128)(2,1)}, bf16[256,2,256]{2,1,0:T(2,128)(2,1)S(1)}, u32[]{:S(2)}, u32[]{:S(2)}) collective-permute-start(bf16[256,2,256]{2,1,0:T(2,128)(2,1)} %get-tuple-element.38.refs_8_), channel_id=1, source_target_pairs={{0,4},{4,0},{8,12},{12,8},{16,20},{20,16},{24,28},{28,24},{1,5},{5... | collective-permute-start | bytes 786440 | tf_op jit(solution)/shard_map/ppermute | solution.py:444
  35.3 1.3 %collective-permute-start.10 = (bf16[256,2,256]{2,1,0:T(2,128)(2,1)}, bf16[256,2,256]{2,1,0:T(2,128)(2,1)S(1)}, u32[]{:S(2)}, u32[]{:S(2)}) collective-permute-start(bf16[256,2,256]{2,1,0:T(2,128)(2,1)} %get-tuple-element.38.refs_8_), channel_id=1, source_target_pairs={{0,8},{4,12},{8,16},{12,20},{16,24},{20,28},{24,0},{28,4},{1,9},{5... | collective-permute-start | bytes 786440 | tf_op jit(solution)/shard_map/ppermute | solution.py:441
  36.6 1.9 %collective-permute-done.8.refs_6_ = bf16[256,2,256]{2,1,0:T(2,128)(2,1)S(1)} collective-permute-done((bf16[256,2,256]{2,1,0:T(2,128)(2,1)S(1)}, bf16[256,2,256]{2,1,0:T(2,128)(2,1)S(1)}, u32[]{:S(2)}, u32[]{:S(2)}) %collective-permute-start.8) | collective-permute-done | bytes 262176 | tf_op jit(solution)/shard_map/ppermute | solution.py:441
  38.4 0.5 collective-permute-start.16
  39.0 10.3 %attend.1 = (bf16[256,512]{1,0:T(8,128)(2,1)}, bf16[256,512]{1,0:T(8,128)(2,1)}) custom-call(s32[19]{0:T(128)} %stack.79.place.refs_0_, s32[8,512]{1,0:T(8,128)} %ids.5, bf16[256,2048]{1,0:T(8,128)(2,1)} %get-tuple-element.27.near_far, bf16[256,2048]{1,0:T(8,128)(2,1)} %get-tuple-element.31.far_far, bf16[2048,512]{1,0:T(8,128)(2,1)} %wq_far.1, ...), custom_call_target="tpu_custom_call" | custom-call | flops 1 | bytes 1 | tf_op jit(solution)/shard_map/attend/pallas_call | solution.py:245
  49.5 1.4 %fusion.9 = f32[128,2048]{1,0:T(8,128)S(1)} fusion(bf16[512,2048]{1,0:T(8,128)(2,1)S(1)} %copy-done.5, bf16[256,512]{1,0:T(8,128)(2,1)} %get-tuple-element.41), kind=kOutput, calls=%fused_computation.14 | convolution fusion | flops 268435456 | bytes 3276800 | tf_op jit(solution)/shard_map/dot_general | solution.py:26
  51.0 1.6 %collective-permute-start.18 = (bf16[256,2,256]{2,1,0:T(2,128)(2,1)S(1)}, bf16[256,2,256]{2,1,0:T(2,128)(2,1)S(1)}, u32[]{:S(2)}, u32[]{:S(2)}) collective-permute-start(bf16[256,2,256]{2,1,0:T(2,128)(2,1)S(1)} %collective-permute-done.10.refs_9_), channel_id=1, source_target_pairs={{0,4},{4,0},{8,12},{12,8},{16,20},{20,16},{24,28},{28,24},{1,5},{5... | collective-permute-start | bytes 786440 | tf_op jit(solution)/shard_map/ppermute | solution.py:444
  52.5 1.8 %collective-permute-start.17 = (bf16[256,2,256]{2,1,0:T(2,128)(2,1)S(1)}, bf16[256,2,256]{2,1,0:T(2,128)(2,1)S(1)}, u32[]{:S(2)}, u32[]{:S(2)}) collective-permute-start(bf16[256,2,256]{2,1,0:T(2,128)(2,1)S(1)} %collective-permute-done.10.refs_9_), channel_id=1, source_target_pairs={{0,8},{4,12},{8,16},{12,20},{16,24},{20,28},{24,0},{28,4},{1,9},{5... | collective-permute-start | bytes 786440 | tf_op jit(solution)/shard_map/ppermute | solution.py:441
  54.3 2.0 %fusion.2 = bf16[128,2048]{1,0:T(8,128)(2,1)S(1)} fusion(f32[128,2048]{1,0:T(8,128)S(1)} %fusion.9, bf16[512,2048]{1,0:T(8,128)(2,1)} %collective-permute-done.13, bf16[256,512]{1,0:T(8,128)(2,1)S(1)} %collective-permute-done.12), kind=kOutput, calls=%fused_computation.6 | convolution fusion | flops 268959744 | bytes 3801088 | tf_op jit(solution)/shard_map/dot_general | solution.py:26
  56.4 0.6 collective-permute-start.14
  57.1 0.4 fusion.7
  57.6 2.2 %convolution_add_fusion.2 = f32[128,2048]{1,0:T(8,128)S(1)} fusion(f32[128,2048]{1,0:T(8,128)S(1)} %fusion.7, bf16[512,2048]{1,0:T(8,128)(2,1)} %collective-permute-done.13, bf16[256,512]{1,0:T(8,128)(2,1)S(1)} %collective-permute-done.12), kind=kOutput, calls=%fused_computation.4 | convolution fusion | flops 268697600 | bytes 4325376 | tf_op jit(solution)/shard_map/dot_general | solution.py:26
  59.8 4.4 %collective-permute-done.17.refs_10_ = bf16[256,2,256]{2,1,0:T(2,128)(2,1)S(1)} collective-permute-done((bf16[256,2,256]{2,1,0:T(2,128)(2,1)S(1)}, bf16[256,2,256]{2,1,0:T(2,128)(2,1)S(1)}, u32[]{:S(2)}, u32[]{:S(2)}) %collective-permute-start.17) | collective-permute-done | bytes 262176 | tf_op jit(solution)/shard_map/ppermute | solution.py:441
  64.2 6.0 %collective-permute-done.14 = bf16[128,2048]{1,0:T(8,128)(2,1)S(1)} collective-permute-done((bf16[128,2048]{1,0:T(8,128)(2,1)S(1)}, bf16[128,2048]{1,0:T(8,128)(2,1)S(1)}, u32[]{:S(2)}, u32[]{:S(2)}) %collective-permute-start.14) | collective-permute-done | bytes 524320 | tf_op jit(solution)/shard_map/ppermute | solution.py:438
  70.2 0.2 add_convert_fusion.refs_0_
  70.5 0.5 collective-permute-start.21
  71.1 0.4 collective-permute-start.19
  71.6 0.3 collective-permute-done.22.refs_4_
  71.9 0.2 collective-permute-done.21.refs_3_
  72.0 0.3 collective-permute-done.20.refs_2_
  72.4 0.2 collective-permute-done.19.refs_1_
  72.6 2.0 %gate_up.2 = (bf16[128,768]{1,0:T(8,128)(2,1)S(1)}, bf16[128,768]{1,0:T(8,128)(2,1)S(1)}) custom-call(bf16[128,2048]{1,0:T(8,128)(2,1)S(1)} %add_convert_fusion.refs_0_, bf16[32,2048]{1,0:T(8,128)(2,1)S(1)} %collective-permute-done.19.refs_1_, bf16[32,2048]{1,0:T(8,128)(2,1)S(1)} %collective-permute-done.20.refs_2_, ...), custom_call_target="tpu_custom_call" | custom-call | flops 1 | bytes 1 | tf_op jit(solution)/shard_map/gate_up/pallas_call | solution.py:290
  74.6 0.4 collective-permute-start.30
  75.0 0.6 collective-permute-start.24
  75.6 0.5 collective-permute-start.26
  76.1 1.5 %collective-permute-start.27 = (bf16[256,2,256]{2,1,0:T(2,128)(2,1)S(1)}, bf16[256,2,256]{2,1,0:T(2,128)(2,1)S(1)}, u32[]{:S(2)}, u32[]{:S(2)}) collective-permute-start(bf16[256,2,256]{2,1,0:T(2,128)(2,1)S(1)} %collective-permute-done.17.refs_10_), channel_id=1, source_target_pairs={{0,4},{4,0},{8,12},{12,8},{16,20},{20,16},{24,28},{28,24},{1,5},{5... | collective-permute-start | bytes 786440 | tf_op jit(solution)/shard_map/ppermute | solution.py:444
  77.6 0.3 collective-permute-start.25
  77.9 6.9 %collective-permute-done.26.refs_15_ = bf16[256,2,256]{2,1,0:T(2,128)(2,1)S(1)} collective-permute-done((bf16[256,2,256]{2,1,0:T(2,128)(2,1)S(1)}, bf16[256,2,256]{2,1,0:T(2,128)(2,1)S(1)}, u32[]{:S(2)}, u32[]{:S(2)}) %collective-permute-start.26) | collective-permute-done | bytes 262176 | tf_op jit(solution)/shard_map/ppermute | solution.py:444
  84.8 4.6 %collective-permute-done.27.refs_18_ = bf16[256,2,256]{2,1,0:T(2,128)(2,1)S(1)} collective-permute-done((bf16[256,2,256]{2,1,0:T(2,128)(2,1)S(1)}, bf16[256,2,256]{2,1,0:T(2,128)(2,1)S(1)}, u32[]{:S(2)}, u32[]{:S(2)}) %collective-permute-start.27) | collective-permute-done | bytes 262176 | tf_op jit(solution)/shard_map/ppermute | solution.py:444
  89.4 1.9 %collective-permute-done.28.refs_1_ = bf16[128,2048]{1,0:T(8,128)(2,1)S(1)} collective-permute-done((bf16[128,2048]{1,0:T(8,128)(2,1)S(1)}, bf16[128,2048]{1,0:T(8,128)(2,1)S(1)}, u32[]{:S(2)}, u32[]{:S(2)}) %collective-permute-start.28) | collective-permute-done | bytes 524320 | tf_op jit(solution)/shard_map/ppermute | solution.py:432
  91.3 2.0 %gate_up.3 = (bf16[128,768]{1,0:T(8,128)(2,1)S(1)}, bf16[128,768]{1,0:T(8,128)(2,1)S(1)}) custom-call(bf16[128,2048]{1,0:T(8,128)(2,1)S(1)} %collective-permute-done.24.refs_0_, bf16[128,2048]{1,0:T(8,128)(2,1)S(1)} %collective-permute-done.28.refs_1_, bf16[1,2048]{1,0:T(2,128)(2,1)S(1)} %reshape.24.refs_5_.refs_2_, bf16[2048,768]{1,0:T(8,128)(2,1)S(1)} %copy-done, ...), custom_call_target="tpu_custom_call" | custom-call | flops 1 | bytes 1 | tf_op jit(solution)/shard_map/gate_up/pallas_call | solution.py:290
  93.4 0.2 collective-permute-start.29
  93.6 0.5 collective-permute-start.32
  94.2 0.7 collective-permute-done.29
  94.9 0.6 fusion.13
  95.5 0.7 fusion.4
  96.2 0.4 copy-done.4
  96.5 1.4 %collective-permute-start.31 = (bf16[128,2048]{1,0:T(8,128)(2,1)S(1)}, bf16[128,2048]{1,0:T(8,128)(2,1)S(1)}, u32[]{:S(2)}, u32[]{:S(2)}) collective-permute-start(bf16[128,2048]{1,0:T(8,128)(2,1)S(1)} %fusion.4), channel_id=1, source_target_pairs={{0,2},{1,3},{2,0},{3,1},{4,6},{5,7},{6,4},{7,5},{8,10},{9,11},{10,... | collective-permute-start | bytes 1572872 | tf_op jit(solution)/shard_map/ppermute | solution.py:438
  98.0 0.7 copy.22.refs_3_
  98.7 3.5 %collective-permute-done.32.refs_19_ = bf16[256,2,256]{2,1,0:T(2,128)(2,1)S(1)} collective-permute-done((bf16[256,2,256]{2,1,0:T(2,128)(2,1)S(1)}, bf16[256,2,256]{2,1,0:T(2,128)(2,1)S(1)}, u32[]{:S(2)}, u32[]{:S(2)}) %collective-permute-start.32) | collective-permute-done | bytes 262176 | tf_op jit(solution)/shard_map/ppermute | solution.py:444
  102.2 0.7 copy-done.23
  102.9 10.7 %fill_pages.1 = bf16[512,16,2,256]{3,2,1,0:T(2,128)(2,1)} custom-call(s32[19]{0:T(128)} %stack.79.place.refs_0_, s32[32]{0:T(128)} %reshape.22.refs_1_, s32[32]{0:T(128)} %refs_2_.1, s32[32,16]{1,0:T(8,128)} %copy.22.refs_3_, bf16[256,2,256]{2,1,0:T(2,128)(2,1)} %get-tuple-element.28.refs_4_, bf16[256,2,256]{2,1,0:T(2,128)(2,1)} %copy-done.11, ...), custom_call_target="tpu_custom_call" | custom-call | flops 1 | bytes 1 | tf_op jit(solution)/shard_map/fill_pages/pallas_call | solution.py:385
  113.7 2.6 %fusion.14 = f32[128,2048]{1,0:T(8,128)S(1)} fusion(bf16[128,768]{1,0:T(8,128)(2,1)S(1)} %collective-permute-done.23, bf16[768,2048]{1,0:T(8,128)(2,1)} %copy-done.4), kind=kOutput, calls=%fused_computation.21 | convolution fusion | flops 402653184 | bytes 4390912 | tf_op jit(solution)/shard_map/dot_general | solution.py:26
  116.3 0.2 copy-done.3
  116.5 1.6 %fusion.3 = bf16[128,2048]{1,0:T(8,128)(2,1)} fusion(f32[128,2048]{1,0:T(8,128)S(1)} %fusion.14, bf16[128,768]{1,0:T(8,128)(2,1)S(1)} %get-tuple-element.44, bf16[768,2048]{1,0:T(8,128)(2,1)S(1)} %copy-done.3, bf16[128,2048]{1,0:T(8,128)(2,1)S(1)} %collective-permute-done.31, bf16[128,2048]{1,0:T(8,128)(2,1)S(1)} %add_convert_fusion.refs_0_), kind=kOutput, calls=%fused_computation.7 | convolution fusion | flops 404226048 | bytes 5963776 | tf_op jit(solution)/shard_map/dot_general | solution.py:26
  (86 shorter events, 1.0 us)
Async XLA Ops:
  0.6 16.9 %copy-start.9 = (s32[8,512]{1,0:T(8,128)S(1)}, s32[8,512]{1,0:T(8,128)}, u32[]{:S(2)}) copy-start(s32[8,512]{1,0:T(8,128)} %ids.5) | copy-start | bytes 49156
  0.6 27.3 %copy-start.5 = (bf16[512,2048]{1,0:T(8,128)(2,1)S(1)}, bf16[512,2048]{1,0:T(8,128)(2,1)}, u32[]{:S(2)}) copy-start(bf16[512,2048]{1,0:T(8,128)(2,1)} %param.27) | copy-start | bytes 6291460
  0.7 25.3 %collective-permute-start.4 = (bf16[128,2048]{1,0:T(8,128)(2,1)}, bf16[128,2048]{1,0:T(8,128)(2,1)S(1)}, u32[]{:S(2)}, u32[]{:S(2)}) collective-permute-start(bf16[128,2048]{1,0:T(8,128)(2,1)} %refs_0_.1), channel_id=1, source_target_pairs={{0,2},{1,3},{2,0},{3,1},{4,6},{5,7},{6,4},{7,5},{8,10},{9,11},{10,... | collective-permute-start | bytes 1572872 | tf_op jit(solution)/shard_map/ppermute | solution.py:438
  5.5 2.9 %collective-permute-start.3 = (bf16[32,2048]{1,0:T(8,128)(2,1)}, bf16[32,2048]{1,0:T(8,128)(2,1)S(1)}, u32[]{:S(2)}, u32[]{:S(2)}) collective-permute-start(bf16[32,2048]{1,0:T(8,128)(2,1)} %get-tuple-element.56), channel_id=1, source_target_pairs={{0,1},{1,0},{2,3},{3,2},{4,5},{5,4},{6,7},{7,6},{8,9},{9,8},{10,11... | collective-permute-start | bytes 393224 | tf_op jit(solution)/shard_map/ppermute | solution.py:432
  5.5 2.9 %collective-permute-start.2 = (bf16[32,2048]{1,0:T(8,128)(2,1)S(1)}, bf16[32,2048]{1,0:T(8,128)(2,1)S(1)}, u32[]{:S(2)}, u32[]{:S(2)}) collective-permute-start(bf16[32,2048]{1,0:T(8,128)(2,1)S(1)} %get-tuple-element.57), channel_id=1, source_target_pairs={{0,1},{1,0},{2,3},{3,2},{4,5},{5,4},{6,7},{7,6},{8,9},{9,8},{10,11... | collective-permute-start | bytes 393224 | tf_op jit(solution)/shard_map/ppermute | solution.py:432
  6.0 2.4 %collective-permute-start.1 = (bf16[32,2048]{1,0:T(8,128)(2,1)S(1)}, bf16[32,2048]{1,0:T(8,128)(2,1)S(1)}, u32[]{:S(2)}, u32[]{:S(2)}) collective-permute-start(bf16[32,2048]{1,0:T(8,128)(2,1)S(1)} %get-tuple-element.58), channel_id=1, source_target_pairs={{0,1},{1,0},{2,3},{3,2},{4,5},{5,4},{6,7},{7,6},{8,9},{9,8},{10,11... | collective-permute-start | bytes 393224 | tf_op jit(solution)/shard_map/ppermute | solution.py:432
  6.0 2.4 %collective-permute-start = (bf16[32,2048]{1,0:T(8,128)(2,1)S(1)}, bf16[32,2048]{1,0:T(8,128)(2,1)S(1)}, u32[]{:S(2)}, u32[]{:S(2)}) collective-permute-start(bf16[32,2048]{1,0:T(8,128)(2,1)S(1)} %get-tuple-element.59), channel_id=1, source_target_pairs={{0,1},{1,0},{2,3},{3,2},{4,5},{5,4},{6,7},{7,6},{8,9},{9,8},{10,11... | collective-permute-start | bytes 393224 | tf_op jit(solution)/shard_map/ppermute | solution.py:432
  8.3 0.6 copy-start.24
  8.4 0.7 copy-start.25
  8.4 0.7 copy-start.26
  8.4 0.7 copy-start.27
  14.3 8.5 %collective-permute-start.6 = (bf16[256,2,256]{2,1,0:T(2,128)(2,1)}, bf16[256,2,256]{2,1,0:T(2,128)(2,1)S(1)}, u32[]{:S(2)}, u32[]{:S(2)}) collective-permute-start(bf16[256,2,256]{2,1,0:T(2,128)(2,1)} %get-tuple-element.28.refs_4_), channel_id=1, source_target_pairs={{0,4},{4,0},{8,12},{12,8},{16,20},{20,16},{24,28},{28,24},{1,5},{5... | collective-permute-start | bytes 786440 | tf_op jit(solution)/shard_map/ppermute | solution.py:444
  15.9 10.0 %collective-permute-start.5 = (bf16[256,2,256]{2,1,0:T(2,128)(2,1)}, bf16[256,2,256]{2,1,0:T(2,128)(2,1)S(1)}, u32[]{:S(2)}, u32[]{:S(2)}) collective-permute-start(bf16[256,2,256]{2,1,0:T(2,128)(2,1)} %get-tuple-element.28.refs_4_), channel_id=1, source_target_pairs={{0,8},{4,12},{8,16},{12,20},{16,24},{20,28},{24,0},{28,4},{1,9},{5... | collective-permute-start | bytes 786440 | tf_op jit(solution)/shard_map/ppermute | solution.py:441
  22.8 34.7 %copy-start.10 = (bf16[256,2,256]{2,1,0:T(2,128)(2,1)}, bf16[256,2,256]{2,1,0:T(2,128)(2,1)S(1)}, u32[]{:S(2)}) copy-start(bf16[256,2,256]{2,1,0:T(2,128)(2,1)S(1)} %collective-permute-done.6.refs_12_) | copy-start | bytes 786436
  25.9 31.6 %copy-start.11 = (bf16[256,2,256]{2,1,0:T(2,128)(2,1)}, bf16[256,2,256]{2,1,0:T(2,128)(2,1)S(1)}, u32[]{:S(2)}) copy-start(bf16[256,2,256]{2,1,0:T(2,128)(2,1)S(1)} %collective-permute-done.5.refs_5_) | copy-start | bytes 786436
  25.9 2.6 %copy-start.7 = (bf16[128,2048]{1,0:T(8,128)(2,1)}, bf16[128,2048]{1,0:T(8,128)(2,1)S(1)}, u32[]{:S(2)}) copy-start(bf16[128,2048]{1,0:T(8,128)(2,1)S(1)} %collective-permute-done.4.refs_0_) | copy-start | bytes 1572868
  26.0 2.0 %collective-permute-start.7 = (bf16[128,2048]{1,0:T(8,128)(2,1)S(1)}, bf16[128,2048]{1,0:T(8,128)(2,1)S(1)}, u32[]{:S(2)}, u32[]{:S(2)}) collective-permute-start(bf16[128,2048]{1,0:T(8,128)(2,1)S(1)} %collective-permute-done.4.refs_0_), channel_id=1, source_target_pairs={{0,1},{1,0},{2,3},{3,2},{4,5},{5,4},{6,7},{7,6},{8,9},{9,8},{10,11... | collective-permute-start | bytes 1572872 | tf_op jit(solution)/shard_map/ppermute | solution.py:432
  27.9 0.8 copy-start.8
  27.9 26.4 %collective-permute-start.13 = (bf16[512,2048]{1,0:T(8,128)(2,1)S(1)}, bf16[512,2048]{1,0:T(8,128)(2,1)}, u32[]{:S(2)}, u32[]{:S(2)}) collective-permute-start(bf16[512,2048]{1,0:T(8,128)(2,1)S(1)} %copy-done.5), channel_id=1, source_target_pairs={{0,1},{1,0},{2,3},{3,2},{4,5},{5,4},{6,7},{7,6},{8,9},{9,8},{10,11... | collective-permute-start | bytes 6291464 | tf_op jit(solution)/shard_map/ppermute | solution.py:432
  28.1 10.4 %collective-permute-start.8 = (bf16[256,2,256]{2,1,0:T(2,128)(2,1)S(1)}, bf16[256,2,256]{2,1,0:T(2,128)(2,1)S(1)}, u32[]{:S(2)}, u32[]{:S(2)}) collective-permute-start(bf16[256,2,256]{2,1,0:T(2,128)(2,1)S(1)} %collective-permute-done.5.refs_5_), channel_id=1, source_target_pairs={{0,8},{4,12},{8,16},{12,20},{16,24},{20,28},{24,0},{28,4},{1,9},{5... | collective-permute-start | bytes 786440 | tf_op jit(solution)/shard_map/ppermute | solution.py:441
  28.1 21.2 %collective-permute-start.9 = (bf16[256,2,256]{2,1,0:T(2,128)(2,1)S(1)}, bf16[256,2,256]{2,1,0:T(2,128)(2,1)}, u32[]{:S(2)}, u32[]{:S(2)}) collective-permute-start(bf16[256,2,256]{2,1,0:T(2,128)(2,1)S(1)} %collective-permute-done.5.refs_5_), channel_id=1, source_target_pairs={{0,4},{4,0},{8,12},{12,8},{16,20},{20,16},{24,28},{28,24},{1,5},{5... | collective-permute-start | bytes 786440 | tf_op jit(solution)/shard_map/ppermute | solution.py:444
  33.9 15.5 %collective-permute-start.11 = (bf16[256,2,256]{2,1,0:T(2,128)(2,1)}, bf16[256,2,256]{2,1,0:T(2,128)(2,1)S(1)}, u32[]{:S(2)}, u32[]{:S(2)}) collective-permute-start(bf16[256,2,256]{2,1,0:T(2,128)(2,1)} %get-tuple-element.38.refs_8_), channel_id=1, source_target_pairs={{0,4},{4,0},{8,12},{12,8},{16,20},{20,16},{24,28},{28,24},{1,5},{5... | collective-permute-start | bytes 786440 | tf_op jit(solution)/shard_map/ppermute | solution.py:444
  35.3 14.1 %collective-permute-start.10 = (bf16[256,2,256]{2,1,0:T(2,128)(2,1)}, bf16[256,2,256]{2,1,0:T(2,128)(2,1)S(1)}, u32[]{:S(2)}, u32[]{:S(2)}) collective-permute-start(bf16[256,2,256]{2,1,0:T(2,128)(2,1)} %get-tuple-element.38.refs_8_), channel_id=1, source_target_pairs={{0,8},{4,12},{8,16},{12,20},{16,24},{20,28},{24,0},{28,4},{1,9},{5... | collective-permute-start | bytes 786440 | tf_op jit(solution)/shard_map/ppermute | solution.py:441
  38.4 12.5 %copy-start.12 = (bf16[256,2,256]{2,1,0:T(2,128)(2,1)}, bf16[256,2,256]{2,1,0:T(2,128)(2,1)S(1)}, u32[]{:S(2)}) copy-start(bf16[256,2,256]{2,1,0:T(2,128)(2,1)S(1)} %collective-permute-done.8.refs_6_) | copy-start | bytes 786436
  38.4 21.3 %collective-permute-start.16 = (bf16[256,2,256]{2,1,0:T(2,128)(2,1)S(1)}, bf16[256,2,256]{2,1,0:T(2,128)(2,1)S(1)}, u32[]{:S(2)}, u32[]{:S(2)}) collective-permute-start(bf16[256,2,256]{2,1,0:T(2,128)(2,1)S(1)} %collective-permute-done.8.refs_6_), channel_id=1, source_target_pairs={{0,4},{4,0},{8,12},{12,8},{16,20},{20,16},{24,28},{28,24},{1,5},{5... | collective-permute-start | bytes 786440 | tf_op jit(solution)/shard_map/ppermute | solution.py:444
  49.3 10.5 %collective-permute-start.15 = (bf16[256,2,256]{2,1,0:T(2,128)(2,1)S(1)}, bf16[256,2,256]{2,1,0:T(2,128)(2,1)S(1)}, u32[]{:S(2)}, u32[]{:S(2)}) collective-permute-start(bf16[256,2,256]{2,1,0:T(2,128)(2,1)S(1)} %collective-permute-done.8.refs_6_), channel_id=1, source_target_pairs={{0,8},{4,12},{8,16},{12,20},{16,24},{20,28},{24,0},{28,4},{1,9},{5... | collective-permute-start | bytes 786440 | tf_op jit(solution)/shard_map/ppermute | solution.py:441
  49.4 7.0 %copy-start.13 = (bf16[256,2,256]{2,1,0:T(2,128)(2,1)}, bf16[256,2,256]{2,1,0:T(2,128)(2,1)S(1)}, u32[]{:S(2)}) copy-start(bf16[256,2,256]{2,1,0:T(2,128)(2,1)S(1)} %collective-permute-done.11.refs_16_) | copy-start | bytes 786436
  49.4 7.0 %copy-start.14 = (bf16[256,2,256]{2,1,0:T(2,128)(2,1)}, bf16[256,2,256]{2,1,0:T(2,128)(2,1)S(1)}, u32[]{:S(2)}) copy-start(bf16[256,2,256]{2,1,0:T(2,128)(2,1)S(1)} %collective-permute-done.10.refs_9_) | copy-start | bytes 786436
  49.4 3.1 %collective-permute-start.12 = (bf16[256,512]{1,0:T(8,128)(2,1)}, bf16[256,512]{1,0:T(8,128)(2,1)S(1)}, u32[]{:S(2)}, u32[]{:S(2)}) collective-permute-start(bf16[256,512]{1,0:T(8,128)(2,1)} %get-tuple-element.39), channel_id=1, source_target_pairs={{0,1},{1,0},{2,3},{3,2},{4,5},{5,4},{6,7},{7,6},{8,9},{9,8},{10,11... | collective-permute-start | bytes 786440 | tf_op jit(solution)/shard_map/ppermute | solution.py:432
  49.5 7.6 %copy-start.22 = (bf16[256,512]{1,0:T(8,128)(2,1)S(1)}, bf16[256,512]{1,0:T(8,128)(2,1)}, u32[]{:S(2)}) copy-start(bf16[256,512]{1,0:T(8,128)(2,1)} %get-tuple-element.41) | copy-start | bytes 786436
  51.0 8.9 %collective-permute-start.18 = (bf16[256,2,256]{2,1,0:T(2,128)(2,1)S(1)}, bf16[256,2,256]{2,1,0:T(2,128)(2,1)S(1)}, u32[]{:S(2)}, u32[]{:S(2)}) collective-permute-start(bf16[256,2,256]{2,1,0:T(2,128)(2,1)S(1)} %collective-permute-done.10.refs_9_), channel_id=1, source_target_pairs={{0,4},{4,0},{8,12},{12,8},{16,20},{20,16},{24,28},{28,24},{1,5},{5... | collective-permute-start | bytes 786440 | tf_op jit(solution)/shard_map/ppermute | solution.py:444
  52.5 11.7 %collective-permute-start.17 = (bf16[256,2,256]{2,1,0:T(2,128)(2,1)S(1)}, bf16[256,2,256]{2,1,0:T(2,128)(2,1)S(1)}, u32[]{:S(2)}, u32[]{:S(2)}) collective-permute-start(bf16[256,2,256]{2,1,0:T(2,128)(2,1)S(1)} %collective-permute-done.10.refs_9_), channel_id=1, source_target_pairs={{0,8},{4,12},{8,16},{12,20},{16,24},{20,28},{24,0},{28,4},{1,9},{5... | collective-permute-start | bytes 786440 | tf_op jit(solution)/shard_map/ppermute | solution.py:441
  56.4 13.8 %copy-start.6 = (bf16[128,2048]{1,0:T(8,128)(2,1)S(1)}, bf16[128,2048]{1,0:T(8,128)(2,1)}, u32[]{:S(2)}) copy-start(bf16[128,2048]{1,0:T(8,128)(2,1)} %refs_0_.1) | copy-start | bytes 1572868
  56.4 13.8 %collective-permute-start.14 = (bf16[128,2048]{1,0:T(8,128)(2,1)S(1)}, bf16[128,2048]{1,0:T(8,128)(2,1)S(1)}, u32[]{:S(2)}, u32[]{:S(2)}) collective-permute-start(bf16[128,2048]{1,0:T(8,128)(2,1)S(1)} %fusion.2), channel_id=1, source_target_pairs={{0,2},{1,3},{2,0},{3,1},{4,6},{5,7},{6,4},{7,5},{8,10},{9,11},{10,... | collective-permute-start | bytes 1572872 | tf_op jit(solution)/shard_map/ppermute | solution.py:438
  57.5 14.0 %copy-start.29 = (bf16[2048]{0:T(1024)(128)(2,1)S(1)}, bf16[2048]{0:T(1024)(128)(2,1)}, u32[]{:S(2)}) copy-start(bf16[2048]{0:T(1024)(128)(2,1)} %param.28) | copy-start | bytes 12292
  57.5 15.0 %copy-start = (bf16[2048,768]{1,0:T(8,128)(2,1)S(1)}, bf16[2048,768]{1,0:T(8,128)(2,1)}, u32[]{:S(2)}) copy-start(bf16[2048,768]{1,0:T(8,128)(2,1)} %refs_3_.4) | copy-start | bytes 9437188
  57.5 15.0 %copy-start.1 = (bf16[2048,768]{1,0:T(8,128)(2,1)S(1)}, bf16[2048,768]{1,0:T(8,128)(2,1)}, u32[]{:S(2)}) copy-start(bf16[2048,768]{1,0:T(8,128)(2,1)} %refs_4_.3) | copy-start | bytes 9437188
  59.8 14.8 %copy-start.15 = (bf16[256,2,256]{2,1,0:T(2,128)(2,1)}, bf16[256,2,256]{2,1,0:T(2,128)(2,1)S(1)}, u32[]{:S(2)}) copy-start(bf16[256,2,256]{2,1,0:T(2,128)(2,1)S(1)} %collective-permute-done.16.refs_14_) | copy-start | bytes 786436
  59.8 15.8 %copy-start.16 = (bf16[256,2,256]{2,1,0:T(2,128)(2,1)}, bf16[256,2,256]{2,1,0:T(2,128)(2,1)S(1)}, u32[]{:S(2)}) copy-start(bf16[256,2,256]{2,1,0:T(2,128)(2,1)S(1)} %collective-permute-done.15.refs_7_) | copy-start | bytes 786436
  59.8 12.5 %copy-start.17 = (bf16[256,2,256]{2,1,0:T(2,128)(2,1)}, bf16[256,2,256]{2,1,0:T(2,128)(2,1)S(1)}, u32[]{:S(2)}) copy-start(bf16[256,2,256]{2,1,0:T(2,128)(2,1)S(1)} %collective-permute-done.18.refs_17_) | copy-start | bytes 786436
  64.2 13.4 %copy-start.18 = (bf16[256,2,256]{2,1,0:T(2,128)(2,1)}, bf16[256,2,256]{2,1,0:T(2,128)(2,1)S(1)}, u32[]{:S(2)}) copy-start(bf16[256,2,256]{2,1,0:T(2,128)(2,1)S(1)} %collective-permute-done.17.refs_10_) | copy-start | bytes 786436
  70.4 1.4 %collective-permute-start.22 = (bf16[32,2048]{1,0:T(8,128)(2,1)S(1)}, bf16[32,2048]{1,0:T(8,128)(2,1)S(1)}, u32[]{:S(2)}, u32[]{:S(2)}) collective-permute-start(bf16[32,2048]{1,0:T(8,128)(2,1)S(1)} %get-tuple-element.52), channel_id=1, source_target_pairs={{0,1},{1,0},{2,3},{3,2},{4,5},{5,4},{6,7},{7,6},{8,9},{9,8},{10,11... | collective-permute-start | bytes 393224 | tf_op jit(solution)/shard_map/ppermute | solution.py:432
  70.5 1.5 %collective-permute-start.21 = (bf16[32,2048]{1,0:T(8,128)(2,1)S(1)}, bf16[32,2048]{1,0:T(8,128)(2,1)S(1)}, u32[]{:S(2)}, u32[]{:S(2)}) collective-permute-start(bf16[32,2048]{1,0:T(8,128)(2,1)S(1)} %get-tuple-element.53), channel_id=1, source_target_pairs={{0,1},{1,0},{2,3},{3,2},{4,5},{5,4},{6,7},{7,6},{8,9},{9,8},{10,11... | collective-permute-start | bytes 393224 | tf_op jit(solution)/shard_map/ppermute | solution.py:432
  71.0 1.3 %collective-permute-start.20 = (bf16[32,2048]{1,0:T(8,128)(2,1)S(1)}, bf16[32,2048]{1,0:T(8,128)(2,1)S(1)}, u32[]{:S(2)}, u32[]{:S(2)}) collective-permute-start(bf16[32,2048]{1,0:T(8,128)(2,1)S(1)} %get-tuple-element.54), channel_id=1, source_target_pairs={{0,1},{1,0},{2,3},{3,2},{4,5},{5,4},{6,7},{7,6},{8,9},{9,8},{10,11... | collective-permute-start | bytes 393224 | tf_op jit(solution)/shard_map/ppermute | solution.py:432
  71.1 1.5 %collective-permute-start.19 = (bf16[32,2048]{1,0:T(8,128)(2,1)S(1)}, bf16[32,2048]{1,0:T(8,128)(2,1)S(1)}, u32[]{:S(2)}, u32[]{:S(2)}) collective-permute-start(bf16[32,2048]{1,0:T(8,128)(2,1)S(1)} %get-tuple-element.55), channel_id=1, source_target_pairs={{0,1},{1,0},{2,3},{3,2},{4,5},{5,4},{6,7},{7,6},{8,9},{9,8},{10,11... | collective-permute-start | bytes 393224 | tf_op jit(solution)/shard_map/ppermute | solution.py:432
  71.5 3.1 %copy-start.2 = (bf16[768,2048]{1,0:T(8,128)(2,1)S(1)}, bf16[768,2048]{1,0:T(8,128)(2,1)}, u32[]{:S(2)}) copy-start(bf16[768,2048]{1,0:T(8,128)(2,1)} %param.31) | copy-start | bytes 9437188
  74.6 20.3 %collective-permute-start.30 = (bf16[768,2048]{1,0:T(8,128)(2,1)S(1)}, bf16[768,2048]{1,0:T(8,128)(2,1)S(1)}, u32[]{:S(2)}, u32[]{:S(2)}) collective-permute-start(bf16[768,2048]{1,0:T(8,128)(2,1)S(1)} %copy-done.2), channel_id=1, source_target_pairs={{0,1},{1,0},{2,3},{3,2},{4,5},{5,4},{6,7},{7,6},{8,9},{9,8},{10,11... | collective-permute-start | bytes 9437192 | tf_op jit(solution)/shard_map/ppermute | solution.py:432
  75.0 14.3 %collective-permute-start.24 = (bf16[128,2048]{1,0:T(8,128)(2,1)S(1)}, bf16[128,2048]{1,0:T(8,128)(2,1)S(1)}, u32[]{:S(2)}, u32[]{:S(2)}) collective-permute-start(bf16[128,2048]{1,0:T(8,128)(2,1)S(1)} %add_convert_fusion.refs_0_), channel_id=1, source_target_pairs={{0,2},{1,3},{2,0},{3,1},{4,6},{5,7},{6,4},{7,5},{8,10},{9,11},{10,... | collective-permute-start | bytes 1572872 | tf_op jit(solution)/shard_map/ppermute | solution.py:438
  75.6 9.2 %collective-permute-start.26 = (bf16[256,2,256]{2,1,0:T(2,128)(2,1)S(1)}, bf16[256,2,256]{2,1,0:T(2,128)(2,1)S(1)}, u32[]{:S(2)}, u32[]{:S(2)}) collective-permute-start(bf16[256,2,256]{2,1,0:T(2,128)(2,1)S(1)} %collective-permute-done.15.refs_7_), channel_id=1, source_target_pairs={{0,4},{4,0},{8,12},{12,8},{16,20},{20,16},{24,28},{28,24},{1,5},{5... | collective-permute-start | bytes 786440 | tf_op jit(solution)/shard_map/ppermute | solution.py:444
  76.1 13.2 %collective-permute-start.27 = (bf16[256,2,256]{2,1,0:T(2,128)(2,1)S(1)}, bf16[256,2,256]{2,1,0:T(2,128)(2,1)S(1)}, u32[]{:S(2)}, u32[]{:S(2)}) collective-permute-start(bf16[256,2,256]{2,1,0:T(2,128)(2,1)S(1)} %collective-permute-done.17.refs_10_), channel_id=1, source_target_pairs={{0,4},{4,0},{8,12},{12,8},{16,20},{20,16},{24,28},{28,24},{1,5},{5... | collective-permute-start | bytes 786440 | tf_op jit(solution)/shard_map/ppermute | solution.py:444
  77.6 11.7 %collective-permute-start.25 = (bf16[256,2,256]{2,1,0:T(2,128)(2,1)S(1)}, bf16[256,2,256]{2,1,0:T(2,128)(2,1)S(1)}, u32[]{:S(2)}, u32[]{:S(2)}) collective-permute-start(bf16[256,2,256]{2,1,0:T(2,128)(2,1)S(1)} %collective-permute-done.17.refs_10_), channel_id=1, source_target_pairs={{0,8},{4,12},{8,16},{12,20},{16,24},{20,28},{24,0},{28,4},{1,9},{5... | collective-permute-start | bytes 786440 | tf_op jit(solution)/shard_map/ppermute | solution.py:441
  84.8 8.6 %copy-start.19 = (bf16[256,2,256]{2,1,0:T(2,128)(2,1)}, bf16[256,2,256]{2,1,0:T(2,128)(2,1)S(1)}, u32[]{:S(2)}) copy-start(bf16[256,2,256]{2,1,0:T(2,128)(2,1)S(1)} %collective-permute-done.26.refs_15_) | copy-start | bytes 786436
  89.3 4.1 %copy-start.20 = (bf16[256,2,256]{2,1,0:T(2,128)(2,1)}, bf16[256,2,256]{2,1,0:T(2,128)(2,1)S(1)}, u32[]{:S(2)}) copy-start(bf16[256,2,256]{2,1,0:T(2,128)(2,1)S(1)} %collective-permute-done.27.refs_18_) | copy-start | bytes 786436
  89.3 4.3 %copy-start.21 = (bf16[256,2,256]{2,1,0:T(2,128)(2,1)}, bf16[256,2,256]{2,1,0:T(2,128)(2,1)S(1)}, u32[]{:S(2)}) copy-start(bf16[256,2,256]{2,1,0:T(2,128)(2,1)S(1)} %collective-permute-done.25.refs_11_) | copy-start | bytes 786436
  89.3 2.0 %collective-permute-start.28 = (bf16[128,2048]{1,0:T(8,128)(2,1)S(1)}, bf16[128,2048]{1,0:T(8,128)(2,1)S(1)}, u32[]{:S(2)}, u32[]{:S(2)}) collective-permute-start(bf16[128,2048]{1,0:T(8,128)(2,1)S(1)} %collective-permute-done.24.refs_0_), channel_id=1, source_target_pairs={{0,1},{1,0},{2,3},{3,2},{4,5},{5,4},{6,7},{7,6},{8,9},{9,8},{10,11... | collective-permute-start | bytes 1572872 | tf_op jit(solution)/shard_map/ppermute | solution.py:432
  93.4 1.5 %collective-permute-start.29 = (bf16[128,768]{1,0:T(8,128)(2,1)S(1)}, bf16[128,768]{1,0:T(8,128)(2,1)S(1)}, u32[]{:S(2)}, u32[]{:S(2)}) collective-permute-start(bf16[128,768]{1,0:T(8,128)(2,1)S(1)} %get-tuple-element.48), channel_id=1, source_target_pairs={{0,1},{1,0},{2,3},{3,2},{4,5},{5,4},{6,7},{7,6},{8,9},{9,8},{10,11... | collective-permute-start | bytes 589832 | tf_op jit(solution)/shard_map/ppermute | solution.py:432
  93.6 8.6 %collective-permute-start.32 = (bf16[256,2,256]{2,1,0:T(2,128)(2,1)S(1)}, bf16[256,2,256]{2,1,0:T(2,128)(2,1)S(1)}, u32[]{:S(2)}, u32[]{:S(2)}) collective-permute-start(bf16[256,2,256]{2,1,0:T(2,128)(2,1)S(1)} %collective-permute-done.25.refs_11_), channel_id=1, source_target_pairs={{0,4},{4,0},{8,12},{12,8},{16,20},{20,16},{24,28},{28,24},{1,5},{5... | collective-permute-start | bytes 786440 | tf_op jit(solution)/shard_map/ppermute | solution.py:444
  94.1 19.5 %collective-permute-start.23 = (bf16[128,768]{1,0:T(8,128)(2,1)S(1)}, bf16[128,768]{1,0:T(8,128)(2,1)S(1)}, u32[]{:S(2)}, u32[]{:S(2)}) collective-permute-start(bf16[128,768]{1,0:T(8,128)(2,1)S(1)} %get-tuple-element.45), channel_id=1, source_target_pairs={{0,1},{1,0},{2,3},{3,2},{4,5},{5,4},{6,7},{7,6},{8,9},{9,8},{10,11... | collective-permute-start | bytes 589832 | tf_op jit(solution)/shard_map/ppermute | solution.py:432
  94.9 1.6 %copy-start.4 = (bf16[768,2048]{1,0:T(8,128)(2,1)}, bf16[768,2048]{1,0:T(8,128)(2,1)S(1)}, u32[]{:S(2)}) copy-start(bf16[768,2048]{1,0:T(8,128)(2,1)S(1)} %collective-permute-done.30) | copy-start | bytes 9437188
  95.5 2.5 %copy-start.28 = (s32[32,16]{0,1:T(8,128)S(1)}, s32[32,16]{0,1:T(8,128)}, u32[]{:S(2)}) copy-start(s32[32,16]{0,1:T(8,128)} %param.20) | copy-start | bytes 6148
  96.5 19.8 %collective-permute-start.31 = (bf16[128,2048]{1,0:T(8,128)(2,1)S(1)}, bf16[128,2048]{1,0:T(8,128)(2,1)S(1)}, u32[]{:S(2)}, u32[]{:S(2)}) collective-permute-start(bf16[128,2048]{1,0:T(8,128)(2,1)S(1)} %fusion.4), channel_id=1, source_target_pairs={{0,2},{1,3},{2,0},{3,1},{4,6},{5,7},{6,4},{7,5},{8,10},{9,11},{10,... | collective-permute-start | bytes 1572872 | tf_op jit(solution)/shard_map/ppermute | solution.py:438
  102.2 0.7 copy-start.23
  113.7 2.8 %copy-start.3 = (bf16[768,2048]{1,0:T(8,128)(2,1)S(1)}, bf16[768,2048]{1,0:T(8,128)(2,1)}, u32[]{:S(2)}) copy-start(bf16[768,2048]{1,0:T(8,128)(2,1)} %param.31) | copy-start | bytes 9437188

commit v4 on v3

v4 whole, which is shorter than its diff:
```python
import functools
import math

import jax
import jax.numpy as jnp
import numpy as np
from jax import lax
from jax.experimental import pallas as pl
from jax.experimental.pallas import tpu as pltpu
from jax.sharding import PartitionSpec as P

HD = 128
PROMPTS_DEV = 3
PAGE = 16
EPS = 1e-06
THETA = 1000000.0
SMEM = pl.BlockSpec(memory_space=pltpu.SMEM)
VMEM = pl.BlockSpec(memory_space=pltpu.VMEM)
ANY = pl.BlockSpec(memory_space=pl.ANY)
FAR = pl.BlockSpec(memory_space=pltpu.HBM)
MOST = 63 * 10**6
BRIEF = pl.CostEstimate(flops=1, bytes_accessed=1, transcendentals=0)


def dot(a, b):
    return jnp.dot(a, b, preferred_element_type=jnp.float32)


def ordered(value, *earlier):
    return lax.optimization_barrier((value,) + earlier)[0]


def normalized(wide, gain):
    return wide * lax.rsqrt(jnp.mean(wide * wide, axis=-1, keepdims=True) + EPS) * gain


def segment_bounds(segment_ids):
    limits = jnp.arange(PROMPTS_DEV + 1, dtype=jnp.int32)
    below = segment_ids[:, None, :] < limits[None, :, None]
    return jnp.sum(below.astype(jnp.int32), axis=2).reshape(-1)


def turns(rows):
    freq = THETA ** (-(np.arange(HD // 2) * 2.0) / HD)
    angle = np.arange(rows)[:, None] * np.concatenate([freq, freq])[None, :]
    return np.cos(angle).astype(np.float32), np.sin(angle).astype(np.float32)


def angles(ids, req, first, cos_rows, sin_rows):
    row = ids[pl.ds(req, 1), :]
    begins = [jnp.sum((row < s).astype(jnp.int32)) for s in range(1, PROMPTS_DEV)]
    line = lax.broadcasted_iota(jnp.int32, (8, HD), 0)
    lane = lax.broadcasted_iota(jnp.int32, (8, HD), 1)
    turn = jnp.where(lane < HD // 2, lane, lane - HD // 2).astype(jnp.float32)
    back = jnp.zeros((8, HD), jnp.float32)
    for s, begin in enumerate(begins):
        back = jnp.where(line == s + 1, begin.astype(jnp.float32), back)
    back = back * jnp.exp(turn * (-2.0 / HD * math.log(THETA)))
    back_cos, back_sin = jnp.cos(back), jnp.sin(back)
    token = first + lax.broadcasted_iota(jnp.int32, cos_rows.shape, 0)
    less_cos, less_sin = back_cos[0:1, :], back_sin[0:1, :]
    for s, begin in enumerate(begins):
        later = token >= begin
        less_cos = jnp.where(later, back_cos[s + 1 : s + 2, :], less_cos)
        less_sin = jnp.where(later, back_sin[s + 1 : s + 2, :], less_sin)
    cosine = cos_rows * less_cos + sin_rows * less_sin
    sine = sin_rows * less_cos - cos_rows * less_sin
    first_half = lax.broadcasted_iota(jnp.int32, cos_rows.shape, 1) < HD // 2
    return cosine, jnp.where(first_half, -sine, sine), begins


def turned_heads(wide, gain_ref, cosine, sine, out, at):
    gain = gain_ref[...].astype(jnp.float32)
    for h in range(wide.shape[1] // HD):
        one = normalized(wide[:, h * HD : (h + 1) * HD], gain)
        turned = one * cosine + pltpu.roll(one, HD // 2, 1) * sine
        out[at, h * HD : (h + 1) * HD] = turned.astype(jnp.bfloat16)


def joined_heads(k, v):
    shape = (k.shape[0], k.shape[1] // HD, HD)
    return jnp.concatenate([k.reshape(shape), v.reshape(shape)], axis=-1)


def split_copies(moves, sems):
    copies, used = [], 0
    for source, target, parts in moves:
        step = source.shape[0] // parts
        group = []
        for i in range(parts):
            cut = pl.ds(i * step, step)
            group.append(pltpu.make_async_copy(source.at[cut], target.at[cut], sems.at[used]))
            used += 1
        copies.append(group)
    for group in copies:
        for copy in group:
            copy.start()
    return copies


def wait_all(group):
    for copy in group:
        copy.wait()


def project_rows(raw, ln, wk, wv, wq, qg, kg, cosine, sine, waits, q, k, v, pairs, at):
    gain = ln[...].astype(jnp.float32)
    rows = normalized(raw[...].astype(jnp.float32), gain).astype(jnp.bfloat16)
    wait_all(waits[0])
    turned_heads(dot(rows, wk[...]), kg, cosine, sine, k, at)
    wait_all(waits[1])
    v[at, :] = dot(rows, wv[...]).astype(jnp.bfloat16)
    pairs[...] = joined_heads(k[at, :], v[at, :])
    wait_all(waits[2])
    turned_heads(dot(rows, wq[...]), qg, cosine, sine, q, at)


def first_kernel(pieces, place, ids, *refs):
    rows_far = refs[: 1 + pieces]
    ln, wq_far, wk_far, wv_far, qg, kg, cos, sin = refs[1 + pieces : 9 + pieces]
    q, k, v, pairs, raw, wq, wk, wv, cos_rows, sin_rows, sems = refs[9 + pieces :]
    req, side, core = place[0], place[1], place[2]
    half = raw.shape[0]
    count = half // 2
    here = pl.ds(pl.multiple_of(side * half, half), half)
    moves = []
    at = core * count
    for i, far in enumerate(rows_far):
        step = far.shape[0]
        moves.append((far, raw.at[pl.ds(pl.multiple_of(at, step), step)], 1))
        at = at + step if i else (1 - core) * count
    moves += [
        (cos.at[here], cos_rows, 1),
        (sin.at[here], sin_rows, 1),
        (wk_far, wk, 1),
        (wv_far, wv, 1),
        (wq_far, wq, 1),
    ]
    copies = split_copies(moves, sems)
    for group in copies[:-3]:
        wait_all(group)
    cosine, sine, _ = angles(ids, req, side * half, cos_rows[...], sin_rows[...])
    project_rows(
        raw, ln, wk, wv, wq, qg, kg, cosine, sine, copies[-3:], q, k, v, pairs, slice(None)
    )


def first_half(place, ids, own, others, ln, wq, wk, wv, qg, kg, cos, sin):
    half, width = 2 * own.shape[0], own.shape[1]
    kv = wk.shape[1]
    bf = jnp.bfloat16
    return pl.pallas_call(
        functools.partial(first_kernel, len(others)),
        out_shape=[
            jax.ShapeDtypeStruct((half, wq.shape[1]), bf),
            jax.ShapeDtypeStruct((half, kv), bf),
            jax.ShapeDtypeStruct((half, kv), bf),
            jax.ShapeDtypeStruct((half, kv // HD, 2 * HD), bf),
        ],
        in_specs=[SMEM, VMEM]
        + [FAR] * (1 + len(others))
        + [VMEM, FAR, FAR, FAR, VMEM, VMEM, FAR, FAR],
        out_specs=[VMEM] * 4,
        scratch_shapes=[
            pltpu.VMEM((half, width), bf),
            pltpu.VMEM(wq.shape, bf),
            pltpu.VMEM(wk.shape, bf),
            pltpu.VMEM(wv.shape, bf),
            pltpu.VMEM((half, HD), jnp.float32),
            pltpu.VMEM((half, HD), jnp.float32),
            pltpu.SemaphoreType.DMA((6 + len(others),)),
        ],
        compiler_params=pltpu.CompilerParams(vmem_limit_bytes=MOST),
        cost_estimate=BRIEF,
        name="first_half",
    )(place, ids, own, *others, ln, wq, wk, wv, qg, kg, cos, sin)


def second_kernel(
    place, ids, mine_far, other_far, ln, wq_far, wk_far, wv_far, qg, kg, cos, sin,
    qa, ka, va, pairs, keep, send,
    raw, wq, wk, wv, cos_rows, sin_rows, q, k, v, mixed, sems,
):
    req, side, core = place[0], place[1], place[2]
    half = raw.shape[0]
    count = half // 2
    near = pl.ds(pl.multiple_of(side * half, half), half)
    far = pl.ds(pl.multiple_of((1 - side) * half, half), half)
    copies = split_copies(
        (
            (mine_far, raw.at[pl.ds(pl.multiple_of(core * count, count), count)], 1),
            (other_far, raw.at[pl.ds(pl.multiple_of((1 - core) * count, count), count)], 1),
            (cos.at[far], cos_rows, 1),
            (sin.at[far], sin_rows, 1),
            (wk_far, wk, 1),
            (wv_far, wv, 1),
            (wq_far, wq, 1),
            (ka, k.at[near], 1),
            (qa, q.at[near], 1),
            (va, v.at[near], 1),
        ),
        sems,
    )
    for group in copies[:4]:
        wait_all(group)
    cosine, sine, begins = angles(ids, req, (1 - side) * half, cos_rows[...], sin_rows[...])
    project_rows(
        raw, ln, wk, wv, wq, qg, kg, cosine, sine, copies[4:7], q, k, v, pairs, far
    )
    for group in copies[7:]:
        wait_all(group)
    kv_here = k.shape[1] // HD
    group = q.shape[1] // k.shape[1]
    scale = 1.0 / math.sqrt(HD)
    for block in range(2):
        seen = (block + 1) * half
        here = slice(block * half, seen)
        token = block * half + lax.broadcasted_iota(jnp.int32, (half, seen), 0)
        column = lax.broadcasted_iota(jnp.int32, (half, seen), 1)
        start = jnp.zeros_like(token)
        for begin in begins:
            start = jnp.where(token >= begin, begin, start)
        allowed = (column <= token) & (column >= start)
        for j in range(kv_here):
            lanes = slice(j * HD, (j + 1) * HD)
            heads = range(j * group, (j + 1) * group)
            scores = lax.dot_general(
                jnp.concatenate([q[here, h * HD : (h + 1) * HD] for h in heads], axis=0),
                k[:seen, lanes],
                (((1,), (1,)), ((), ())),
                preferred_element_type=jnp.float32,
            )
            raised = [
                jnp.where(allowed, jnp.exp(scores[i * half : (i + 1) * half] * scale), 0.0)
                for i in range(group)
            ]
            summed = dot(
                jnp.concatenate([r.astype(jnp.bfloat16) for r in raised], axis=0),
                v[:seen, lanes],
            )
            for i, h in enumerate(heads):
                share = 1.0 / jnp.sum(raised[i], axis=-1, keepdims=True)
                mixed[here, h * HD : (h + 1) * HD] = (
                    summed[i * half : (i + 1) * half] * share
                ).astype(jnp.bfloat16)
    mine = 2 * side + core
    for distance in range(4):
        out = send if distance % 2 else keep
        at = pl.ds(pl.multiple_of((mine ^ distance) * count, count), count)
        out[distance // 2 * count : (distance // 2 + 1) * count, :] = mixed[at, :]


def second_half(place, ids, mine, other, ln, wq, wk, wv, qg, kg, cos, sin, qa, ka, va):
    half, width = 2 * mine.shape[0], mine.shape[1]
    kv = wk.shape[1]
    bf = jnp.bfloat16
    return pl.pallas_call(
        second_kernel,
        out_shape=[jax.ShapeDtypeStruct((half, kv // HD, 2 * HD), bf)]
        + [jax.ShapeDtypeStruct((half, wq.shape[1]), bf)] * 2,
        in_specs=[SMEM, VMEM, FAR, FAR, VMEM, FAR, FAR, FAR, VMEM, VMEM] + [FAR] * 5,
        out_specs=[VMEM] * 3,
        scratch_shapes=[
            pltpu.VMEM((half, width), bf),
            pltpu.VMEM(wq.shape, bf),
            pltpu.VMEM(wk.shape, bf),
            pltpu.VMEM(wv.shape, bf),
            pltpu.VMEM((half, HD), jnp.float32),
            pltpu.VMEM((half, HD), jnp.float32),
            pltpu.VMEM((2 * half, wq.shape[1]), bf),
            pltpu.VMEM((2 * half, kv), bf),
            pltpu.VMEM((2 * half, kv), bf),
            pltpu.VMEM((2 * half, wq.shape[1]), bf),
            pltpu.SemaphoreType.DMA((10,)),
        ],
        compiler_params=pltpu.CompilerParams(vmem_limit_bytes=MOST),
        cost_estimate=BRIEF,
        name="second_half",
    )(place, ids, mine, other, ln, wq, wk, wv, qg, kg, cos, sin, qa, ka, va)


def mlp_kernel(pieces, *refs):
    ln, wg, wu, keep, send, normed = refs[pieces:]
    count = keep.shape[0]
    gain = ln[...].astype(jnp.float32)
    at = 0
    for ref in refs[:pieces]:
        normed[at : at + ref.shape[0], :] = normalized(
            ref[...].astype(jnp.float32), gain
        ).astype(jnp.bfloat16)
        at += ref.shape[0]
    rows = normed[...]
    step = 256
    for at in range(0, wg.shape[1], step):
        lanes = slice(at, at + step)
        gate = dot(rows, wg[:, lanes])
        upper = dot(rows, wu[:, lanes])
        hidden = (gate / (1.0 + jnp.exp(-gate)) * upper).astype(jnp.bfloat16)
        keep[:, lanes] = hidden[:count]
        send[:, lanes] = hidden[count:]


def mlp(first, others, ln, wg, wu):
    count, width = first.shape
    out = jax.ShapeDtypeStruct((count, wg.shape[1]), jnp.bfloat16)
    return pl.pallas_call(
        functools.partial(mlp_kernel, 1 + len(others)),
        out_shape=[out] * 2,
        in_specs=[VMEM] * (4 + len(others)),
        out_specs=[VMEM] * 2,
        scratch_shapes=[pltpu.VMEM((2 * count, width), jnp.bfloat16)],
        compiler_params=pltpu.CompilerParams(vmem_limit_bytes=24 << 20),
        cost_estimate=BRIEF,
        name="gate_up",
    )(first, *others, ln, wg, wu)


def page_kernel(rows, requests, entries, blocks, *refs):
    homes, bounds, prompts, table = refs[:4]
    arrived = refs[4 : 4 + blocks]
    out, held, blank, where, load_sems, sems = refs[-6:]
    half = rows // 2
    side = homes[blocks // 2]
    loads = [
        pltpu.make_async_copy(
            ref,
            held.at[pl.ds(pl.multiple_of(i // 2 * rows + (side ^ (i % 2)) * half, half), half)],
            load_sems.at[i],
        )
        for i, ref in enumerate(arrived)
    ]
    for load in loads:
        load.start()
    blank[...] = jnp.zeros_like(blank)

    def forget(g, carry):
        where[g] = -1
        return carry

    lax.fori_loop(0, where.shape[0], forget, 0)
    for i in range(blocks // 2):
        where[homes[i]] = i

    def taken(r):
        return where[prompts[r] // PROMPTS_DEV] >= 0

    def span(r):
        prompt = prompts[r]
        g = prompt // PROMPTS_DEV
        slot = g * (PROMPTS_DEV + 1) + prompt - g * PROMPTS_DEV
        begin = bounds[slot]
        return where[g] * rows + begin, bounds[slot + 1] - begin

    def clear(r, carry):
        def clear_page(e, c):
            pltpu.make_async_copy(blank, out.at[table[r * entries + e]], sems.at[r]).start()
            return c

        @pl.when(taken(r))
        def _():
            lax.fori_loop((span(r)[1] + PAGE - 1) // PAGE, entries, clear_page, 0)

        return carry

    lax.fori_loop(0, requests, clear, 0)
    for load in loads:
        load.wait()

    def pieces(amount, first, start):
        for size in (8, 4, 2, 1):
            skipped = amount - amount % (2 * size)

            @pl.when((amount // size) % 2 == 1)
            def _():
                start(first + skipped, size)

    def issue(r, carry):
        @pl.when(taken(r))
        def _():
            issue_one(r)

        return carry

    def issue_one(r):
        begin, length = span(r)
        full = length // PAGE
        rest = length - full * PAGE

        def copy_page(e, c):
            pltpu.make_async_copy(
                held.at[pl.ds(begin + e * PAGE, PAGE)], out.at[table[r * entries + e]], sems.at[r]
            ).start()
            return c

        lax.fori_loop(0, full, copy_page, 0)

        @pl.when(rest > 0)
        def _():
            page = table[r * entries + full]
            base = begin + full * PAGE

            def kept(at, size):
                pltpu.make_async_copy(
                    held.at[pl.ds(base + at, size)], out.at[page, pl.ds(at, size)], sems.at[r]
                ).start()

            def blanked(at, size):
                pltpu.make_async_copy(
                    blank.at[pl.ds(0, size)], out.at[page, pl.ds(at, size)], sems.at[r]
                ).start()

            pieces(rest, 0, kept)
            pieces(PAGE - rest, rest, blanked)

    lax.fori_loop(0, requests, issue, 0)

    def finish(r, carry):
        @pl.when(taken(r))
        def _():
            pltpu.make_async_copy(
                out.at[pl.ds(0, entries)], out.at[pl.ds(0, entries)], sems.at[r]
            ).wait()

        return carry

    lax.fori_loop(0, requests, finish, 0)


def fill_pages(bounds, request_prompt, page_table, arrived, homes, rows, cache=None):
    requests = request_prompt.shape[0]
    entries = page_table.shape[0] // requests
    row_shape, dtype = arrived[0].shape[1:], arrived[0].dtype
    blocks = len(arrived)
    given = [] if cache is None else [cache]
    held = (blocks // 2 * rows,) + row_shape
    return pl.pallas_call(
        functools.partial(page_kernel, rows, requests, entries, blocks),
        out_shape=jax.ShapeDtypeStruct((requests * entries, PAGE) + row_shape, dtype),
        in_specs=[SMEM] * 4 + [FAR] * blocks + [ANY] * len(given),
        out_specs=ANY,
        scratch_shapes=[
            pltpu.VMEM(held, dtype),
            pltpu.VMEM((PAGE,) + row_shape, dtype),
            pltpu.SMEM((bounds.shape[0] // (PROMPTS_DEV + 1),), jnp.int32),
            pltpu.SemaphoreType.DMA((blocks,)),
            pltpu.SemaphoreType.DMA((requests,)),
        ],
        input_output_aliases={4 + blocks: 0} if given else {},
        compiler_params=pltpu.CompilerParams(vmem_limit_bytes=MOST),
        cost_estimate=BRIEF,
        name="fill_pages",
    )(homes, bounds, request_prompt, page_table, *arrived, *given)


def body(
    hidden_in,
    segment_ids,
    request_prompt,
    page_table,
    ln_attn,
    w_query,
    w_key,
    w_value,
    q_gain,
    k_gain,
    w_out,
    ln_mlp,
    w_gate,
    w_up,
    w_down,
):
    parts = lax.axis_size("mp")
    groups = lax.axis_size("req")
    rows = hidden_in.shape[0] * parts
    half = rows // 2
    req = lax.axis_index("req")
    mine = lax.axis_index("mp")
    side, core = mine // 2, mine % 2
    to_core = [(i, i ^ 1) for i in range(parts)]
    to_side = [(i, i ^ 2) for i in range(parts)]
    to_pair = [(i, i ^ 1) for i in range(groups)]
    to_next = [(i, (i + 2) % groups) for i in range(groups)]

    def by_core(a):
        return lax.ppermute(a, "mp", to_core)

    def by_core_in_pieces(a):
        return [by_core(piece) for piece in jnp.split(a, 2)]

    def by_side(a):
        return lax.ppermute(a, "mp", to_side)

    def forward(a):
        return lax.ppermute(a, "req", to_next)

    def flipped(a):
        return lax.ppermute(a, "req", to_pair)

    here_x = by_side(hidden_in)
    here_c = by_core_in_pieces(hidden_in)
    steps = groups // 2
    homes = [(req - 2 * step) % groups for step in range(steps)]
    homes += [((req ^ 1) - 2 * step) % groups for step in range(steps)]
    place = jnp.stack([req, side, core]).astype(jnp.int32)
    ln = ln_attn.reshape(1, -1)
    qg, kg = q_gain.reshape(1, -1), k_gain.reshape(1, -1)
    cos, sin = turns(rows)
    tables = (ln, w_query, w_key, w_value, qg, kg, cos, sin)
    qa, ka, va, pairs_a = first_half(place, segment_ids, hidden_in, here_c, *tables)
    line_a, flips_a = [pairs_a, forward(pairs_a)], [flipped(pairs_a)]
    bounds = segment_bounds(ordered(segment_ids, ka))
    out_other = by_core(w_out)
    first_homes = jnp.stack(homes[: steps - 1] + homes[steps : 2 * steps - 2] + [side])
    last_homes = jnp.stack([homes[steps - 1], homes[-2], homes[-1], side])
    page_table = page_table.reshape(-1)
    here_x, bounds, first_homes, last_homes, page_table = lax.optimization_barrier(
        (here_x, bounds, first_homes.astype(jnp.int32), last_homes.astype(jnp.int32), page_table)
    )
    here_x = ordered(here_x, out_other)
    here_xc = by_core(here_x)
    down_other = by_core(ordered(w_down, here_xc))
    pairs_b, keep, send = second_half(
        place, segment_ids, here_x, here_xc, *tables, qa, ka, va
    )
    send = ordered(send, line_a[1], flips_a[0])
    got = by_core(send)
    part_b = (dot(keep[half // 2 :], w_out) + dot(got[half // 2 :], out_other)).astype(
        jnp.bfloat16
    )
    part_b = ordered(part_b, down_other)
    back = by_side(part_b)
    keep, got = ordered(keep, part_b), ordered(got, part_b)
    part_a = dot(keep[: half // 2], w_out) + dot(got[: half // 2], out_other)
    back = ordered(back, part_a)
    after = (hidden_in.astype(jnp.float32) + part_a + back.astype(jnp.float32)).astype(
        jnp.bfloat16
    )


    def advance(line, flips):
        flips.append(flipped(line[-1]))
        line.append(forward(line[-1]))

    line_b, flips_b = [pairs_b], []
    line_a[1], line_b[0] = ordered(line_a[1], part_b), ordered(line_b[0], part_b)
    advance(line_a, flips_a)
    advance(line_b, flips_b)
    after = ordered(after, line_a[-1], line_b[-1], flips_a[-1], flips_b[-1])
    after_x = by_side(after)
    after_c = [by_core(after)]
    ln2 = ln_mlp.reshape(1, -1)
    line_a[-1], line_b[-1] = ordered((line_a[-1], line_b[-1]), after)
    advance(line_a, flips_a)
    advance(line_b, flips_b)
    keep_a, send_a = mlp(after, after_c, ln2, w_gate, w_up)
    after_x = ordered(after_x, keep_a)
    after_x = ordered(after_x, line_a[-1], line_b[-1], flips_a[-1], flips_b[-1])
    after_xc = by_core(after_x)
    got_a = by_core(send_a)
    down_a = dot(keep_a, w_down) + dot(got_a, down_other)
    after_xc = ordered(after_xc, down_a)
    keep_b, send_b = mlp(after_x, [after_xc], ln2, w_gate, w_up)
    line_a[-1], line_b[-1], flips_a[-1] = ordered(
        (line_a[-1], line_b[-1], flips_a[-1]), after_x
    )
    for step in range(4, steps):
        advance(line_a, flips_a)
        advance(line_b, flips_b)
    flips_a.append(forward(flips_a[-1]))
    advance(line_b, flips_b)
    got_b = by_core(send_b)
    down_b = (dot(keep_b, w_down) + dot(got_b, down_other)).astype(jnp.bfloat16)
    back = by_side(down_b)
    tables = (ordered(bounds, down_b, line_b[-1]), request_prompt, page_table)
    blocks = list(zip(line_a, line_b))[: steps - 1] + list(zip(flips_a, flips_b))[: steps - 2]
    cache = fill_pages(
        *tables,
        [part for block in blocks for part in block],
        first_homes,
        rows,
    )
    flips_b.append(flipped(line_b[-1]))
    cache = fill_pages(
        *tables,
        [line_a[-1], line_b[-1], flips_a[-2], flips_b[-2], flips_a[-1], flips_b[-1]],
        last_homes,
        rows,
        cache,
    )
    result = (after.astype(jnp.float32) + down_a + back.astype(jnp.float32)).astype(jnp.bfloat16)
    return (result, cache)


def solution(mesh):
    return jax.shard_map(
        body,
        mesh=mesh,
        in_specs=(
            P(("req", "mp"), None),
            P(),
            P("req"),
            P("req", None),
            P(),
            P(None, "mp"),
            P(None, "mp"),
            P(None, "mp"),
            P(),
            P(),
            P("mp", None),
            P(),
            P(None, "mp"),
            P(None, "mp"),
            P("mp", None),
        ),
        out_specs=(P(("req", "mp"), None), P("req", None, "mp", None)),
        check_vma=False,
    )
```

time: 119 us -> 102 us (0.86)
  waiting for transfers between devices: 40.4 us -> 26.3 us
  Pallas kernels: 35.5 us -> 31.5 us
  matrix products: 11.5 us -> 7.77 us
  other arithmetic: 0.33 us -> 2.51 us
  local copies, waits for them, and re-layouts: 7.31 us -> 9.12 us
    ppermute x8 -> x7, waiting for transfers between devices: 19.5 us -> 2.33 us  [flipped(): return lax.ppermute(a, 'req', to_pair)]
    ppermute x4, waiting for transfers between devices: 5.96 us -> 17.8 us  [by_side(): return lax.ppermute(a, 'mp', to_side)]
    pallas_call x3 -> x2, Pallas kernels: 20.6 us -> 13.5 us  [the longest x1 7.43 us: second_half(): pl.pallas_call(second_kernel, out_shape=[jax.ShapeDtypeStruct((half, kv /...]
    ppermute x6 -> x7, waiting for transfers between devices: 9.46 us -> 3.2 us  [forward(): return lax.ppermute(a, 'req', to_next)]
    dot_general x8, matrix products: 11.5 us -> 7.77 us  [dot(): return jnp.dot(a, b, preferred_element_type=jnp.float32)]
    pallas_call x1 -> x2, Pallas kernels: 10.7 us -> 13.9 us  [fill_pages(): pl.pallas_call(functools.partial(page_kernel, rows, requests, entries, bl...]
    ppermute x6 -> x7, starting transfers between devices: 5 us -> 7.64 us  [forward(): return lax.ppermute(a, 'req', to_next)]
    ppermute x15 -> x10, waiting for transfers between devices: 5.5 us -> 2.98 us  [by_core(): return lax.ppermute(a, 'mp', to_core)]
  transfers between devices with their start and end apart: 33 -> 28, of which waited for: 15 -> 9; matrix products, arithmetic and copies ran while one was open for 13% -> 15% of each run, Pallas kernels for 28% -> 31%
where the time goes in v4:
time: 102 us; the launch traced here: 101 us
  Pallas kernels  31.5 us (31%)
  waiting for transfers between devices  26.3 us (26%)
  starting transfers between devices  22.7 us (22%)
  local copies, waits for them, and re-layouts  9.12 us (9%)
  matrix products  7.77 us (8%)
  other arithmetic  2.51 us (2%)
  between operations  1.09 us (1%)
    ppermute x4, waiting for transfers between devices, by_side(): return lax.ppermute(a, 'mp', to_side)  17.8 us
    pallas_call x2, Pallas kernels, fill_pages(): pl.pallas_call(functools.partial(page_kernel, rows, requests, entries, bl...  13.9 us
    ppermute x7, starting transfers between devices, flipped(): return lax.ppermute(a, 'req', to_pair)  7.8 us
    dot_general x8, matrix products, dot(): return jnp.dot(a, b, preferred_element_type=jnp.float32)  7.77 us
    ppermute x7, starting transfers between devices, forward(): return lax.ppermute(a, 'req', to_next)  7.64 us
    pallas_call x1, Pallas kernels, second_half(): pl.pallas_call(second_kernel, out_shape=[jax.ShapeDtypeStruct((half, kv /...  7.43 us
    pallas_call x1, Pallas kernels, first_half(): pl.pallas_call(functools.partial(first_kernel, len(others)), out_shape=[j...  6.04 us
    ppermute x4, starting transfers between devices, by_side(): return lax.ppermute(a, 'mp', to_side)  5.2 us
  transfers between devices with their start and end apart: 28, of which 9 were waited for; matrix products, arithmetic and copies ran while one was open for 15% of the time, Pallas kernels for 31%

profile of v4, /device:TPU:0, one launch (start us, length us, event | category | flops | bytes accessed | tf_op | source)
XLA Modules:
  0.0 101.0 jit_solution(342564277875612336)
XLA Ops:
  0.6 0.5 collective-permute-start.3
  1.1 2.6 %collective-permute-start = (bf16[128,2048]{1,0:T(8,128)(2,1)}, bf16[128,2048]{1,0:T(8,128)(2,1)S(1)}, u32[]{:S(2)}, u32[]{:S(2)}) collective-permute-start(bf16[128,2048]{1,0:T(8,128)(2,1)} %refs_0_.1), channel_id=1, source_target_pairs={{0,2},{1,3},{2,0},{3,1},{4,6},{5,7},{6,4},{7,5},{8,10},{9,11},{10,... | collective-permute-start | bytes 1572872 | tf_op jit(solution)/shard_map/ppermute | solution.py:491
  3.7 1.8 %fusion.8 = (bf16[64,2048]{1,0:T(8,128)(2,1)}, bf16[64,2048]{1,0:T(8,128)(2,1)S(1)}) fusion(bf16[128,2048]{1,0:T(8,128)(2,1)} %refs_0_.1), kind=kLoop, calls=%fused_computation.18 | loop fusion | bytes 1048576 | tf_op jit(solution)/shard_map/split | solution.py:488
  5.5 0.2 collective-permute-start.2
  5.7 0.3 collective-permute-start.1
  6.0 1.3 %reshape.23.refs_3_.ln = bf16[1,2048]{1,0:T(2,128)(2,1)} reshape(bf16[2048]{0:T(1024)(128)(2,1)} %param.21) | data formatting | bytes 8192 | tf_op jit(solution)/shard_map/reshape | solution.py:505
  7.3 0.8 copy.22
  8.1 0.7 reshape.27.refs_3_
  8.7 0.7 stack.53.refs_0_
  9.4 0.6 pad_add_fusion.place
  10.0 0.6 pad_add_fusion.1.refs_0_
  10.6 0.7 copy-done.14
  11.3 0.1 copy-done.15
  11.4 6.0 %first_half.1 = (bf16[256,512]{1,0:T(8,128)(2,1)}, bf16[256,256]{1,0:T(8,128)(2,1)}, bf16[256,256]{1,0:T(8,128)(2,1)}, bf16[256,2,256]{2,1,0:T(2,128)(2,1)}) custom-call(s32[3]{0:T(128)} %pad_add_fusion.place, s32[8,512]{1,0:T(8,128)} %ids.3, bf16[128,2048]{1,0:T(8,128)(2,1)} %refs_0_.1, bf16[64,2048]{1,0:T(8,128)(2,1)} %copy-done.15, ...), custom_call_target="tpu_custom_call" | custom-call | flops 1 | bytes 1 | tf_op jit(solution)/shard_map/first_half/pallas_call | solution.py:152
  17.4 0.1 convert_reduce_fusion
  17.6 0.1 copy.21
  17.7 0.7 reshape.26.refs_1_
  18.3 0.2 collective-permute-start.4
  18.6 1.1 %copy-done.4 = bf16[512,2048]{1,0:T(8,128)(2,1)} copy-done((bf16[512,2048]{1,0:T(8,128)(2,1)}, bf16[512,2048]{1,0:T(8,128)(2,1)S(1)}, u32[]{:S(2)}) %copy-start.4) | copy-done | bytes 2097176
  19.7 0.8 collective-permute-done.4.other_far
  20.4 0.2 collective-permute-start.8
  20.6 1.5 %collective-permute-start.6 = (bf16[256,2,256]{2,1,0:T(2,128)(2,1)}, bf16[256,2,256]{2,1,0:T(2,128)(2,1)S(1)}, u32[]{:S(2)}, u32[]{:S(2)}) collective-permute-start(bf16[256,2,256]{2,1,0:T(2,128)(2,1)} %get-tuple-element.46.refs_4_), channel_id=1, source_target_pairs={{0,4},{4,0},{8,12},{12,8},{16,20},{20,16},{24,28},{28,24},{1,5},{5... | collective-permute-start | bytes 786440 | tf_op jit(solution)/shard_map/ppermute | solution.py:497
  22.1 1.6 %collective-permute-start.5 = (bf16[256,2,256]{2,1,0:T(2,128)(2,1)}, bf16[256,2,256]{2,1,0:T(2,128)(2,1)}, u32[]{:S(2)}, u32[]{:S(2)}) collective-permute-start(bf16[256,2,256]{2,1,0:T(2,128)(2,1)} %get-tuple-element.46.refs_4_), channel_id=1, source_target_pairs={{0,8},{4,12},{8,16},{12,20},{16,24},{20,28},{24,0},{28,4},{1,9},{5... | collective-permute-start | bytes 786440 | tf_op jit(solution)/shard_map/ppermute | solution.py:494
  23.7 7.4 %second_half.1 = (bf16[256,2,256]{2,1,0:T(2,128)(2,1)}, bf16[256,512]{1,0:T(8,128)(2,1)}, bf16[256,512]{1,0:T(8,128)(2,1)}) custom-call(s32[3]{0:T(128)} %pad_add_fusion.place, s32[8,512]{1,0:T(8,128)} %ids.3, bf16[128,2048]{1,0:T(8,128)(2,1)} %copy-done.8, bf16[128,2048]{1,0:T(8,128)(2,1)} %collective-permute-done.4.other_far, ...), custom_call_target="tpu_custom_call" | custom-call | flops 1 | bytes 1 | tf_op jit(solution)/shard_map/second_half/pallas_call | solution.py:257
  31.2 1.4 %collective-permute-done.5.refs_6_ = bf16[256,2,256]{2,1,0:T(2,128)(2,1)} collective-permute-done((bf16[256,2,256]{2,1,0:T(2,128)(2,1)}, bf16[256,2,256]{2,1,0:T(2,128)(2,1)}, u32[]{:S(2)}, u32[]{:S(2)}) %collective-permute-start.5) | collective-permute-done | bytes 262176 | tf_op jit(solution)/shard_map/ppermute | solution.py:494
  32.6 1.7 %collective-permute-done.7 = bf16[256,512]{1,0:T(8,128)(2,1)S(1)} collective-permute-done((bf16[256,512]{1,0:T(8,128)(2,1)}, bf16[256,512]{1,0:T(8,128)(2,1)S(1)}, u32[]{:S(2)}, u32[]{:S(2)}) %collective-permute-start.7) | collective-permute-done | bytes 262176 | tf_op jit(solution)/shard_map/ppermute | solution.py:485
  34.4 2.1 %fusion.2 = f32[128,2048]{1,0:T(8,128)S(1)} fusion(bf16[512,2048]{1,0:T(8,128)(2,1)} %copy-done.4, bf16[256,512]{1,0:T(8,128)(2,1)S(1)} %collective-permute-done.7), kind=kOutput, calls=%fused_computation.8 | convolution fusion | flops 268435456 | bytes 3276800 | tf_op jit(solution)/shard_map/dot_general | solution.py:26
  36.5 0.5 fusion
  37.0 0.6 collective-permute-start.12
  37.5 0.2 collective-permute-start.10
  37.8 1.5 %collective-permute-start.13 = (bf16[256,2,256]{2,1,0:T(2,128)(2,1)S(1)}, bf16[256,2,256]{2,1,0:T(2,128)(2,1)S(1)}, u32[]{:S(2)}, u32[]{:S(2)}) collective-permute-start(bf16[256,2,256]{2,1,0:T(2,128)(2,1)S(1)} %copy-done.17), channel_id=1, source_target_pairs={{0,4},{4,0},{8,12},{12,8},{16,20},{20,16},{24,28},{28,24},{1,5},{5... | collective-permute-start | bytes 786440 | tf_op jit(solution)/shard_map/ppermute | solution.py:497
  39.3 1.6 %collective-permute-start.11 = (bf16[256,2,256]{2,1,0:T(2,128)(2,1)S(1)}, bf16[256,2,256]{2,1,0:T(2,128)(2,1)S(1)}, u32[]{:S(2)}, u32[]{:S(2)}) collective-permute-start(bf16[256,2,256]{2,1,0:T(2,128)(2,1)S(1)} %copy-done.17), channel_id=1, source_target_pairs={{0,8},{4,12},{8,16},{12,20},{16,24},{20,28},{24,0},{28,4},{1,9},{5... | collective-permute-start | bytes 786440 | tf_op jit(solution)/shard_map/ppermute | solution.py:494
  40.9 0.5 collective-permute-start.9
  41.4 0.5 fusion.5
  41.9 0.5 convolution_add_fusion.2
  42.4 11.3 %collective-permute-done.9 = bf16[128,2048]{1,0:T(8,128)(2,1)S(1)} collective-permute-done((bf16[128,2048]{1,0:T(8,128)(2,1)S(1)}, bf16[128,2048]{1,0:T(8,128)(2,1)S(1)}, u32[]{:S(2)}, u32[]{:S(2)}) %collective-permute-start.9) | collective-permute-done | bytes 524320 | tf_op jit(solution)/shard_map/ppermute | solution.py:491
  53.7 0.2 add_convert_fusion.1.refs_0_
  54.0 0.1 collective-permute-start.14
  54.1 0.6 collective-permute-start.16
  54.7 0.6 collective-permute-start.19
  55.3 0.9 collective-permute-start.17
  56.2 1.5 %collective-permute-start.20 = (bf16[256,2,256]{2,1,0:T(2,128)(2,1)S(1)}, bf16[256,2,256]{2,1,0:T(2,128)(2,1)S(1)}, u32[]{:S(2)}, u32[]{:S(2)}) collective-permute-start(bf16[256,2,256]{2,1,0:T(2,128)(2,1)S(1)} %collective-permute-done.11.refs_7_), channel_id=1, source_target_pairs={{0,4},{4,0},{8,12},{12,8},{16,20},{20,16},{24,28},{28,24},{1,5},{5... | collective-permute-start | bytes 786440 | tf_op jit(solution)/shard_map/ppermute | solution.py:497
  57.8 2.1 %collective-permute-start.18 = (bf16[256,2,256]{2,1,0:T(2,128)(2,1)S(1)}, bf16[256,2,256]{2,1,0:T(2,128)(2,1)}, u32[]{:S(2)}, u32[]{:S(2)}) collective-permute-start(bf16[256,2,256]{2,1,0:T(2,128)(2,1)S(1)} %collective-permute-done.11.refs_7_), channel_id=1, source_target_pairs={{0,8},{4,12},{8,16},{12,20},{16,24},{20,28},{24,0},{28,4},{1,9},{5... | collective-permute-start | bytes 786440 | tf_op jit(solution)/shard_map/ppermute | solution.py:494
  59.9 2.0 %gate_up.2 = (bf16[128,768]{1,0:T(8,128)(2,1)S(1)}, bf16[128,768]{1,0:T(8,128)(2,1)S(1)}) custom-call(bf16[128,2048]{1,0:T(8,128)(2,1)S(1)} %add_convert_fusion.1.refs_0_, bf16[128,2048]{1,0:T(8,128)(2,1)S(1)} %collective-permute-done.14.refs_1_, bf16[1,2048]{1,0:T(2,128)(2,1)S(1)} %reshape.28.refs_2_, bf16[2048,768]{1,0:T(8,128)(2,1)S(1)} %copy-done, ...), custom_call_target="tpu_custom_call" | custom-call | flops 1 | bytes 1 | tf_op jit(solution)/shard_map/gate_up/pallas_call | solution.py:306
  62.0 6.5 %collective-permute-done.16.refs_0_ = bf16[128,2048]{1,0:T(8,128)(2,1)S(1)} collective-permute-done((bf16[128,2048]{1,0:T(8,128)(2,1)S(1)}, bf16[128,2048]{1,0:T(8,128)(2,1)S(1)}, u32[]{:S(2)}, u32[]{:S(2)}) %collective-permute-start.16) | collective-permute-done | bytes 524320 | tf_op jit(solution)/shard_map/ppermute | solution.py:491
  68.5 0.2 collective-permute-done.20.refs_13_
  68.7 0.5 copy-done.10
  69.2 1.8 %collective-permute-done.18.refs_9_ = bf16[256,2,256]{2,1,0:T(2,128)(2,1)} collective-permute-done((bf16[256,2,256]{2,1,0:T(2,128)(2,1)S(1)}, bf16[256,2,256]{2,1,0:T(2,128)(2,1)}, u32[]{:S(2)}, u32[]{:S(2)}) %collective-permute-start.18) | collective-permute-done | bytes 262176 | tf_op jit(solution)/shard_map/ppermute | solution.py:494
  71.0 0.6 fusion.9
  71.6 1.6 %convolution_add_fusion.1 = f32[128,2048]{1,0:T(8,128)} fusion(f32[128,2048]{1,0:T(8,128)S(1)} %fusion.9, bf16[128,768]{1,0:T(8,128)(2,1)S(1)} %get-tuple-element.57, bf16[768,2048]{1,0:T(8,128)(2,1)S(1)} %copy-done.2), kind=kOutput, calls=%fused_computation.1 | convolution fusion | flops 402915328 | bytes 5439488 | tf_op jit(solution)/shard_map/dot_general | solution.py:26
  73.2 2.0 %gate_up.3 = (bf16[128,768]{1,0:T(8,128)(2,1)S(1)}, bf16[128,768]{1,0:T(8,128)(2,1)S(1)}) custom-call(bf16[128,2048]{1,0:T(8,128)(2,1)S(1)} %collective-permute-done.16.refs_0_, bf16[128,2048]{1,0:T(8,128)(2,1)S(1)} %collective-permute-done.21.refs_1_, bf16[1,2048]{1,0:T(2,128)(2,1)S(1)} %reshape.28.refs_2_, bf16[2048,768]{1,0:T(8,128)(2,1)S(1)} %copy-done, ...), custom_call_target="tpu_custom_call" | custom-call | flops 1 | bytes 1 | tf_op jit(solution)/shard_map/gate_up/pallas_call | solution.py:306
  75.3 0.6 collective-permute-start.22
  75.9 0.6 fusion.10
  76.5 0.4 collective-permute-done.22
  76.9 1.4 %fusion.1 = bf16[128,2048]{1,0:T(8,128)(2,1)} fusion(f32[128,2048]{1,0:T(8,128)S(1)} %fusion.10, bf16[128,768]{1,0:T(8,128)(2,1)S(1)} %collective-permute-done.22, bf16[768,2048]{1,0:T(8,128)(2,1)S(1)} %collective-permute-done.8), kind=kOutput, calls=%fused_computation.5 | convolution fusion | flops 403177472 | bytes 4915200 | tf_op jit(solution)/shard_map/dot_general | solution.py:26
  78.4 1.5 %collective-permute-start.23 = (bf16[128,2048]{1,0:T(8,128)(2,1)}, bf16[128,2048]{1,0:T(8,128)(2,1)S(1)}, u32[]{:S(2)}, u32[]{:S(2)}) collective-permute-start(bf16[128,2048]{1,0:T(8,128)(2,1)} %fusion.1), channel_id=1, source_target_pairs={{0,2},{1,3},{2,0},{3,1},{4,6},{5,7},{6,4},{7,5},{8,10},{9,11},{10,... | collective-permute-start | bytes 1572872 | tf_op jit(solution)/shard_map/ppermute | solution.py:491
  79.9 1.4 %collective-permute-start.25 = (bf16[256,2,256]{2,1,0:T(2,128)(2,1)}, bf16[256,2,256]{2,1,0:T(2,128)(2,1)S(1)}, u32[]{:S(2)}, u32[]{:S(2)}) collective-permute-start(bf16[256,2,256]{2,1,0:T(2,128)(2,1)} %collective-permute-done.18.refs_9_), channel_id=1, source_target_pairs={{0,4},{4,0},{8,12},{12,8},{16,20},{20,16},{24,28},{28,24},{1,5},{5... | collective-permute-start | bytes 786440 | tf_op jit(solution)/shard_map/ppermute | solution.py:497
  81.3 1.2 %collective-permute-start.26 = (bf16[256,2,256]{2,1,0:T(2,128)(2,1)S(1)}, bf16[256,2,256]{2,1,0:T(2,128)(2,1)S(1)}, u32[]{:S(2)}, u32[]{:S(2)}) collective-permute-start(bf16[256,2,256]{2,1,0:T(2,128)(2,1)S(1)} %collective-permute-done.19.refs_6_), channel_id=1, source_target_pairs={{0,8},{4,12},{8,16},{12,20},{16,24},{20,28},{24,0},{28,4},{1,9},{5... | collective-permute-start | bytes 786440 | tf_op jit(solution)/shard_map/ppermute | solution.py:494
  82.5 0.7 collective-permute-start.27
  83.2 8.7 %fill_pages.2.refs_10_ = bf16[512,16,2,256]{3,2,1,0:T(2,128)(2,1)} custom-call(s32[6]{0:T(128)} %stack.53.refs_0_, s32[32]{0:T(128)} %reshape.26.refs_1_, s32[32]{0:T(128)} %refs_2_.3, s32[512]{0:T(512)} %reshape.27.refs_3_, bf16[256,2,256]{2,1,0:T(2,128)(2,1)} %get-tuple-element.46.refs_4_, bf16[256,2,256]{2,1,0:T(2,128)(2,1)} %get-tuple-element.55.refs_5_, ...), custom_call_target="tpu_custom_call" | custom-call | flops 1 | bytes 1 | tf_op jit(solution)/shard_map/fill_pages/pallas_call | solution.py:436
  91.9 2.1 %collective-permute-done.27.refs_9_ = bf16[256,2,256]{2,1,0:T(2,128)(2,1)S(1)} collective-permute-done((bf16[256,2,256]{2,1,0:T(2,128)(2,1)}, bf16[256,2,256]{2,1,0:T(2,128)(2,1)S(1)}, u32[]{:S(2)}, u32[]{:S(2)}) %collective-permute-start.27) | collective-permute-done | bytes 262176 | tf_op jit(solution)/shard_map/ppermute | solution.py:497
  94.0 0.7 copy-done.13
  94.7 5.3 %fill_pages.3 = bf16[512,16,2,256]{3,2,1,0:T(2,128)(2,1)} custom-call(s32[4]{0:T(128)} %pad_add_fusion.1.refs_0_, s32[32]{0:T(128)} %reshape.26.refs_1_, s32[32]{0:T(128)} %refs_2_.3, s32[512]{0:T(512)} %reshape.27.refs_3_, bf16[256,2,256]{2,1,0:T(2,128)(2,1)} %copy-done.10, ...), custom_call_target="tpu_custom_call", output_to_operand_aliasing={{}: (10, {})} | custom-call | flops 1 | bytes 1 | tf_op jit(solution)/shard_map/fill_pages/pallas_call | solution.py:436
  100.0 1.0 add_convert_fusion
  (71 shorter events, 0.2 us)
Async XLA Ops:
  0.6 17.7 %collective-permute-start.3 = (bf16[512,2048]{1,0:T(8,128)(2,1)}, bf16[512,2048]{1,0:T(8,128)(2,1)S(1)}, u32[]{:S(2)}, u32[]{:S(2)}) collective-permute-start(bf16[512,2048]{1,0:T(8,128)(2,1)} %param.27), channel_id=1, source_target_pairs={{0,1},{1,0},{2,3},{3,2},{4,5},{5,4},{6,7},{7,6},{8,9},{9,8},{10,11... | collective-permute-start | bytes 6291464 | tf_op jit(solution)/shard_map/ppermute | solution.py:485
  1.1 17.2 %collective-permute-start = (bf16[128,2048]{1,0:T(8,128)(2,1)}, bf16[128,2048]{1,0:T(8,128)(2,1)S(1)}, u32[]{:S(2)}, u32[]{:S(2)}) collective-permute-start(bf16[128,2048]{1,0:T(8,128)(2,1)} %refs_0_.1), channel_id=1, source_target_pairs={{0,2},{1,3},{2,0},{3,1},{4,6},{5,7},{6,4},{7,5},{8,10},{9,11},{10,... | collective-permute-start | bytes 1572872 | tf_op jit(solution)/shard_map/ppermute | solution.py:491
  5.5 11.9 %copy-start.24 = (s32[8,512]{1,0:T(8,128)S(1)}, s32[8,512]{1,0:T(8,128)}, u32[]{:S(2)}) copy-start(s32[8,512]{1,0:T(8,128)} %ids.3) | copy-start | bytes 49156
  5.5 5.1 %collective-permute-start.2 = (bf16[64,2048]{1,0:T(8,128)(2,1)}, bf16[64,2048]{1,0:T(8,128)(2,1)S(1)}, u32[]{:S(2)}, u32[]{:S(2)}) collective-permute-start(bf16[64,2048]{1,0:T(8,128)(2,1)} %get-tuple-element.74), channel_id=1, source_target_pairs={{0,1},{1,0},{2,3},{3,2},{4,5},{5,4},{6,7},{7,6},{8,9},{9,8},{10,11... | collective-permute-start | bytes 786440 | tf_op jit(solution)/shard_map/ppermute | solution.py:485
  5.7 4.9 %collective-permute-start.1 = (bf16[64,2048]{1,0:T(8,128)(2,1)S(1)}, bf16[64,2048]{1,0:T(8,128)(2,1)S(1)}, u32[]{:S(2)}, u32[]{:S(2)}) collective-permute-start(bf16[64,2048]{1,0:T(8,128)(2,1)S(1)} %get-tuple-element.75), channel_id=1, source_target_pairs={{0,1},{1,0},{2,3},{3,2},{4,5},{5,4},{6,7},{7,6},{8,9},{9,8},{10,11... | collective-permute-start | bytes 786440 | tf_op jit(solution)/shard_map/ppermute | solution.py:485
  10.6 0.7 copy-start.14
  10.6 0.8 copy-start.15
  18.3 5.4 %copy-start.8 = (bf16[128,2048]{1,0:T(8,128)(2,1)}, bf16[128,2048]{1,0:T(8,128)(2,1)S(1)}, u32[]{:S(2)}) copy-start(bf16[128,2048]{1,0:T(8,128)(2,1)S(1)} %collective-permute-done.mine_far) | copy-start | bytes 1572868
  18.3 1.3 %copy-start.4 = (bf16[512,2048]{1,0:T(8,128)(2,1)}, bf16[512,2048]{1,0:T(8,128)(2,1)S(1)}, u32[]{:S(2)}) copy-start(bf16[512,2048]{1,0:T(8,128)(2,1)S(1)} %collective-permute-done.3) | copy-start | bytes 6291460
  18.3 2.1 %collective-permute-start.4 = (bf16[128,2048]{1,0:T(8,128)(2,1)S(1)}, bf16[128,2048]{1,0:T(8,128)(2,1)}, u32[]{:S(2)}, u32[]{:S(2)}) collective-permute-start(bf16[128,2048]{1,0:T(8,128)(2,1)S(1)} %collective-permute-done.mine_far), channel_id=1, source_target_pairs={{0,1},{1,0},{2,3},{3,2},{4,5},{5,4},{6,7},{7,6},{8,9},{9,8},{10,11... | collective-permute-start | bytes 1572872 | tf_op jit(solution)/shard_map/ppermute | solution.py:485
  20.4 16.5 %collective-permute-start.8 = (bf16[768,2048]{1,0:T(8,128)(2,1)}, bf16[768,2048]{1,0:T(8,128)(2,1)S(1)}, u32[]{:S(2)}, u32[]{:S(2)}) collective-permute-start(bf16[768,2048]{1,0:T(8,128)(2,1)} %param.31), channel_id=1, source_target_pairs={{0,1},{1,0},{2,3},{3,2},{4,5},{5,4},{6,7},{7,6},{8,9},{9,8},{10,11... | collective-permute-start | bytes 9437192 | tf_op jit(solution)/shard_map/ppermute | solution.py:485
  20.6 10.6 %collective-permute-start.6 = (bf16[256,2,256]{2,1,0:T(2,128)(2,1)}, bf16[256,2,256]{2,1,0:T(2,128)(2,1)S(1)}, u32[]{:S(2)}, u32[]{:S(2)}) collective-permute-start(bf16[256,2,256]{2,1,0:T(2,128)(2,1)} %get-tuple-element.46.refs_4_), channel_id=1, source_target_pairs={{0,4},{4,0},{8,12},{12,8},{16,20},{20,16},{24,28},{28,24},{1,5},{5... | collective-permute-start | bytes 786440 | tf_op jit(solution)/shard_map/ppermute | solution.py:497
  22.1 10.5 %collective-permute-start.5 = (bf16[256,2,256]{2,1,0:T(2,128)(2,1)}, bf16[256,2,256]{2,1,0:T(2,128)(2,1)}, u32[]{:S(2)}, u32[]{:S(2)}) collective-permute-start(bf16[256,2,256]{2,1,0:T(2,128)(2,1)} %get-tuple-element.46.refs_4_), channel_id=1, source_target_pairs={{0,8},{4,12},{8,16},{12,20},{16,24},{20,28},{24,0},{28,4},{1,9},{5... | collective-permute-start | bytes 786440 | tf_op jit(solution)/shard_map/ppermute | solution.py:494
  31.1 5.3 %copy-start.3 = (bf16[512,2048]{1,0:T(8,128)(2,1)S(1)}, bf16[512,2048]{1,0:T(8,128)(2,1)}, u32[]{:S(2)}) copy-start(bf16[512,2048]{1,0:T(8,128)(2,1)} %param.27) | copy-start | bytes 6291460
  31.2 5.3 %copy-start.23 = (bf16[256,512]{1,0:T(8,128)(2,1)S(1)}, bf16[256,512]{1,0:T(8,128)(2,1)}, u32[]{:S(2)}) copy-start(bf16[256,512]{1,0:T(8,128)(2,1)} %get-tuple-element.50) | copy-start | bytes 786436
  31.2 5.8 %copy-start.16 = (bf16[256,2,256]{2,1,0:T(2,128)(2,1)}, bf16[256,2,256]{2,1,0:T(2,128)(2,1)S(1)}, u32[]{:S(2)}) copy-start(bf16[256,2,256]{2,1,0:T(2,128)(2,1)S(1)} %collective-permute-done.6.refs_10_) | copy-start | bytes 786436
  32.6 5.2 %copy-start.17 = (bf16[256,2,256]{2,1,0:T(2,128)(2,1)S(1)}, bf16[256,2,256]{2,1,0:T(2,128)(2,1)}, u32[]{:S(2)}) copy-start(bf16[256,2,256]{2,1,0:T(2,128)(2,1)} %get-tuple-element.55.refs_5_) | copy-start | bytes 786436
  32.6 1.7 %collective-permute-start.7 = (bf16[256,512]{1,0:T(8,128)(2,1)}, bf16[256,512]{1,0:T(8,128)(2,1)S(1)}, u32[]{:S(2)}, u32[]{:S(2)}) collective-permute-start(bf16[256,512]{1,0:T(8,128)(2,1)} %get-tuple-element.47), channel_id=1, source_target_pairs={{0,1},{1,0},{2,3},{3,2},{4,5},{5,4},{6,7},{7,6},{8,9},{9,8},{10,11... | collective-permute-start | bytes 786440 | tf_op jit(solution)/shard_map/ppermute | solution.py:485
  36.4 5.4 %copy-start.5 = (bf16[512,2048]{1,0:T(8,128)(2,1)S(1)}, bf16[512,2048]{1,0:T(8,128)(2,1)}, u32[]{:S(2)}) copy-start(bf16[512,2048]{1,0:T(8,128)(2,1)} %copy-done.4) | copy-start | bytes 6291460
  37.0 17.0 %collective-permute-start.12 = (bf16[256,2,256]{2,1,0:T(2,128)(2,1)}, bf16[256,2,256]{2,1,0:T(2,128)(2,1)S(1)}, u32[]{:S(2)}, u32[]{:S(2)}) collective-permute-start(bf16[256,2,256]{2,1,0:T(2,128)(2,1)} %collective-permute-done.5.refs_6_), channel_id=1, source_target_pairs={{0,4},{4,0},{8,12},{12,8},{16,20},{20,16},{24,28},{28,24},{1,5},{5... | collective-permute-start | bytes 786440 | tf_op jit(solution)/shard_map/ppermute | solution.py:497
  37.5 16.4 %collective-permute-start.10 = (bf16[256,2,256]{2,1,0:T(2,128)(2,1)}, bf16[256,2,256]{2,1,0:T(2,128)(2,1)S(1)}, u32[]{:S(2)}, u32[]{:S(2)}) collective-permute-start(bf16[256,2,256]{2,1,0:T(2,128)(2,1)} %collective-permute-done.5.refs_6_), channel_id=1, source_target_pairs={{0,8},{4,12},{8,16},{12,20},{16,24},{20,28},{24,0},{28,4},{1,9},{5... | collective-permute-start | bytes 786440 | tf_op jit(solution)/shard_map/ppermute | solution.py:494
  37.8 15.9 %copy-start.6 = (bf16[128,2048]{1,0:T(8,128)(2,1)S(1)}, bf16[128,2048]{1,0:T(8,128)(2,1)}, u32[]{:S(2)}) copy-start(bf16[128,2048]{1,0:T(8,128)(2,1)} %refs_0_.1) | copy-start | bytes 1572868
  37.8 16.2 %collective-permute-start.13 = (bf16[256,2,256]{2,1,0:T(2,128)(2,1)S(1)}, bf16[256,2,256]{2,1,0:T(2,128)(2,1)S(1)}, u32[]{:S(2)}, u32[]{:S(2)}) collective-permute-start(bf16[256,2,256]{2,1,0:T(2,128)(2,1)S(1)} %copy-done.17), channel_id=1, source_target_pairs={{0,4},{4,0},{8,12},{12,8},{16,20},{20,16},{24,28},{28,24},{1,5},{5... | collective-permute-start | bytes 786440 | tf_op jit(solution)/shard_map/ppermute | solution.py:497
  39.3 14.7 %collective-permute-start.11 = (bf16[256,2,256]{2,1,0:T(2,128)(2,1)S(1)}, bf16[256,2,256]{2,1,0:T(2,128)(2,1)S(1)}, u32[]{:S(2)}, u32[]{:S(2)}) collective-permute-start(bf16[256,2,256]{2,1,0:T(2,128)(2,1)S(1)} %copy-done.17), channel_id=1, source_target_pairs={{0,8},{4,12},{8,16},{12,20},{16,24},{20,28},{24,0},{28,4},{1,9},{5... | collective-permute-start | bytes 786440 | tf_op jit(solution)/shard_map/ppermute | solution.py:494
  40.9 12.8 %collective-permute-start.9 = (bf16[128,2048]{1,0:T(8,128)(2,1)S(1)}, bf16[128,2048]{1,0:T(8,128)(2,1)S(1)}, u32[]{:S(2)}, u32[]{:S(2)}) collective-permute-start(bf16[128,2048]{1,0:T(8,128)(2,1)S(1)} %fusion), channel_id=1, source_target_pairs={{0,2},{1,3},{2,0},{3,1},{4,6},{5,7},{6,4},{7,5},{8,10},{9,11},{10,... | collective-permute-start | bytes 1572872 | tf_op jit(solution)/shard_map/ppermute | solution.py:491
  41.9 18.0 %copy-start.25 = (bf16[2048]{0:T(1024)(128)(2,1)S(1)}, bf16[2048]{0:T(1024)(128)(2,1)}, u32[]{:S(2)}) copy-start(bf16[2048]{0:T(1024)(128)(2,1)} %param.28) | copy-start | bytes 12292
  41.9 18.0 %copy-start = (bf16[2048,768]{1,0:T(8,128)(2,1)S(1)}, bf16[2048,768]{1,0:T(8,128)(2,1)}, u32[]{:S(2)}) copy-start(bf16[2048,768]{1,0:T(8,128)(2,1)} %refs_3_.3) | copy-start | bytes 9437188
  41.9 18.0 %copy-start.1 = (bf16[2048,768]{1,0:T(8,128)(2,1)S(1)}, bf16[2048,768]{1,0:T(8,128)(2,1)}, u32[]{:S(2)}) copy-start(bf16[2048,768]{1,0:T(8,128)(2,1)} %refs_4_.5) | copy-start | bytes 9437188
  53.9 5.9 %copy-start.18 = (bf16[256,2,256]{2,1,0:T(2,128)(2,1)}, bf16[256,2,256]{2,1,0:T(2,128)(2,1)S(1)}, u32[]{:S(2)}) copy-start(bf16[256,2,256]{2,1,0:T(2,128)(2,1)S(1)} %collective-permute-done.12.refs_12_) | copy-start | bytes 786436
  54.0 8.0 %copy-start.19 = (bf16[256,2,256]{2,1,0:T(2,128)(2,1)}, bf16[256,2,256]{2,1,0:T(2,128)(2,1)S(1)}, u32[]{:S(2)}) copy-start(bf16[256,2,256]{2,1,0:T(2,128)(2,1)S(1)} %collective-permute-done.10.refs_8_) | copy-start | bytes 786436
  54.0 5.9 %copy-start.20 = (bf16[256,2,256]{2,1,0:T(2,128)(2,1)}, bf16[256,2,256]{2,1,0:T(2,128)(2,1)S(1)}, u32[]{:S(2)}) copy-start(bf16[256,2,256]{2,1,0:T(2,128)(2,1)S(1)} %collective-permute-done.13.refs_11_) | copy-start | bytes 786436
  54.0 8.0 %copy-start.21 = (bf16[256,2,256]{2,1,0:T(2,128)(2,1)}, bf16[256,2,256]{2,1,0:T(2,128)(2,1)S(1)}, u32[]{:S(2)}) copy-start(bf16[256,2,256]{2,1,0:T(2,128)(2,1)S(1)} %collective-permute-done.11.refs_7_) | copy-start | bytes 786436
  54.0 3.7 %collective-permute-start.14 = (bf16[128,2048]{1,0:T(8,128)(2,1)S(1)}, bf16[128,2048]{1,0:T(8,128)(2,1)S(1)}, u32[]{:S(2)}, u32[]{:S(2)}) collective-permute-start(bf16[128,2048]{1,0:T(8,128)(2,1)S(1)} %add_convert_fusion.1.refs_0_), channel_id=1, source_target_pairs={{0,1},{1,0},{2,3},{3,2},{4,5},{5,4},{6,7},{7,6},{8,9},{9,8},{10,11... | collective-permute-start | bytes 1572872 | tf_op jit(solution)/shard_map/ppermute | solution.py:485
  54.1 14.3 %collective-permute-start.16 = (bf16[128,2048]{1,0:T(8,128)(2,1)S(1)}, bf16[128,2048]{1,0:T(8,128)(2,1)S(1)}, u32[]{:S(2)}, u32[]{:S(2)}) collective-permute-start(bf16[128,2048]{1,0:T(8,128)(2,1)S(1)} %add_convert_fusion.1.refs_0_), channel_id=1, source_target_pairs={{0,2},{1,3},{2,0},{3,1},{4,6},{5,7},{6,4},{7,5},{8,10},{9,11},{10,... | collective-permute-start | bytes 1572872 | tf_op jit(solution)/shard_map/ppermute | solution.py:491
  54.7 13.8 %collective-permute-start.19 = (bf16[256,2,256]{2,1,0:T(2,128)(2,1)S(1)}, bf16[256,2,256]{2,1,0:T(2,128)(2,1)S(1)}, u32[]{:S(2)}, u32[]{:S(2)}) collective-permute-start(bf16[256,2,256]{2,1,0:T(2,128)(2,1)S(1)} %collective-permute-done.10.refs_8_), channel_id=1, source_target_pairs={{0,4},{4,0},{8,12},{12,8},{16,20},{20,16},{24,28},{28,24},{1,5},{5... | collective-permute-start | bytes 786440 | tf_op jit(solution)/shard_map/ppermute | solution.py:497
  55.3 13.2 %collective-permute-start.17 = (bf16[256,2,256]{2,1,0:T(2,128)(2,1)S(1)}, bf16[256,2,256]{2,1,0:T(2,128)(2,1)S(1)}, u32[]{:S(2)}, u32[]{:S(2)}) collective-permute-start(bf16[256,2,256]{2,1,0:T(2,128)(2,1)S(1)} %collective-permute-done.10.refs_8_), channel_id=1, source_target_pairs={{0,8},{4,12},{8,16},{12,20},{16,24},{20,28},{24,0},{28,4},{1,9},{5... | collective-permute-start | bytes 786440 | tf_op jit(solution)/shard_map/ppermute | solution.py:494
  56.2 12.5 %collective-permute-start.20 = (bf16[256,2,256]{2,1,0:T(2,128)(2,1)S(1)}, bf16[256,2,256]{2,1,0:T(2,128)(2,1)S(1)}, u32[]{:S(2)}, u32[]{:S(2)}) collective-permute-start(bf16[256,2,256]{2,1,0:T(2,128)(2,1)S(1)} %collective-permute-done.11.refs_7_), channel_id=1, source_target_pairs={{0,4},{4,0},{8,12},{12,8},{16,20},{20,16},{24,28},{28,24},{1,5},{5... | collective-permute-start | bytes 786440 | tf_op jit(solution)/shard_map/ppermute | solution.py:497
  57.8 13.2 %collective-permute-start.18 = (bf16[256,2,256]{2,1,0:T(2,128)(2,1)S(1)}, bf16[256,2,256]{2,1,0:T(2,128)(2,1)}, u32[]{:S(2)}, u32[]{:S(2)}) collective-permute-start(bf16[256,2,256]{2,1,0:T(2,128)(2,1)S(1)} %collective-permute-done.11.refs_7_), channel_id=1, source_target_pairs={{0,8},{4,12},{8,16},{12,20},{16,24},{20,28},{24,0},{28,4},{1,9},{5... | collective-permute-start | bytes 786440 | tf_op jit(solution)/shard_map/ppermute | solution.py:494
  62.0 9.6 %copy-start.2 = (bf16[768,2048]{1,0:T(8,128)(2,1)S(1)}, bf16[768,2048]{1,0:T(8,128)(2,1)}, u32[]{:S(2)}) copy-start(bf16[768,2048]{1,0:T(8,128)(2,1)} %param.31) | copy-start | bytes 9437188
  68.4 2.5 %collective-permute-start.15 = (bf16[128,768]{1,0:T(8,128)(2,1)S(1)}, bf16[128,768]{1,0:T(8,128)(2,1)S(1)}, u32[]{:S(2)}, u32[]{:S(2)}) collective-permute-start(bf16[128,768]{1,0:T(8,128)(2,1)S(1)} %get-tuple-element.58), channel_id=1, source_target_pairs={{0,1},{1,0},{2,3},{3,2},{4,5},{5,4},{6,7},{7,6},{8,9},{9,8},{10,11... | collective-permute-start | bytes 589832 | tf_op jit(solution)/shard_map/ppermute | solution.py:485
  68.4 12.8 %copy-start.9 = (bf16[256,2,256]{2,1,0:T(2,128)(2,1)}, bf16[256,2,256]{2,1,0:T(2,128)(2,1)S(1)}, u32[]{:S(2)}) copy-start(bf16[256,2,256]{2,1,0:T(2,128)(2,1)S(1)} %collective-permute-done.19.refs_6_) | copy-start | bytes 786436
  68.5 0.7 copy-start.10
  69.2 4.0 %copy-start.22 = (bf16[256,2,256]{2,1,0:T(2,128)(2,1)}, bf16[256,2,256]{2,1,0:T(2,128)(2,1)S(1)}, u32[]{:S(2)}) copy-start(bf16[256,2,256]{2,1,0:T(2,128)(2,1)S(1)} %collective-permute-done.20.refs_13_) | copy-start | bytes 786436
  71.0 2.3 %collective-permute-start.21 = (bf16[128,2048]{1,0:T(8,128)(2,1)S(1)}, bf16[128,2048]{1,0:T(8,128)(2,1)S(1)}, u32[]{:S(2)}, u32[]{:S(2)}) collective-permute-start(bf16[128,2048]{1,0:T(8,128)(2,1)S(1)} %collective-permute-done.16.refs_0_), channel_id=1, source_target_pairs={{0,1},{1,0},{2,3},{3,2},{4,5},{5,4},{6,7},{7,6},{8,9},{9,8},{10,11... | collective-permute-start | bytes 1572872 | tf_op jit(solution)/shard_map/ppermute | solution.py:485
  71.0 11.5 %collective-permute-start.24 = (bf16[256,2,256]{2,1,0:T(2,128)(2,1)}, bf16[256,2,256]{2,1,0:T(2,128)(2,1)}, u32[]{:S(2)}, u32[]{:S(2)}) collective-permute-start(bf16[256,2,256]{2,1,0:T(2,128)(2,1)} %collective-permute-done.18.refs_9_), channel_id=1, source_target_pairs={{0,8},{4,12},{8,16},{12,20},{16,24},{20,28},{24,0},{28,4},{1,9},{5... | collective-permute-start | bytes 786440 | tf_op jit(solution)/shard_map/ppermute | solution.py:494
  75.3 1.6 %collective-permute-start.22 = (bf16[128,768]{1,0:T(8,128)(2,1)S(1)}, bf16[128,768]{1,0:T(8,128)(2,1)S(1)}, u32[]{:S(2)}, u32[]{:S(2)}) collective-permute-start(bf16[128,768]{1,0:T(8,128)(2,1)S(1)} %get-tuple-element.65), channel_id=1, source_target_pairs={{0,1},{1,0},{2,3},{3,2},{4,5},{5,4},{6,7},{7,6},{8,9},{9,8},{10,11... | collective-permute-start | bytes 589832 | tf_op jit(solution)/shard_map/ppermute | solution.py:485
  78.4 21.6 %collective-permute-start.23 = (bf16[128,2048]{1,0:T(8,128)(2,1)}, bf16[128,2048]{1,0:T(8,128)(2,1)S(1)}, u32[]{:S(2)}, u32[]{:S(2)}) collective-permute-start(bf16[128,2048]{1,0:T(8,128)(2,1)} %fusion.1), channel_id=1, source_target_pairs={{0,2},{1,3},{2,0},{3,1},{4,6},{5,7},{6,4},{7,5},{8,10},{9,11},{10,... | collective-permute-start | bytes 1572872 | tf_op jit(solution)/shard_map/ppermute | solution.py:491
  79.9 12.0 %collective-permute-start.25 = (bf16[256,2,256]{2,1,0:T(2,128)(2,1)}, bf16[256,2,256]{2,1,0:T(2,128)(2,1)S(1)}, u32[]{:S(2)}, u32[]{:S(2)}) collective-permute-start(bf16[256,2,256]{2,1,0:T(2,128)(2,1)} %collective-permute-done.18.refs_9_), channel_id=1, source_target_pairs={{0,4},{4,0},{8,12},{12,8},{16,20},{20,16},{24,28},{28,24},{1,5},{5... | collective-permute-start | bytes 786440 | tf_op jit(solution)/shard_map/ppermute | solution.py:497
  81.3 10.6 %collective-permute-start.26 = (bf16[256,2,256]{2,1,0:T(2,128)(2,1)S(1)}, bf16[256,2,256]{2,1,0:T(2,128)(2,1)S(1)}, u32[]{:S(2)}, u32[]{:S(2)}) collective-permute-start(bf16[256,2,256]{2,1,0:T(2,128)(2,1)S(1)} %collective-permute-done.19.refs_6_), channel_id=1, source_target_pairs={{0,8},{4,12},{8,16},{12,20},{16,24},{20,28},{24,0},{28,4},{1,9},{5... | collective-permute-start | bytes 786440 | tf_op jit(solution)/shard_map/ppermute | solution.py:494
  82.5 11.5 %collective-permute-start.27 = (bf16[256,2,256]{2,1,0:T(2,128)(2,1)}, bf16[256,2,256]{2,1,0:T(2,128)(2,1)S(1)}, u32[]{:S(2)}, u32[]{:S(2)}) collective-permute-start(bf16[256,2,256]{2,1,0:T(2,128)(2,1)} %collective-permute-done.24.refs_5_), channel_id=1, source_target_pairs={{0,4},{4,0},{8,12},{12,8},{16,20},{20,16},{24,28},{28,24},{1,5},{5... | collective-permute-start | bytes 786440 | tf_op jit(solution)/shard_map/ppermute | solution.py:497
  91.8 8.2 %copy-start.7 = (f32[128,2048]{1,0:T(8,128)S(1)}, f32[128,2048]{1,0:T(8,128)}, u32[]{:S(2)}) copy-start(f32[128,2048]{1,0:T(8,128)} %convolution_add_fusion.1) | copy-start | bytes 3145732
  91.9 2.1 %copy-start.12 = (bf16[256,2,256]{2,1,0:T(2,128)(2,1)}, bf16[256,2,256]{2,1,0:T(2,128)(2,1)S(1)}, u32[]{:S(2)}) copy-start(bf16[256,2,256]{2,1,0:T(2,128)(2,1)S(1)} %collective-permute-done.26.refs_8_) | copy-start | bytes 786436
  91.9 2.1 %copy-start.11 = (bf16[256,2,256]{2,1,0:T(2,128)(2,1)}, bf16[256,2,256]{2,1,0:T(2,128)(2,1)S(1)}, u32[]{:S(2)}) copy-start(bf16[256,2,256]{2,1,0:T(2,128)(2,1)S(1)} %collective-permute-done.25.refs_7_) | copy-start | bytes 786436
  94.0 0.7 copy-start.13

commit v5 on v4

--- a/solution.py
+++ b/solution.py
@@ -315,10 +315,21 @@
     )(first, *others, ln, wg, wu)
 
 
+class Part:
+    def __init__(self, packed, base):
+        self.packed, self.base = packed, base
+
+    def __getitem__(self, i):
+        return self.packed[self.base + i]
+
+
 def page_kernel(rows, requests, entries, blocks, *refs):
-    homes, bounds, prompts, table = refs[:4]
-    arrived = refs[4 : 4 + blocks]
+    homes, packed = refs[:2]
+    arrived = refs[2 : 2 + blocks]
     out, held, blank, where, load_sems, sems = refs[-6:]
+    bounds = Part(packed, 0)
+    prompts = Part(packed, (PROMPTS_DEV + 1) * where.shape[0])
+    table = Part(packed, prompts.base + requests)
     half = rows // 2
     side = homes[blocks // 2]
     loads = [
@@ -426,9 +437,8 @@
     lax.fori_loop(0, requests, finish, 0)
 
 
-def fill_pages(bounds, request_prompt, page_table, arrived, homes, rows, cache=None):
-    requests = request_prompt.shape[0]
-    entries = page_table.shape[0] // requests
+def fill_pages(packed, requests, entries, arrived, homes, rows, cache=None):
+    bounds = packed.shape[0] - requests * (1 + entries)
     row_shape, dtype = arrived[0].shape[1:], arrived[0].dtype
     blocks = len(arrived)
     given = [] if cache is None else [cache]
@@ -436,20 +446,20 @@
     return pl.pallas_call(
         functools.partial(page_kernel, rows, requests, entries, blocks),
         out_shape=jax.ShapeDtypeStruct((requests * entries, PAGE) + row_shape, dtype),
-        in_specs=[SMEM] * 4 + [FAR] * blocks + [ANY] * len(given),
+        in_specs=[SMEM] * 2 + [FAR] * blocks + [ANY] * len(given),
         out_specs=ANY,
         scratch_shapes=[
             pltpu.VMEM(held, dtype),
             pltpu.VMEM((PAGE,) + row_shape, dtype),
-            pltpu.SMEM((bounds.shape[0] // (PROMPTS_DEV + 1),), jnp.int32),
+            pltpu.SMEM((bounds // (PROMPTS_DEV + 1),), jnp.int32),
             pltpu.SemaphoreType.DMA((blocks,)),
             pltpu.SemaphoreType.DMA((requests,)),
         ],
-        input_output_aliases={4 + blocks: 0} if given else {},
+        input_output_aliases={2 + blocks: 0} if given else {},
         compiler_params=pltpu.CompilerParams(vmem_limit_bytes=MOST),
         cost_estimate=BRIEF,
         name="fill_pages",
-    )(homes, bounds, request_prompt, page_table, *arrived, *given)
+    )(homes, packed, *arrived, *given)
 
 
 def body(
@@ -512,9 +522,10 @@
     out_other = by_core(w_out)
     first_homes = jnp.stack(homes[: steps - 1] + homes[steps : 2 * steps - 2] + [side])
     last_homes = jnp.stack([homes[steps - 1], homes[-2], homes[-1], side])
-    page_table = page_table.reshape(-1)
-    here_x, bounds, first_homes, last_homes, page_table = lax.optimization_barrier(
-        (here_x, bounds, first_homes.astype(jnp.int32), last_homes.astype(jnp.int32), page_table)
+    requests, entries = page_table.shape
+    packed = jnp.concatenate([bounds, request_prompt, page_table.reshape(-1)])
+    here_x, packed, first_homes, last_homes = lax.optimization_barrier(
+        (here_x, packed, first_homes.astype(jnp.int32), last_homes.astype(jnp.int32))
     )
     here_x = ordered(here_x, out_other)
     here_xc = by_core(here_x)
@@ -522,7 +533,7 @@
     pairs_b, keep, send = second_half(
         place, segment_ids, here_x, here_xc, *tables, qa, ka, va
     )
-    send = ordered(send, line_a[1], flips_a[0])
+    send = ordered(ordered(send, line_a[1]), flips_a[0])
     got = by_core(send)
     part_b = (dot(keep[half // 2 :], w_out) + dot(got[half // 2 :], out_other)).astype(
         jnp.bfloat16
@@ -554,7 +565,8 @@
     advance(line_b, flips_b)
     keep_a, send_a = mlp(after, after_c, ln2, w_gate, w_up)
     after_x = ordered(after_x, keep_a)
-    after_x = ordered(after_x, line_a[-1], line_b[-1], flips_a[-1], flips_b[-1])
+    for arrival in (line_b[-1], line_a[-1], flips_b[-1], flips_a[-1]):
+        after_x = ordered(after_x, arrival)
     after_xc = by_core(after_x)
     got_a = by_core(send_a)
     down_a = dot(keep_a, w_down) + dot(got_a, down_other)
@@ -571,7 +583,7 @@
     got_b = by_core(send_b)
     down_b = (dot(keep_b, w_down) + dot(got_b, down_other)).astype(jnp.bfloat16)
     back = by_side(down_b)
-    tables = (ordered(bounds, down_b, line_b[-1]), request_prompt, page_table)
+    tables = (ordered(packed, down_b, line_b[-1]), requests, entries)
     blocks = list(zip(line_a, line_b))[: steps - 1] + list(zip(flips_a, flips_b))[: steps - 2]
     cache = fill_pages(
         *tables,
@@ -579,7 +591,7 @@
         first_homes,
         rows,
     )
-    flips_b.append(flipped(line_b[-1]))
+    flips_b.append(flipped(ordered(line_b[-1], flips_b[-1])))
     cache = fill_pages(
         *tables,
         [line_a[-1], line_b[-1], flips_a[-2], flips_b[-2], flips_a[-1], flips_b[-1]],

time: 102 us -> 101 us (level)
  starting transfers between devices: 22.7 us -> 24.2 us
  waiting for transfers between devices: 26.3 us -> 25 us
  local copies, waits for them, and re-layouts: 9.12 us -> 8.08 us
    ppermute x7, waiting for transfers between devices: 2.33 us -> 0.02 us  [flipped(): return lax.ppermute(a, 'req', to_pair)]
    ppermute x4, waiting for transfers between devices: 17.8 us -> 19.1 us  [by_side(): return lax.ppermute(a, 'mp', to_side)]
  transfers between devices with their start and end apart: 28 -> 28, of which waited for: 9 -> 8; matrix products, arithmetic and copies ran while one was open for 15% -> 15% of each run, Pallas kernels for 31% -> 31%
where the time goes in v5:
time: 101 us
  Pallas kernels  31.2 us (31%)
  waiting for transfers between devices  25 us (25%)
  starting transfers between devices  24.2 us (24%)
  local copies, waits for them, and re-layouts  8.08 us (8%)
  matrix products  7.76 us (8%)
  other arithmetic  3.32 us (3%)
  between operations  1.07 us (1%)
    ppermute x4, waiting for transfers between devices, by_side(): return lax.ppermute(a, 'mp', to_side)  19.1 us
    pallas_call x2, Pallas kernels, fill_pages(): pl.pallas_call(functools.partial(page_kernel, rows, requests, entries, bl...  13.7 us
    ppermute x7, starting transfers between devices, forward(): return lax.ppermute(a, 'req', to_next)  8.66 us
    ppermute x7, starting transfers between devices, flipped(): return lax.ppermute(a, 'req', to_pair)  8.2 us
    dot_general x8, matrix products, dot(): return jnp.dot(a, b, preferred_element_type=jnp.float32)  7.76 us
    pallas_call x1, Pallas kernels, second_half(): pl.pallas_call(second_kernel, out_shape=[jax.ShapeDtypeStruct((half, kv /...  7.43 us
    pallas_call x1, Pallas kernels, first_half(): pl.pallas_call(functools.partial(first_kernel, len(others)), out_shape=[j...  6.04 us
    ppermute x4, starting transfers between devices, by_side(): return lax.ppermute(a, 'mp', to_side)  5.21 us
  transfers between devices with their start and end apart: 28, of which 8 were waited for; matrix products, arithmetic and copies ran while one was open for 15% of the time, Pallas kernels for 31%

profile of v5, /device:TPU:0, one launch (start us, length us, event | category | flops | bytes accessed | tf_op | source)
XLA Modules:
  0.0 100.7 jit_solution(4342183312641636718)
XLA Ops:
  0.6 0.5 collective-permute-start.3
  1.1 2.6 %collective-permute-start = (bf16[128,2048]{1,0:T(8,128)(2,1)}, bf16[128,2048]{1,0:T(8,128)(2,1)S(1)}, u32[]{:S(2)}, u32[]{:S(2)}) collective-permute-start(bf16[128,2048]{1,0:T(8,128)(2,1)} %refs_0_.1), channel_id=1, source_target_pairs={{0,2},{1,3},{2,0},{3,1},{4,6},{5,7},{6,4},{7,5},{8,10},{9,11},{10,... | collective-permute-start | bytes 1572872 | tf_op jit(solution)/shard_map/ppermute | solution.py:501
  3.7 1.8 %fusion.8 = (bf16[64,2048]{1,0:T(8,128)(2,1)}, bf16[64,2048]{1,0:T(8,128)(2,1)S(1)}) fusion(bf16[128,2048]{1,0:T(8,128)(2,1)} %refs_0_.1), kind=kLoop, calls=%fused_computation.19 | loop fusion | bytes 1048576 | tf_op jit(solution)/shard_map/split | solution.py:498
  5.5 0.2 collective-permute-start.2
  5.7 0.3 collective-permute-start.1
  6.0 1.3 %reshape.23.refs_3_.ln = bf16[1,2048]{1,0:T(2,128)(2,1)} reshape(bf16[2048]{0:T(1024)(128)(2,1)} %param.21) | data formatting | bytes 8192 | tf_op jit(solution)/shard_map/reshape | solution.py:515
  7.3 0.8 copy.22
  8.1 0.1 reshape.27
  8.2 0.6 stack.53.refs_0_
  8.8 0.6 pad_add_fusion.1.place
  9.4 0.7 pad_add_fusion.2.refs_0_
  10.1 0.7 copy-done.12
  10.8 0.1 copy-done.13
  10.9 6.0 %first_half.1 = (bf16[256,512]{1,0:T(8,128)(2,1)}, bf16[256,256]{1,0:T(8,128)(2,1)}, bf16[256,256]{1,0:T(8,128)(2,1)}, bf16[256,2,256]{2,1,0:T(2,128)(2,1)}) custom-call(s32[3]{0:T(128)} %pad_add_fusion.1.place, s32[8,512]{1,0:T(8,128)} %ids.3, bf16[128,2048]{1,0:T(8,128)(2,1)} %refs_0_.1, bf16[64,2048]{1,0:T(8,128)(2,1)} %copy-done.13, ...), custom_call_target="tpu_custom_call" | custom-call | flops 1 | bytes 1 | tf_op jit(solution)/shard_map/first_half/pallas_call | solution.py:152
  16.9 0.1 convert_reduce_fusion
  17.1 0.1 copy.21
  17.2 0.1 reshape.26
  17.2 0.7 pad_add_fusion.refs_1_
  17.9 0.2 collective-permute-start.4
  18.2 1.1 %copy-done.4 = bf16[512,2048]{1,0:T(8,128)(2,1)} copy-done((bf16[512,2048]{1,0:T(8,128)(2,1)}, bf16[512,2048]{1,0:T(8,128)(2,1)S(1)}, u32[]{:S(2)}) %copy-start.4) | copy-done | bytes 2097176
  19.3 0.8 collective-permute-done.4.other_far
  20.1 0.2 collective-permute-start.8
  20.2 1.6 %collective-permute-start.5 = (bf16[256,2,256]{2,1,0:T(2,128)(2,1)}, bf16[256,2,256]{2,1,0:T(2,128)(2,1)S(1)}, u32[]{:S(2)}, u32[]{:S(2)}) collective-permute-start(bf16[256,2,256]{2,1,0:T(2,128)(2,1)} %get-tuple-element.50.refs_2_), channel_id=1, source_target_pairs={{0,8},{4,12},{8,16},{12,20},{16,24},{20,28},{24,0},{28,4},{1,9},{5... | collective-permute-start | bytes 786440 | tf_op jit(solution)/shard_map/ppermute | solution.py:504
  21.8 1.5 %collective-permute-start.6 = (bf16[256,2,256]{2,1,0:T(2,128)(2,1)}, bf16[256,2,256]{2,1,0:T(2,128)(2,1)}, u32[]{:S(2)}, u32[]{:S(2)}) collective-permute-start(bf16[256,2,256]{2,1,0:T(2,128)(2,1)} %get-tuple-element.50.refs_2_), channel_id=1, source_target_pairs={{0,4},{4,0},{8,12},{12,8},{16,20},{20,16},{24,28},{28,24},{1,5},{5... | collective-permute-start | bytes 786440 | tf_op jit(solution)/shard_map/ppermute | solution.py:507
  23.3 7.4 %second_half.1 = (bf16[256,2,256]{2,1,0:T(2,128)(2,1)}, bf16[256,512]{1,0:T(8,128)(2,1)}, bf16[256,512]{1,0:T(8,128)(2,1)}) custom-call(s32[3]{0:T(128)} %pad_add_fusion.1.place, s32[8,512]{1,0:T(8,128)} %ids.3, bf16[128,2048]{1,0:T(8,128)(2,1)} %copy-done.8, bf16[128,2048]{1,0:T(8,128)(2,1)} %collective-permute-done.4.other_far, ...), custom_call_target="tpu_custom_call" | custom-call | flops 1 | bytes 1 | tf_op jit(solution)/shard_map/second_half/pallas_call | solution.py:257
  30.8 0.1 collective-permute-done.5.refs_4_
  30.9 1.7 %collective-permute-done.7 = bf16[256,512]{1,0:T(8,128)(2,1)S(1)} collective-permute-done((bf16[256,512]{1,0:T(8,128)(2,1)}, bf16[256,512]{1,0:T(8,128)(2,1)S(1)}, u32[]{:S(2)}, u32[]{:S(2)}) %collective-permute-start.7) | collective-permute-done | bytes 262176 | tf_op jit(solution)/shard_map/ppermute | solution.py:495
  32.7 2.1 %fusion.2 = f32[128,2048]{1,0:T(8,128)S(1)} fusion(bf16[512,2048]{1,0:T(8,128)(2,1)} %copy-done.4, bf16[256,512]{1,0:T(8,128)(2,1)S(1)} %collective-permute-done.7), kind=kOutput, calls=%fused_computation.8 | convolution fusion | flops 268435456 | bytes 3276800 | tf_op jit(solution)/shard_map/dot_general | solution.py:26
  34.8 0.5 fusion
  35.2 1.6 %collective-permute-start.12 = (bf16[256,2,256]{2,1,0:T(2,128)(2,1)S(1)}, bf16[256,2,256]{2,1,0:T(2,128)(2,1)S(1)}, u32[]{:S(2)}, u32[]{:S(2)}) collective-permute-start(bf16[256,2,256]{2,1,0:T(2,128)(2,1)S(1)} %collective-permute-done.5.refs_4_), channel_id=1, source_target_pairs={{0,4},{4,0},{8,12},{12,8},{16,20},{20,16},{24,28},{28,24},{1,5},{5... | collective-permute-start | bytes 786440 | tf_op jit(solution)/shard_map/ppermute | solution.py:507
  36.8 1.1 %collective-permute-start.10 = (bf16[256,2,256]{2,1,0:T(2,128)(2,1)S(1)}, bf16[256,2,256]{2,1,0:T(2,128)(2,1)S(1)}, u32[]{:S(2)}, u32[]{:S(2)}) collective-permute-start(bf16[256,2,256]{2,1,0:T(2,128)(2,1)S(1)} %collective-permute-done.5.refs_4_), channel_id=1, source_target_pairs={{0,8},{4,12},{8,16},{12,20},{16,24},{20,28},{24,0},{28,4},{1,9},{5... | collective-permute-start | bytes 786440 | tf_op jit(solution)/shard_map/ppermute | solution.py:504
  37.9 1.0 collective-permute-start.13
  38.9 1.6 %collective-permute-start.11 = (bf16[256,2,256]{2,1,0:T(2,128)(2,1)S(1)}, bf16[256,2,256]{2,1,0:T(2,128)(2,1)S(1)}, u32[]{:S(2)}, u32[]{:S(2)}) collective-permute-start(bf16[256,2,256]{2,1,0:T(2,128)(2,1)S(1)} %copy-done.15), channel_id=1, source_target_pairs={{0,8},{4,12},{8,16},{12,20},{16,24},{20,28},{24,0},{28,4},{1,9},{5... | collective-permute-start | bytes 786440 | tf_op jit(solution)/shard_map/ppermute | solution.py:504
  40.5 0.5 collective-permute-start.9
  41.0 0.5 fusion.5
  41.5 0.5 convolution_add_fusion.2
  42.0 11.3 %collective-permute-done.9 = bf16[128,2048]{1,0:T(8,128)(2,1)S(1)} collective-permute-done((bf16[128,2048]{1,0:T(8,128)(2,1)S(1)}, bf16[128,2048]{1,0:T(8,128)(2,1)S(1)}, u32[]{:S(2)}, u32[]{:S(2)}) %collective-permute-start.9) | collective-permute-done | bytes 524320 | tf_op jit(solution)/shard_map/ppermute | solution.py:501
  53.3 0.2 add_convert_fusion.1.refs_0_
  53.7 0.6 collective-permute-start.16
  54.3 0.4 collective-permute-start.17
  54.7 1.5 %collective-permute-start.18 = (bf16[256,2,256]{2,1,0:T(2,128)(2,1)S(1)}, bf16[256,2,256]{2,1,0:T(2,128)(2,1)S(1)}, u32[]{:S(2)}, u32[]{:S(2)}) collective-permute-start(bf16[256,2,256]{2,1,0:T(2,128)(2,1)S(1)} %collective-permute-done.10.refs_6_), channel_id=1, source_target_pairs={{0,8},{4,12},{8,16},{12,20},{16,24},{20,28},{24,0},{28,4},{1,9},{5... | collective-permute-start | bytes 786440 | tf_op jit(solution)/shard_map/ppermute | solution.py:504
  56.1 1.5 %collective-permute-start.19 = (bf16[256,2,256]{2,1,0:T(2,128)(2,1)S(1)}, bf16[256,2,256]{2,1,0:T(2,128)(2,1)S(1)}, u32[]{:S(2)}, u32[]{:S(2)}) collective-permute-start(bf16[256,2,256]{2,1,0:T(2,128)(2,1)S(1)} %collective-permute-done.11.refs_5_), channel_id=1, source_target_pairs={{0,4},{4,0},{8,12},{12,8},{16,20},{20,16},{24,28},{28,24},{1,5},{5... | collective-permute-start | bytes 786440 | tf_op jit(solution)/shard_map/ppermute | solution.py:507
  57.7 0.5 collective-permute-start.20
  58.2 2.0 %gate_up.2 = (bf16[128,768]{1,0:T(8,128)(2,1)S(1)}, bf16[128,768]{1,0:T(8,128)(2,1)S(1)}) custom-call(bf16[128,2048]{1,0:T(8,128)(2,1)S(1)} %add_convert_fusion.1.refs_0_, bf16[128,2048]{1,0:T(8,128)(2,1)S(1)} %collective-permute-done.14.refs_1_, bf16[1,2048]{1,0:T(2,128)(2,1)S(1)} %reshape.28.refs_2_, bf16[2048,768]{1,0:T(8,128)(2,1)S(1)} %copy-done, ...), custom_call_target="tpu_custom_call" | custom-call | flops 1 | bytes 1 | tf_op jit(solution)/shard_map/gate_up/pallas_call | solution.py:306
  60.3 7.8 %collective-permute-done.16.refs_0_ = bf16[128,2048]{1,0:T(8,128)(2,1)S(1)} collective-permute-done((bf16[128,2048]{1,0:T(8,128)(2,1)S(1)}, bf16[128,2048]{1,0:T(8,128)(2,1)S(1)}, u32[]{:S(2)}, u32[]{:S(2)}) %collective-permute-start.16) | collective-permute-done | bytes 524320 | tf_op jit(solution)/shard_map/ppermute | solution.py:501
  68.0 2.0 %collective-permute-done.18.refs_2_ = bf16[256,2,256]{2,1,0:T(2,128)(2,1)S(1)} collective-permute-done((bf16[256,2,256]{2,1,0:T(2,128)(2,1)S(1)}, bf16[256,2,256]{2,1,0:T(2,128)(2,1)S(1)}, u32[]{:S(2)}, u32[]{:S(2)}) %collective-permute-start.18) | collective-permute-done | bytes 262176 | tf_op jit(solution)/shard_map/ppermute | solution.py:504
  70.1 1.1 %collective-permute-start.25 = (bf16[256,2,256]{2,1,0:T(2,128)(2,1)S(1)}, bf16[256,2,256]{2,1,0:T(2,128)(2,1)}, u32[]{:S(2)}, u32[]{:S(2)}) collective-permute-start(bf16[256,2,256]{2,1,0:T(2,128)(2,1)S(1)} %collective-permute-done.17.refs_7_), channel_id=1, source_target_pairs={{0,4},{4,0},{8,12},{12,8},{16,20},{20,16},{24,28},{28,24},{1,5},{5... | collective-permute-start | bytes 786440 | tf_op jit(solution)/shard_map/ppermute | solution.py:507
  71.2 1.0 %collective-permute-start.24 = (bf16[256,2,256]{2,1,0:T(2,128)(2,1)S(1)}, bf16[256,2,256]{2,1,0:T(2,128)(2,1)}, u32[]{:S(2)}, u32[]{:S(2)}) collective-permute-start(bf16[256,2,256]{2,1,0:T(2,128)(2,1)S(1)} %collective-permute-done.17.refs_7_), channel_id=1, source_target_pairs={{0,8},{4,12},{8,16},{12,20},{16,24},{20,28},{24,0},{28,4},{1,9},{5... | collective-permute-start | bytes 786440 | tf_op jit(solution)/shard_map/ppermute | solution.py:504
  72.2 0.6 fusion.9
  72.9 1.6 %convolution_add_fusion.1 = f32[128,2048]{1,0:T(8,128)} fusion(f32[128,2048]{1,0:T(8,128)S(1)} %fusion.9, bf16[128,768]{1,0:T(8,128)(2,1)S(1)} %get-tuple-element.62, bf16[768,2048]{1,0:T(8,128)(2,1)S(1)} %copy-done.2), kind=kOutput, calls=%fused_computation.1 | convolution fusion | flops 402915328 | bytes 5439488 | tf_op jit(solution)/shard_map/dot_general | solution.py:26
  74.5 2.1 %gate_up.3 = (bf16[128,768]{1,0:T(8,128)(2,1)S(1)}, bf16[128,768]{1,0:T(8,128)(2,1)S(1)}) custom-call(bf16[128,2048]{1,0:T(8,128)(2,1)S(1)} %collective-permute-done.16.refs_0_, bf16[128,2048]{1,0:T(8,128)(2,1)S(1)} %collective-permute-done.21.refs_1_, bf16[1,2048]{1,0:T(2,128)(2,1)S(1)} %reshape.28.refs_2_, bf16[2048,768]{1,0:T(8,128)(2,1)S(1)} %copy-done, ...), custom_call_target="tpu_custom_call" | custom-call | flops 1 | bytes 1 | tf_op jit(solution)/shard_map/gate_up/pallas_call | solution.py:306
  76.6 0.6 collective-permute-start.22
  77.1 0.6 fusion.10
  77.8 0.4 collective-permute-done.22
  78.2 1.4 %fusion.1 = bf16[128,2048]{1,0:T(8,128)(2,1)} fusion(f32[128,2048]{1,0:T(8,128)S(1)} %fusion.10, bf16[128,768]{1,0:T(8,128)(2,1)S(1)} %collective-permute-done.22, bf16[768,2048]{1,0:T(8,128)(2,1)S(1)} %collective-permute-done.8), kind=kOutput, calls=%fused_computation.5 | convolution fusion | flops 403177472 | bytes 4915200 | tf_op jit(solution)/shard_map/dot_general | solution.py:26
  79.6 1.5 %collective-permute-start.23 = (bf16[128,2048]{1,0:T(8,128)(2,1)}, bf16[128,2048]{1,0:T(8,128)(2,1)S(1)}, u32[]{:S(2)}, u32[]{:S(2)}) collective-permute-start(bf16[128,2048]{1,0:T(8,128)(2,1)} %fusion.1), channel_id=1, source_target_pairs={{0,2},{1,3},{2,0},{3,1},{4,6},{5,7},{6,4},{7,5},{8,10},{9,11},{10,... | collective-permute-start | bytes 1572872 | tf_op jit(solution)/shard_map/ppermute | solution.py:501
  81.2 1.6 %collective-permute-start.26 = (bf16[256,2,256]{2,1,0:T(2,128)(2,1)}, bf16[256,2,256]{2,1,0:T(2,128)(2,1)S(1)}, u32[]{:S(2)}, u32[]{:S(2)}) collective-permute-start(bf16[256,2,256]{2,1,0:T(2,128)(2,1)} %collective-permute-done.20.refs_4_), channel_id=1, source_target_pairs={{0,8},{4,12},{8,16},{12,20},{16,24},{20,28},{24,0},{28,4},{1,9},{5... | collective-permute-start | bytes 786440 | tf_op jit(solution)/shard_map/ppermute | solution.py:504
  82.7 1.0 collective-permute-start.27
  83.7 6.9 %fill_pages.2.refs_8_ = bf16[512,16,2,256]{3,2,1,0:T(2,128)(2,1)} custom-call(s32[6]{0:T(128)} %stack.53.refs_0_, s32[576]{0:T(1024)} %pad_add_fusion.refs_1_, bf16[256,2,256]{2,1,0:T(2,128)(2,1)} %get-tuple-element.50.refs_2_, bf16[256,2,256]{2,1,0:T(2,128)(2,1)} %get-tuple-element.60.refs_3_, bf16[256,2,256]{2,1,0:T(2,128)(2,1)} %copy-done.14, ...), custom_call_target="tpu_custom_call" | custom-call | flops 1 | bytes 1 | tf_op jit(solution)/shard_map/fill_pages/pallas_call | solution.py:446
  90.7 0.8 collective-permute-done.26.refs_6_
  91.5 0.7 copy-done.10
  92.2 0.7 copy-done.11
  92.9 6.8 %fill_pages.3 = bf16[512,16,2,256]{3,2,1,0:T(2,128)(2,1)} custom-call(s32[4]{0:T(128)} %pad_add_fusion.2.refs_0_, s32[576]{0:T(1024)} %pad_add_fusion.refs_1_, bf16[256,2,256]{2,1,0:T(2,128)(2,1)} %copy-done.9, bf16[256,2,256]{2,1,0:T(2,128)(2,1)} %collective-permute-done.24.refs_3_, ...), custom_call_target="tpu_custom_call", output_to_operand_aliasing={{}: (8, {})} | custom-call | flops 1 | bytes 1 | tf_op jit(solution)/shard_map/fill_pages/pallas_call | solution.py:446
  99.7 1.0 add_convert_fusion
  (72 shorter events, 0.3 us)
Async XLA Ops:
  0.6 17.3 %collective-permute-start.3 = (bf16[512,2048]{1,0:T(8,128)(2,1)}, bf16[512,2048]{1,0:T(8,128)(2,1)S(1)}, u32[]{:S(2)}, u32[]{:S(2)}) collective-permute-start(bf16[512,2048]{1,0:T(8,128)(2,1)} %param.27), channel_id=1, source_target_pairs={{0,1},{1,0},{2,3},{3,2},{4,5},{5,4},{6,7},{7,6},{8,9},{9,8},{10,11... | collective-permute-start | bytes 6291464 | tf_op jit(solution)/shard_map/ppermute | solution.py:495
  1.1 16.8 %collective-permute-start = (bf16[128,2048]{1,0:T(8,128)(2,1)}, bf16[128,2048]{1,0:T(8,128)(2,1)S(1)}, u32[]{:S(2)}, u32[]{:S(2)}) collective-permute-start(bf16[128,2048]{1,0:T(8,128)(2,1)} %refs_0_.1), channel_id=1, source_target_pairs={{0,2},{1,3},{2,0},{3,1},{4,6},{5,7},{6,4},{7,5},{8,10},{9,11},{10,... | collective-permute-start | bytes 1572872 | tf_op jit(solution)/shard_map/ppermute | solution.py:501
  5.5 11.4 %copy-start.23 = (s32[8,512]{1,0:T(8,128)S(1)}, s32[8,512]{1,0:T(8,128)}, u32[]{:S(2)}) copy-start(s32[8,512]{1,0:T(8,128)} %ids.3) | copy-start | bytes 49156
  5.5 11.8 %copy-start.25 = (s32[32]{0:T(128)S(1)}, s32[32]{0:T(128)}, u32[]{:S(2)}) copy-start(s32[32]{0:T(128)} %param.19) | copy-start | bytes 388
  5.5 4.6 %collective-permute-start.2 = (bf16[64,2048]{1,0:T(8,128)(2,1)}, bf16[64,2048]{1,0:T(8,128)(2,1)S(1)}, u32[]{:S(2)}, u32[]{:S(2)}) collective-permute-start(bf16[64,2048]{1,0:T(8,128)(2,1)} %get-tuple-element.82), channel_id=1, source_target_pairs={{0,1},{1,0},{2,3},{3,2},{4,5},{5,4},{6,7},{7,6},{8,9},{9,8},{10,11... | collective-permute-start | bytes 786440 | tf_op jit(solution)/shard_map/ppermute | solution.py:495
  5.7 4.4 %collective-permute-start.1 = (bf16[64,2048]{1,0:T(8,128)(2,1)S(1)}, bf16[64,2048]{1,0:T(8,128)(2,1)S(1)}, u32[]{:S(2)}, u32[]{:S(2)}) collective-permute-start(bf16[64,2048]{1,0:T(8,128)(2,1)S(1)} %get-tuple-element.83), channel_id=1, source_target_pairs={{0,1},{1,0},{2,3},{3,2},{4,5},{5,4},{6,7},{7,6},{8,9},{9,8},{10,11... | collective-permute-start | bytes 786440 | tf_op jit(solution)/shard_map/ppermute | solution.py:495
  10.1 0.7 copy-start.12
  10.1 0.8 copy-start.13
  17.9 5.4 %copy-start.8 = (bf16[128,2048]{1,0:T(8,128)(2,1)}, bf16[128,2048]{1,0:T(8,128)(2,1)S(1)}, u32[]{:S(2)}) copy-start(bf16[128,2048]{1,0:T(8,128)(2,1)S(1)} %collective-permute-done.mine_far) | copy-start | bytes 1572868
  17.9 1.3 %copy-start.4 = (bf16[512,2048]{1,0:T(8,128)(2,1)}, bf16[512,2048]{1,0:T(8,128)(2,1)S(1)}, u32[]{:S(2)}) copy-start(bf16[512,2048]{1,0:T(8,128)(2,1)S(1)} %collective-permute-done.3) | copy-start | bytes 6291460
  17.9 2.1 %collective-permute-start.4 = (bf16[128,2048]{1,0:T(8,128)(2,1)S(1)}, bf16[128,2048]{1,0:T(8,128)(2,1)}, u32[]{:S(2)}, u32[]{:S(2)}) collective-permute-start(bf16[128,2048]{1,0:T(8,128)(2,1)S(1)} %collective-permute-done.mine_far), channel_id=1, source_target_pairs={{0,1},{1,0},{2,3},{3,2},{4,5},{5,4},{6,7},{7,6},{8,9},{9,8},{10,11... | collective-permute-start | bytes 1572872 | tf_op jit(solution)/shard_map/ppermute | solution.py:495
  20.1 15.2 %collective-permute-start.8 = (bf16[768,2048]{1,0:T(8,128)(2,1)}, bf16[768,2048]{1,0:T(8,128)(2,1)S(1)}, u32[]{:S(2)}, u32[]{:S(2)}) collective-permute-start(bf16[768,2048]{1,0:T(8,128)(2,1)} %param.31), channel_id=1, source_target_pairs={{0,1},{1,0},{2,3},{3,2},{4,5},{5,4},{6,7},{7,6},{8,9},{9,8},{10,11... | collective-permute-start | bytes 9437192 | tf_op jit(solution)/shard_map/ppermute | solution.py:495
  20.2 10.6 %collective-permute-start.5 = (bf16[256,2,256]{2,1,0:T(2,128)(2,1)}, bf16[256,2,256]{2,1,0:T(2,128)(2,1)S(1)}, u32[]{:S(2)}, u32[]{:S(2)}) collective-permute-start(bf16[256,2,256]{2,1,0:T(2,128)(2,1)} %get-tuple-element.50.refs_2_), channel_id=1, source_target_pairs={{0,8},{4,12},{8,16},{12,20},{16,24},{20,28},{24,0},{28,4},{1,9},{5... | collective-permute-start | bytes 786440 | tf_op jit(solution)/shard_map/ppermute | solution.py:504
  21.8 9.1 %collective-permute-start.6 = (bf16[256,2,256]{2,1,0:T(2,128)(2,1)}, bf16[256,2,256]{2,1,0:T(2,128)(2,1)}, u32[]{:S(2)}, u32[]{:S(2)}) collective-permute-start(bf16[256,2,256]{2,1,0:T(2,128)(2,1)} %get-tuple-element.50.refs_2_), channel_id=1, source_target_pairs={{0,4},{4,0},{8,12},{12,8},{16,20},{20,16},{24,28},{28,24},{1,5},{5... | collective-permute-start | bytes 786440 | tf_op jit(solution)/shard_map/ppermute | solution.py:507
  30.8 4.0 %copy-start.3 = (bf16[512,2048]{1,0:T(8,128)(2,1)S(1)}, bf16[512,2048]{1,0:T(8,128)(2,1)}, u32[]{:S(2)}) copy-start(bf16[512,2048]{1,0:T(8,128)(2,1)} %param.27) | copy-start | bytes 6291460
  30.8 4.0 %copy-start.22 = (bf16[256,512]{1,0:T(8,128)(2,1)S(1)}, bf16[256,512]{1,0:T(8,128)(2,1)}, u32[]{:S(2)}) copy-start(bf16[256,512]{1,0:T(8,128)(2,1)} %get-tuple-element.55) | copy-start | bytes 786436
  30.8 6.0 %copy-start.14 = (bf16[256,2,256]{2,1,0:T(2,128)(2,1)}, bf16[256,2,256]{2,1,0:T(2,128)(2,1)S(1)}, u32[]{:S(2)}) copy-start(bf16[256,2,256]{2,1,0:T(2,128)(2,1)S(1)} %collective-permute-done.5.refs_4_) | copy-start | bytes 786436
  30.8 7.0 %copy-start.15 = (bf16[256,2,256]{2,1,0:T(2,128)(2,1)S(1)}, bf16[256,2,256]{2,1,0:T(2,128)(2,1)}, u32[]{:S(2)}) copy-start(bf16[256,2,256]{2,1,0:T(2,128)(2,1)} %get-tuple-element.60.refs_3_) | copy-start | bytes 786436
  30.9 1.8 %collective-permute-start.7 = (bf16[256,512]{1,0:T(8,128)(2,1)}, bf16[256,512]{1,0:T(8,128)(2,1)S(1)}, u32[]{:S(2)}, u32[]{:S(2)}) collective-permute-start(bf16[256,512]{1,0:T(8,128)(2,1)} %get-tuple-element.52), channel_id=1, source_target_pairs={{0,1},{1,0},{2,3},{3,2},{4,5},{5,4},{6,7},{7,6},{8,9},{9,8},{10,11... | collective-permute-start | bytes 786440 | tf_op jit(solution)/shard_map/ppermute | solution.py:495
  34.7 6.7 %copy-start.5 = (bf16[512,2048]{1,0:T(8,128)(2,1)S(1)}, bf16[512,2048]{1,0:T(8,128)(2,1)}, u32[]{:S(2)}) copy-start(bf16[512,2048]{1,0:T(8,128)(2,1)} %copy-done.4) | copy-start | bytes 6291460
  35.2 18.3 %collective-permute-start.12 = (bf16[256,2,256]{2,1,0:T(2,128)(2,1)S(1)}, bf16[256,2,256]{2,1,0:T(2,128)(2,1)S(1)}, u32[]{:S(2)}, u32[]{:S(2)}) collective-permute-start(bf16[256,2,256]{2,1,0:T(2,128)(2,1)S(1)} %collective-permute-done.5.refs_4_), channel_id=1, source_target_pairs={{0,4},{4,0},{8,12},{12,8},{16,20},{20,16},{24,28},{28,24},{1,5},{5... | collective-permute-start | bytes 786440 | tf_op jit(solution)/shard_map/ppermute | solution.py:507
  36.8 16.7 %collective-permute-start.10 = (bf16[256,2,256]{2,1,0:T(2,128)(2,1)S(1)}, bf16[256,2,256]{2,1,0:T(2,128)(2,1)S(1)}, u32[]{:S(2)}, u32[]{:S(2)}) collective-permute-start(bf16[256,2,256]{2,1,0:T(2,128)(2,1)S(1)} %collective-permute-done.5.refs_4_), channel_id=1, source_target_pairs={{0,8},{4,12},{8,16},{12,20},{16,24},{20,28},{24,0},{28,4},{1,9},{5... | collective-permute-start | bytes 786440 | tf_op jit(solution)/shard_map/ppermute | solution.py:504
  37.9 15.4 %copy-start.6 = (bf16[128,2048]{1,0:T(8,128)(2,1)S(1)}, bf16[128,2048]{1,0:T(8,128)(2,1)}, u32[]{:S(2)}) copy-start(bf16[128,2048]{1,0:T(8,128)(2,1)} %refs_0_.1) | copy-start | bytes 1572868
  37.9 15.7 %collective-permute-start.13 = (bf16[256,2,256]{2,1,0:T(2,128)(2,1)S(1)}, bf16[256,2,256]{2,1,0:T(2,128)(2,1)S(1)}, u32[]{:S(2)}, u32[]{:S(2)}) collective-permute-start(bf16[256,2,256]{2,1,0:T(2,128)(2,1)S(1)} %copy-done.15), channel_id=1, source_target_pairs={{0,4},{4,0},{8,12},{12,8},{16,20},{20,16},{24,28},{28,24},{1,5},{5... | collective-permute-start | bytes 786440 | tf_op jit(solution)/shard_map/ppermute | solution.py:507
  38.9 14.7 %collective-permute-start.11 = (bf16[256,2,256]{2,1,0:T(2,128)(2,1)S(1)}, bf16[256,2,256]{2,1,0:T(2,128)(2,1)S(1)}, u32[]{:S(2)}, u32[]{:S(2)}) collective-permute-start(bf16[256,2,256]{2,1,0:T(2,128)(2,1)S(1)} %copy-done.15), channel_id=1, source_target_pairs={{0,8},{4,12},{8,16},{12,20},{16,24},{20,28},{24,0},{28,4},{1,9},{5... | collective-permute-start | bytes 786440 | tf_op jit(solution)/shard_map/ppermute | solution.py:504
  40.5 12.8 %collective-permute-start.9 = (bf16[128,2048]{1,0:T(8,128)(2,1)S(1)}, bf16[128,2048]{1,0:T(8,128)(2,1)S(1)}, u32[]{:S(2)}, u32[]{:S(2)}) collective-permute-start(bf16[128,2048]{1,0:T(8,128)(2,1)S(1)} %fusion), channel_id=1, source_target_pairs={{0,2},{1,3},{2,0},{3,1},{4,6},{5,7},{6,4},{7,5},{8,10},{9,11},{10,... | collective-permute-start | bytes 1572872 | tf_op jit(solution)/shard_map/ppermute | solution.py:501
  41.5 16.7 %copy-start.24 = (bf16[2048]{0:T(1024)(128)(2,1)S(1)}, bf16[2048]{0:T(1024)(128)(2,1)}, u32[]{:S(2)}) copy-start(bf16[2048]{0:T(1024)(128)(2,1)} %param.28) | copy-start | bytes 12292
  41.5 16.7 %copy-start = (bf16[2048,768]{1,0:T(8,128)(2,1)S(1)}, bf16[2048,768]{1,0:T(8,128)(2,1)}, u32[]{:S(2)}) copy-start(bf16[2048,768]{1,0:T(8,128)(2,1)} %refs_3_.3) | copy-start | bytes 9437188
  41.5 16.7 %copy-start.1 = (bf16[2048,768]{1,0:T(8,128)(2,1)S(1)}, bf16[2048,768]{1,0:T(8,128)(2,1)}, u32[]{:S(2)}) copy-start(bf16[2048,768]{1,0:T(8,128)(2,1)} %refs_4_.5) | copy-start | bytes 9437188
  53.5 4.6 %copy-start.16 = (bf16[256,2,256]{2,1,0:T(2,128)(2,1)}, bf16[256,2,256]{2,1,0:T(2,128)(2,1)S(1)}, u32[]{:S(2)}) copy-start(bf16[256,2,256]{2,1,0:T(2,128)(2,1)S(1)} %collective-permute-done.12.refs_10_) | copy-start | bytes 786436
  53.6 6.7 %copy-start.17 = (bf16[256,2,256]{2,1,0:T(2,128)(2,1)}, bf16[256,2,256]{2,1,0:T(2,128)(2,1)S(1)}, u32[]{:S(2)}) copy-start(bf16[256,2,256]{2,1,0:T(2,128)(2,1)S(1)} %collective-permute-done.10.refs_6_) | copy-start | bytes 786436
  53.6 4.6 %copy-start.18 = (bf16[256,2,256]{2,1,0:T(2,128)(2,1)}, bf16[256,2,256]{2,1,0:T(2,128)(2,1)S(1)}, u32[]{:S(2)}) copy-start(bf16[256,2,256]{2,1,0:T(2,128)(2,1)S(1)} %collective-permute-done.13.refs_9_) | copy-start | bytes 786436
  53.6 6.6 %copy-start.19 = (bf16[256,2,256]{2,1,0:T(2,128)(2,1)}, bf16[256,2,256]{2,1,0:T(2,128)(2,1)S(1)}, u32[]{:S(2)}) copy-start(bf16[256,2,256]{2,1,0:T(2,128)(2,1)S(1)} %collective-permute-done.11.refs_5_) | copy-start | bytes 786436
  53.6 4.0 %collective-permute-start.14 = (bf16[128,2048]{1,0:T(8,128)(2,1)S(1)}, bf16[128,2048]{1,0:T(8,128)(2,1)S(1)}, u32[]{:S(2)}, u32[]{:S(2)}) collective-permute-start(bf16[128,2048]{1,0:T(8,128)(2,1)S(1)} %add_convert_fusion.1.refs_0_), channel_id=1, source_target_pairs={{0,1},{1,0},{2,3},{3,2},{4,5},{5,4},{6,7},{7,6},{8,9},{9,8},{10,11... | collective-permute-start | bytes 1572872 | tf_op jit(solution)/shard_map/ppermute | solution.py:495
  53.7 14.3 %collective-permute-start.16 = (bf16[128,2048]{1,0:T(8,128)(2,1)S(1)}, bf16[128,2048]{1,0:T(8,128)(2,1)S(1)}, u32[]{:S(2)}, u32[]{:S(2)}) collective-permute-start(bf16[128,2048]{1,0:T(8,128)(2,1)S(1)} %add_convert_fusion.1.refs_0_), channel_id=1, source_target_pairs={{0,2},{1,3},{2,0},{3,1},{4,6},{5,7},{6,4},{7,5},{8,10},{9,11},{10,... | collective-permute-start | bytes 1572872 | tf_op jit(solution)/shard_map/ppermute | solution.py:501
  54.3 13.7 %collective-permute-start.17 = (bf16[256,2,256]{2,1,0:T(2,128)(2,1)S(1)}, bf16[256,2,256]{2,1,0:T(2,128)(2,1)S(1)}, u32[]{:S(2)}, u32[]{:S(2)}) collective-permute-start(bf16[256,2,256]{2,1,0:T(2,128)(2,1)S(1)} %collective-permute-done.11.refs_5_), channel_id=1, source_target_pairs={{0,8},{4,12},{8,16},{12,20},{16,24},{20,28},{24,0},{28,4},{1,9},{5... | collective-permute-start | bytes 786440 | tf_op jit(solution)/shard_map/ppermute | solution.py:504
  54.7 15.4 %collective-permute-start.18 = (bf16[256,2,256]{2,1,0:T(2,128)(2,1)S(1)}, bf16[256,2,256]{2,1,0:T(2,128)(2,1)S(1)}, u32[]{:S(2)}, u32[]{:S(2)}) collective-permute-start(bf16[256,2,256]{2,1,0:T(2,128)(2,1)S(1)} %collective-permute-done.10.refs_6_), channel_id=1, source_target_pairs={{0,8},{4,12},{8,16},{12,20},{16,24},{20,28},{24,0},{28,4},{1,9},{5... | collective-permute-start | bytes 786440 | tf_op jit(solution)/shard_map/ppermute | solution.py:504
  56.1 14.0 %collective-permute-start.19 = (bf16[256,2,256]{2,1,0:T(2,128)(2,1)S(1)}, bf16[256,2,256]{2,1,0:T(2,128)(2,1)S(1)}, u32[]{:S(2)}, u32[]{:S(2)}) collective-permute-start(bf16[256,2,256]{2,1,0:T(2,128)(2,1)S(1)} %collective-permute-done.11.refs_5_), channel_id=1, source_target_pairs={{0,4},{4,0},{8,12},{12,8},{16,20},{20,16},{24,28},{28,24},{1,5},{5... | collective-permute-start | bytes 786440 | tf_op jit(solution)/shard_map/ppermute | solution.py:507
  57.7 12.4 %collective-permute-start.20 = (bf16[256,2,256]{2,1,0:T(2,128)(2,1)S(1)}, bf16[256,2,256]{2,1,0:T(2,128)(2,1)}, u32[]{:S(2)}, u32[]{:S(2)}) collective-permute-start(bf16[256,2,256]{2,1,0:T(2,128)(2,1)S(1)} %collective-permute-done.10.refs_6_), channel_id=1, source_target_pairs={{0,4},{4,0},{8,12},{12,8},{16,20},{20,16},{24,28},{28,24},{1,5},{5... | collective-permute-start | bytes 786440 | tf_op jit(solution)/shard_map/ppermute | solution.py:507
  60.3 12.6 %copy-start.2 = (bf16[768,2048]{1,0:T(8,128)(2,1)S(1)}, bf16[768,2048]{1,0:T(8,128)(2,1)}, u32[]{:S(2)}) copy-start(bf16[768,2048]{1,0:T(8,128)(2,1)} %param.31) | copy-start | bytes 9437188
  68.0 4.2 %collective-permute-start.15 = (bf16[128,768]{1,0:T(8,128)(2,1)S(1)}, bf16[128,768]{1,0:T(8,128)(2,1)S(1)}, u32[]{:S(2)}, u32[]{:S(2)}) collective-permute-start(bf16[128,768]{1,0:T(8,128)(2,1)S(1)} %get-tuple-element.63), channel_id=1, source_target_pairs={{0,1},{1,0},{2,3},{3,2},{4,5},{5,4},{6,7},{7,6},{8,9},{9,8},{10,11... | collective-permute-start | bytes 589832 | tf_op jit(solution)/shard_map/ppermute | solution.py:495
  68.0 6.5 %copy-start.20 = (bf16[256,2,256]{2,1,0:T(2,128)(2,1)}, bf16[256,2,256]{2,1,0:T(2,128)(2,1)S(1)}, u32[]{:S(2)}) copy-start(bf16[256,2,256]{2,1,0:T(2,128)(2,1)S(1)} %collective-permute-done.17.refs_7_) | copy-start | bytes 786436
  70.1 4.4 %copy-start.9 = (bf16[256,2,256]{2,1,0:T(2,128)(2,1)}, bf16[256,2,256]{2,1,0:T(2,128)(2,1)S(1)}, u32[]{:S(2)}) copy-start(bf16[256,2,256]{2,1,0:T(2,128)(2,1)S(1)} %collective-permute-done.18.refs_2_) | copy-start | bytes 786436
  70.1 4.4 %copy-start.21 = (bf16[256,2,256]{2,1,0:T(2,128)(2,1)}, bf16[256,2,256]{2,1,0:T(2,128)(2,1)S(1)}, u32[]{:S(2)}) copy-start(bf16[256,2,256]{2,1,0:T(2,128)(2,1)S(1)} %collective-permute-done.19.refs_11_) | copy-start | bytes 786436
  70.1 12.6 %collective-permute-start.25 = (bf16[256,2,256]{2,1,0:T(2,128)(2,1)S(1)}, bf16[256,2,256]{2,1,0:T(2,128)(2,1)}, u32[]{:S(2)}, u32[]{:S(2)}) collective-permute-start(bf16[256,2,256]{2,1,0:T(2,128)(2,1)S(1)} %collective-permute-done.17.refs_7_), channel_id=1, source_target_pairs={{0,4},{4,0},{8,12},{12,8},{16,20},{20,16},{24,28},{28,24},{1,5},{5... | collective-permute-start | bytes 786440 | tf_op jit(solution)/shard_map/ppermute | solution.py:507
  71.2 11.5 %collective-permute-start.24 = (bf16[256,2,256]{2,1,0:T(2,128)(2,1)S(1)}, bf16[256,2,256]{2,1,0:T(2,128)(2,1)}, u32[]{:S(2)}, u32[]{:S(2)}) collective-permute-start(bf16[256,2,256]{2,1,0:T(2,128)(2,1)S(1)} %collective-permute-done.17.refs_7_), channel_id=1, source_target_pairs={{0,8},{4,12},{8,16},{12,20},{16,24},{20,28},{24,0},{28,4},{1,9},{5... | collective-permute-start | bytes 786440 | tf_op jit(solution)/shard_map/ppermute | solution.py:504
  72.2 2.3 %collective-permute-start.21 = (bf16[128,2048]{1,0:T(8,128)(2,1)S(1)}, bf16[128,2048]{1,0:T(8,128)(2,1)S(1)}, u32[]{:S(2)}, u32[]{:S(2)}) collective-permute-start(bf16[128,2048]{1,0:T(8,128)(2,1)S(1)} %collective-permute-done.16.refs_0_), channel_id=1, source_target_pairs={{0,1},{1,0},{2,3},{3,2},{4,5},{5,4},{6,7},{7,6},{8,9},{9,8},{10,11... | collective-permute-start | bytes 1572872 | tf_op jit(solution)/shard_map/ppermute | solution.py:495
  76.6 1.6 %collective-permute-start.22 = (bf16[128,768]{1,0:T(8,128)(2,1)S(1)}, bf16[128,768]{1,0:T(8,128)(2,1)S(1)}, u32[]{:S(2)}, u32[]{:S(2)}) collective-permute-start(bf16[128,768]{1,0:T(8,128)(2,1)S(1)} %get-tuple-element.73), channel_id=1, source_target_pairs={{0,1},{1,0},{2,3},{3,2},{4,5},{5,4},{6,7},{7,6},{8,9},{9,8},{10,11... | collective-permute-start | bytes 589832 | tf_op jit(solution)/shard_map/ppermute | solution.py:495
  79.6 20.0 %collective-permute-start.23 = (bf16[128,2048]{1,0:T(8,128)(2,1)}, bf16[128,2048]{1,0:T(8,128)(2,1)S(1)}, u32[]{:S(2)}, u32[]{:S(2)}) collective-permute-start(bf16[128,2048]{1,0:T(8,128)(2,1)} %fusion.1), channel_id=1, source_target_pairs={{0,2},{1,3},{2,0},{3,1},{4,6},{5,7},{6,4},{7,5},{8,10},{9,11},{10,... | collective-permute-start | bytes 1572872 | tf_op jit(solution)/shard_map/ppermute | solution.py:501
  81.2 10.3 %collective-permute-start.26 = (bf16[256,2,256]{2,1,0:T(2,128)(2,1)}, bf16[256,2,256]{2,1,0:T(2,128)(2,1)S(1)}, u32[]{:S(2)}, u32[]{:S(2)}) collective-permute-start(bf16[256,2,256]{2,1,0:T(2,128)(2,1)} %collective-permute-done.20.refs_4_), channel_id=1, source_target_pairs={{0,8},{4,12},{8,16},{12,20},{16,24},{20,28},{24,0},{28,4},{1,9},{5... | collective-permute-start | bytes 786440 | tf_op jit(solution)/shard_map/ppermute | solution.py:504
  82.7 8.7 %collective-permute-start.27 = (bf16[256,2,256]{2,1,0:T(2,128)(2,1)}, bf16[256,2,256]{2,1,0:T(2,128)(2,1)S(1)}, u32[]{:S(2)}, u32[]{:S(2)}) collective-permute-start(bf16[256,2,256]{2,1,0:T(2,128)(2,1)} %collective-permute-done.24.refs_3_), channel_id=1, source_target_pairs={{0,4},{4,0},{8,12},{12,8},{16,20},{20,16},{24,28},{28,24},{1,5},{5... | collective-permute-start | bytes 786440 | tf_op jit(solution)/shard_map/ppermute | solution.py:507
  90.7 9.0 %copy-start.7 = (f32[128,2048]{1,0:T(8,128)S(1)}, f32[128,2048]{1,0:T(8,128)}, u32[]{:S(2)}) copy-start(f32[128,2048]{1,0:T(8,128)} %convolution_add_fusion.1) | copy-start | bytes 3145732
  91.5 0.7 copy-start.10
  92.2 0.7 copy-start.11

commit v6 on v5

--- a/solution.py
+++ b/solution.py
@@ -18,7 +18,7 @@
 VMEM = pl.BlockSpec(memory_space=pltpu.VMEM)
 ANY = pl.BlockSpec(memory_space=pl.ANY)
 FAR = pl.BlockSpec(memory_space=pltpu.HBM)
-MOST = 63 * 10**6
+MOST = 61 * 10**6
 BRIEF = pl.CostEstimate(flops=1, bytes_accessed=1, transcendentals=0)
 
 

time: 101 us -> 98 us (0.970)
  matrix products: 7.76 us -> 4.25 us
  waiting for transfers between devices: 25 us -> 26.1 us
    dot_general x8, matrix products: 7.76 us -> 4.25 us  [dot(): return jnp.dot(a, b, preferred_element_type=jnp.float32)]
    ppermute x10, waiting for transfers between devices: 2.97 us -> 4.87 us  [by_core(): return lax.ppermute(a, 'mp', to_core)]
  transfers between devices with their start and end apart: 28 -> 28, of which waited for: 8 -> 8; matrix products, arithmetic and copies ran while one was open for 15% -> 11% of each run, Pallas kernels for 31% -> 32%
where the time goes in v6:
time: 98 us; the launch traced here: 97.5 us
  Pallas kernels  31.2 us (32%)
  waiting for transfers between devices  26.1 us (27%)
  starting transfers between devices  23.9 us (24%)
  local copies, waits for them, and re-layouts  7.81 us (8%)
  matrix products  4.25 us (4%)
  other arithmetic  3.19 us (3%)
  between operations  1.09 us (1%)
    ppermute x4, waiting for transfers between devices, by_side(): return lax.ppermute(a, 'mp', to_side)  19.1 us
    pallas_call x2, Pallas kernels, fill_pages(): pl.pallas_call(functools.partial(page_kernel, rows, requests, entries, bl...  13.7 us
    ppermute x7, starting transfers between devices, forward(): return lax.ppermute(a, 'req', to_next)  8.53 us
    ppermute x7, starting transfers between devices, flipped(): return lax.ppermute(a, 'req', to_pair)  8.28 us
    pallas_call x1, Pallas kernels, second_half(): pl.pallas_call(second_kernel, out_shape=[jax.ShapeDtypeStruct((half, kv /...  7.42 us
    pallas_call x1, Pallas kernels, first_half(): pl.pallas_call(functools.partial(first_kernel, len(others)), out_shape=[j...  6.03 us
    ppermute x4, starting transfers between devices, by_side(): return lax.ppermute(a, 'mp', to_side)  5.27 us
    ppermute x10, waiting for transfers between devices, by_core(): return lax.ppermute(a, 'mp', to_core)  4.87 us
  transfers between devices with their start and end apart: 28, of which 8 were waited for; matrix products, arithmetic and copies ran while one was open for 11% of the time, Pallas kernels for 32%

profile of v6, /device:TPU:0, one launch (start us, length us, event | category | flops | bytes accessed | tf_op | source)
XLA Modules:
  0.0 97.5 jit_solution(13248106219798307804)
XLA Ops:
  0.6 0.5 collective-permute-start.3
  1.1 2.6 %collective-permute-start = (bf16[128,2048]{1,0:T(8,128)(2,1)}, bf16[128,2048]{1,0:T(8,128)(2,1)S(1)}, u32[]{:S(2)}, u32[]{:S(2)}) collective-permute-start(bf16[128,2048]{1,0:T(8,128)(2,1)} %refs_0_.1), channel_id=1, source_target_pairs={{0,2},{1,3},{2,0},{3,1},{4,6},{5,7},{6,4},{7,5},{8,10},{9,11},{10,... | collective-permute-start | bytes 1572872 | tf_op jit(solution)/shard_map/ppermute | solution.py:501
  3.7 1.8 %fusion.8 = (bf16[64,2048]{1,0:T(8,128)(2,1)}, bf16[64,2048]{1,0:T(8,128)(2,1)S(1)}) fusion(bf16[128,2048]{1,0:T(8,128)(2,1)} %refs_0_.1), kind=kLoop, calls=%fused_computation.19 | loop fusion | bytes 1048576 | tf_op jit(solution)/shard_map/split | solution.py:498
  5.5 0.2 collective-permute-start.2
  5.7 0.3 collective-permute-start.1
  6.0 1.3 %reshape.23.refs_3_.ln = bf16[1,2048]{1,0:T(2,128)(2,1)} reshape(bf16[2048]{0:T(1024)(128)(2,1)} %param.21) | data formatting | bytes 8192 | tf_op jit(solution)/shard_map/reshape | solution.py:515
  7.3 0.8 copy.22
  8.1 0.1 reshape.27
  8.2 0.7 stack.53.refs_0_
  8.8 0.6 pad_add_fusion.1.place
  9.4 0.6 pad_add_fusion.2.refs_0_
  10.0 0.7 copy-done.12
  10.7 0.1 copy-done.13
  10.8 6.0 %first_half.1 = (bf16[256,512]{1,0:T(8,128)(2,1)}, bf16[256,256]{1,0:T(8,128)(2,1)}, bf16[256,256]{1,0:T(8,128)(2,1)}, bf16[256,2,256]{2,1,0:T(2,128)(2,1)}) custom-call(s32[3]{0:T(128)} %pad_add_fusion.1.place, s32[8,512]{1,0:T(8,128)} %ids.3, bf16[128,2048]{1,0:T(8,128)(2,1)} %refs_0_.1, bf16[64,2048]{1,0:T(8,128)(2,1)} %copy-done.13, ...), custom_call_target="tpu_custom_call" | custom-call | flops 1 | bytes 1 | tf_op jit(solution)/shard_map/first_half/pallas_call | solution.py:152
  16.8 0.1 convert_reduce_fusion
  17.0 0.1 copy.21
  17.1 0.1 reshape.26
  17.2 0.7 pad_add_fusion.refs_1_
  17.9 0.2 collective-permute-start.4
  18.1 1.7 %collective-permute-done.4.other_far = bf16[128,2048]{1,0:T(8,128)(2,1)S(1)} collective-permute-done((bf16[128,2048]{1,0:T(8,128)(2,1)S(1)}, bf16[128,2048]{1,0:T(8,128)(2,1)S(1)}, u32[]{:S(2)}, u32[]{:S(2)}) %collective-permute-start.4) | collective-permute-done | bytes 524320 | tf_op jit(solution)/shard_map/ppermute | solution.py:495
  19.8 0.8 copy-done.6
  20.6 0.2 collective-permute-start.8
  20.8 1.6 %collective-permute-start.5 = (bf16[256,2,256]{2,1,0:T(2,128)(2,1)}, bf16[256,2,256]{2,1,0:T(2,128)(2,1)S(1)}, u32[]{:S(2)}, u32[]{:S(2)}) collective-permute-start(bf16[256,2,256]{2,1,0:T(2,128)(2,1)} %get-tuple-element.50.refs_2_), channel_id=1, source_target_pairs={{0,8},{4,12},{8,16},{12,20},{16,24},{20,28},{24,0},{28,4},{1,9},{5... | collective-permute-start | bytes 786440 | tf_op jit(solution)/shard_map/ppermute | solution.py:504
  22.4 1.5 %collective-permute-start.6 = (bf16[256,2,256]{2,1,0:T(2,128)(2,1)}, bf16[256,2,256]{2,1,0:T(2,128)(2,1)}, u32[]{:S(2)}, u32[]{:S(2)}) collective-permute-start(bf16[256,2,256]{2,1,0:T(2,128)(2,1)} %get-tuple-element.50.refs_2_), channel_id=1, source_target_pairs={{0,4},{4,0},{8,12},{12,8},{16,20},{20,16},{24,28},{28,24},{1,5},{5... | collective-permute-start | bytes 786440 | tf_op jit(solution)/shard_map/ppermute | solution.py:507
  23.9 7.4 %second_half.1 = (bf16[256,2,256]{2,1,0:T(2,128)(2,1)}, bf16[256,512]{1,0:T(8,128)(2,1)}, bf16[256,512]{1,0:T(8,128)(2,1)}) custom-call(s32[3]{0:T(128)} %pad_add_fusion.1.place, s32[8,512]{1,0:T(8,128)} %ids.3, bf16[128,2048]{1,0:T(8,128)(2,1)} %copy-done.5, bf16[128,2048]{1,0:T(8,128)(2,1)} %copy-done.6, bf16[1,2048]{1,0:T(2,128)(2,1)} %reshape.23.refs_3_.ln, ...), custom_call_target="tpu_custom_call" | custom-call | flops 1 | bytes 1 | tf_op jit(solution)/shard_map/second_half/pallas_call | solution.py:257
  31.3 0.1 collective-permute-done.5.refs_4_
  31.5 1.7 %collective-permute-done.7 = bf16[256,512]{1,0:T(8,128)(2,1)S(1)} collective-permute-done((bf16[256,512]{1,0:T(8,128)(2,1)}, bf16[256,512]{1,0:T(8,128)(2,1)S(1)}, u32[]{:S(2)}, u32[]{:S(2)}) %collective-permute-start.7) | collective-permute-done | bytes 262176 | tf_op jit(solution)/shard_map/ppermute | solution.py:495
  33.2 0.5 fusion.2
  33.7 0.4 fusion
  34.2 1.6 %collective-permute-start.12 = (bf16[256,2,256]{2,1,0:T(2,128)(2,1)S(1)}, bf16[256,2,256]{2,1,0:T(2,128)(2,1)S(1)}, u32[]{:S(2)}, u32[]{:S(2)}) collective-permute-start(bf16[256,2,256]{2,1,0:T(2,128)(2,1)S(1)} %collective-permute-done.5.refs_4_), channel_id=1, source_target_pairs={{0,4},{4,0},{8,12},{12,8},{16,20},{20,16},{24,28},{28,24},{1,5},{5... | collective-permute-start | bytes 786440 | tf_op jit(solution)/shard_map/ppermute | solution.py:507
  35.8 1.0 %collective-permute-start.10 = (bf16[256,2,256]{2,1,0:T(2,128)(2,1)S(1)}, bf16[256,2,256]{2,1,0:T(2,128)(2,1)S(1)}, u32[]{:S(2)}, u32[]{:S(2)}) collective-permute-start(bf16[256,2,256]{2,1,0:T(2,128)(2,1)S(1)} %collective-permute-done.5.refs_4_), channel_id=1, source_target_pairs={{0,8},{4,12},{8,16},{12,20},{16,24},{20,28},{24,0},{28,4},{1,9},{5... | collective-permute-start | bytes 786440 | tf_op jit(solution)/shard_map/ppermute | solution.py:504
  36.8 1.0 %collective-permute-start.13 = (bf16[256,2,256]{2,1,0:T(2,128)(2,1)S(1)}, bf16[256,2,256]{2,1,0:T(2,128)(2,1)S(1)}, u32[]{:S(2)}, u32[]{:S(2)}) collective-permute-start(bf16[256,2,256]{2,1,0:T(2,128)(2,1)S(1)} %copy-done.15), channel_id=1, source_target_pairs={{0,4},{4,0},{8,12},{12,8},{16,20},{20,16},{24,28},{28,24},{1,5},{5... | collective-permute-start | bytes 786440 | tf_op jit(solution)/shard_map/ppermute | solution.py:507
  37.8 1.6 %collective-permute-start.11 = (bf16[256,2,256]{2,1,0:T(2,128)(2,1)S(1)}, bf16[256,2,256]{2,1,0:T(2,128)(2,1)S(1)}, u32[]{:S(2)}, u32[]{:S(2)}) collective-permute-start(bf16[256,2,256]{2,1,0:T(2,128)(2,1)S(1)} %copy-done.15), channel_id=1, source_target_pairs={{0,8},{4,12},{8,16},{12,20},{16,24},{20,28},{24,0},{28,4},{1,9},{5... | collective-permute-start | bytes 786440 | tf_op jit(solution)/shard_map/ppermute | solution.py:504
  39.4 0.5 collective-permute-start.9
  39.9 0.4 fusion.5
  40.4 0.5 convolution_add_fusion.2
  40.9 11.3 %collective-permute-done.9 = bf16[128,2048]{1,0:T(8,128)(2,1)S(1)} collective-permute-done((bf16[128,2048]{1,0:T(8,128)(2,1)S(1)}, bf16[128,2048]{1,0:T(8,128)(2,1)S(1)}, u32[]{:S(2)}, u32[]{:S(2)}) %collective-permute-start.9) | collective-permute-done | bytes 524320 | tf_op jit(solution)/shard_map/ppermute | solution.py:501
  52.2 0.2 add_convert_fusion.1.refs_0_
  52.6 0.6 collective-permute-start.16
  53.2 0.4 collective-permute-start.17
  53.6 1.5 %collective-permute-start.18 = (bf16[256,2,256]{2,1,0:T(2,128)(2,1)S(1)}, bf16[256,2,256]{2,1,0:T(2,128)(2,1)S(1)}, u32[]{:S(2)}, u32[]{:S(2)}) collective-permute-start(bf16[256,2,256]{2,1,0:T(2,128)(2,1)S(1)} %collective-permute-done.10.refs_6_), channel_id=1, source_target_pairs={{0,8},{4,12},{8,16},{12,20},{16,24},{20,28},{24,0},{28,4},{1,9},{5... | collective-permute-start | bytes 786440 | tf_op jit(solution)/shard_map/ppermute | solution.py:504
  55.1 1.5 %collective-permute-start.19 = (bf16[256,2,256]{2,1,0:T(2,128)(2,1)S(1)}, bf16[256,2,256]{2,1,0:T(2,128)(2,1)S(1)}, u32[]{:S(2)}, u32[]{:S(2)}) collective-permute-start(bf16[256,2,256]{2,1,0:T(2,128)(2,1)S(1)} %collective-permute-done.11.refs_5_), channel_id=1, source_target_pairs={{0,4},{4,0},{8,12},{12,8},{16,20},{20,16},{24,28},{28,24},{1,5},{5... | collective-permute-start | bytes 786440 | tf_op jit(solution)/shard_map/ppermute | solution.py:507
  56.6 0.5 collective-permute-start.20
  57.1 2.0 %gate_up.2 = (bf16[128,768]{1,0:T(8,128)(2,1)S(1)}, bf16[128,768]{1,0:T(8,128)(2,1)S(1)}) custom-call(bf16[128,2048]{1,0:T(8,128)(2,1)S(1)} %add_convert_fusion.1.refs_0_, bf16[128,2048]{1,0:T(8,128)(2,1)S(1)} %collective-permute-done.14.refs_1_, bf16[1,2048]{1,0:T(2,128)(2,1)S(1)} %reshape.28.refs_2_, bf16[2048,768]{1,0:T(8,128)(2,1)S(1)} %copy-done, ...), custom_call_target="tpu_custom_call" | custom-call | flops 1 | bytes 1 | tf_op jit(solution)/shard_map/gate_up/pallas_call | solution.py:306
  59.2 7.7 %collective-permute-done.16.refs_0_ = bf16[128,2048]{1,0:T(8,128)(2,1)S(1)} collective-permute-done((bf16[128,2048]{1,0:T(8,128)(2,1)S(1)}, bf16[128,2048]{1,0:T(8,128)(2,1)S(1)}, u32[]{:S(2)}, u32[]{:S(2)}) %collective-permute-start.16) | collective-permute-done | bytes 524320 | tf_op jit(solution)/shard_map/ppermute | solution.py:501
  67.0 2.0 %collective-permute-done.18.refs_2_ = bf16[256,2,256]{2,1,0:T(2,128)(2,1)S(1)} collective-permute-done((bf16[256,2,256]{2,1,0:T(2,128)(2,1)S(1)}, bf16[256,2,256]{2,1,0:T(2,128)(2,1)S(1)}, u32[]{:S(2)}, u32[]{:S(2)}) %collective-permute-start.18) | collective-permute-done | bytes 262176 | tf_op jit(solution)/shard_map/ppermute | solution.py:504
  69.0 1.1 %collective-permute-start.25 = (bf16[256,2,256]{2,1,0:T(2,128)(2,1)S(1)}, bf16[256,2,256]{2,1,0:T(2,128)(2,1)S(1)}, u32[]{:S(2)}, u32[]{:S(2)}) collective-permute-start(bf16[256,2,256]{2,1,0:T(2,128)(2,1)S(1)} %collective-permute-done.17.refs_7_), channel_id=1, source_target_pairs={{0,4},{4,0},{8,12},{12,8},{16,20},{20,16},{24,28},{28,24},{1,5},{5... | collective-permute-start | bytes 786440 | tf_op jit(solution)/shard_map/ppermute | solution.py:507
  70.1 0.9 collective-permute-start.24
  71.1 0.6 fusion.9
  71.7 0.6 convolution_add_fusion.1
  72.3 0.7 collective-permute-done.21.refs_1_
  73.0 2.0 %gate_up.3 = (bf16[128,768]{1,0:T(8,128)(2,1)S(1)}, bf16[128,768]{1,0:T(8,128)(2,1)S(1)}) custom-call(bf16[128,2048]{1,0:T(8,128)(2,1)S(1)} %collective-permute-done.16.refs_0_, bf16[128,2048]{1,0:T(8,128)(2,1)S(1)} %collective-permute-done.21.refs_1_, bf16[1,2048]{1,0:T(2,128)(2,1)S(1)} %reshape.28.refs_2_, bf16[2048,768]{1,0:T(8,128)(2,1)S(1)} %copy-done, ...), custom_call_target="tpu_custom_call" | custom-call | flops 1 | bytes 1 | tf_op jit(solution)/shard_map/gate_up/pallas_call | solution.py:306
  75.0 0.2 collective-permute-start.22
  75.2 0.6 fusion.10
  75.8 0.7 collective-permute-done.22
  76.5 0.6 fusion.1
  77.2 1.6 %collective-permute-start.23 = (bf16[128,2048]{1,0:T(8,128)(2,1)S(1)}, bf16[128,2048]{1,0:T(8,128)(2,1)S(1)}, u32[]{:S(2)}, u32[]{:S(2)}) collective-permute-start(bf16[128,2048]{1,0:T(8,128)(2,1)S(1)} %fusion.1), channel_id=1, source_target_pairs={{0,2},{1,3},{2,0},{3,1},{4,6},{5,7},{6,4},{7,5},{8,10},{9,11},{10,... | collective-permute-start | bytes 1572872 | tf_op jit(solution)/shard_map/ppermute | solution.py:501
  78.7 1.6 %collective-permute-start.26 = (bf16[256,2,256]{2,1,0:T(2,128)(2,1)S(1)}, bf16[256,2,256]{2,1,0:T(2,128)(2,1)S(1)}, u32[]{:S(2)}, u32[]{:S(2)}) collective-permute-start(bf16[256,2,256]{2,1,0:T(2,128)(2,1)S(1)} %collective-permute-done.20.refs_4_), channel_id=1, source_target_pairs={{0,8},{4,12},{8,16},{12,20},{16,24},{20,28},{24,0},{28,4},{1,9},{5... | collective-permute-start | bytes 786440 | tf_op jit(solution)/shard_map/ppermute | solution.py:504
  80.3 1.1 %collective-permute-start.27 = (bf16[256,2,256]{2,1,0:T(2,128)(2,1)}, bf16[256,2,256]{2,1,0:T(2,128)(2,1)S(1)}, u32[]{:S(2)}, u32[]{:S(2)}) collective-permute-start(bf16[256,2,256]{2,1,0:T(2,128)(2,1)} %collective-permute-done.24.refs_3_), channel_id=1, source_target_pairs={{0,4},{4,0},{8,12},{12,8},{16,20},{20,16},{24,28},{28,24},{1,5},{5... | collective-permute-start | bytes 786440 | tf_op jit(solution)/shard_map/ppermute | solution.py:507
  81.4 7.6 %fill_pages.2.refs_8_ = bf16[512,16,2,256]{3,2,1,0:T(2,128)(2,1)} custom-call(s32[6]{0:T(128)} %stack.53.refs_0_, s32[576]{0:T(1024)} %pad_add_fusion.refs_1_, bf16[256,2,256]{2,1,0:T(2,128)(2,1)} %get-tuple-element.50.refs_2_, bf16[256,2,256]{2,1,0:T(2,128)(2,1)} %get-tuple-element.60.refs_3_, bf16[256,2,256]{2,1,0:T(2,128)(2,1)} %copy-done.14, ...), custom_call_target="tpu_custom_call" | custom-call | flops 1 | bytes 1 | tf_op jit(solution)/shard_map/fill_pages/pallas_call | solution.py:446
  89.0 0.7 copy-done.10
  89.7 0.7 copy-done.11
  90.4 6.1 %fill_pages.3 = bf16[512,16,2,256]{3,2,1,0:T(2,128)(2,1)} custom-call(s32[4]{0:T(128)} %pad_add_fusion.2.refs_0_, s32[576]{0:T(1024)} %pad_add_fusion.refs_1_, bf16[256,2,256]{2,1,0:T(2,128)(2,1)} %copy-done.7, bf16[256,2,256]{2,1,0:T(2,128)(2,1)} %collective-permute-done.24.refs_3_, bf16[256,2,256]{2,1,0:T(2,128)(2,1)} %copy-done.8, ...), custom_call_target="tpu_custom_call", output_to_operand_aliasing={{}: (8, {})} | custom-call | flops 1 | bytes 1 | tf_op jit(solution)/shard_map/fill_pages/pallas_call | solution.py:446
  96.5 1.0 %add_convert_fusion = bf16[128,2048]{1,0:T(8,128)(2,1)} fusion(bf16[128,2048]{1,0:T(8,128)(2,1)S(1)} %collective-permute-done.23, f32[128,2048]{1,0:T(8,128)S(1)} %convolution_add_fusion.1, bf16[128,2048]{1,0:T(8,128)(2,1)S(1)} %add_convert_fusion.1.refs_0_), kind=kLoop, calls=%fused_computation.6 | loop fusion | flops 1310720 | bytes 2621440 | tf_op jit(solution)/shard_map/convert_element_type | solution.py:602
  (72 shorter events, 0.3 us)
Async XLA Ops:
  0.6 17.2 %collective-permute-start.3 = (bf16[512,2048]{1,0:T(8,128)(2,1)}, bf16[512,2048]{1,0:T(8,128)(2,1)S(1)}, u32[]{:S(2)}, u32[]{:S(2)}) collective-permute-start(bf16[512,2048]{1,0:T(8,128)(2,1)} %param.27), channel_id=1, source_target_pairs={{0,1},{1,0},{2,3},{3,2},{4,5},{5,4},{6,7},{7,6},{8,9},{9,8},{10,11... | collective-permute-start | bytes 6291464 | tf_op jit(solution)/shard_map/ppermute | solution.py:495
  1.1 16.7 %collective-permute-start = (bf16[128,2048]{1,0:T(8,128)(2,1)}, bf16[128,2048]{1,0:T(8,128)(2,1)S(1)}, u32[]{:S(2)}, u32[]{:S(2)}) collective-permute-start(bf16[128,2048]{1,0:T(8,128)(2,1)} %refs_0_.1), channel_id=1, source_target_pairs={{0,2},{1,3},{2,0},{3,1},{4,6},{5,7},{6,4},{7,5},{8,10},{9,11},{10,... | collective-permute-start | bytes 1572872 | tf_op jit(solution)/shard_map/ppermute | solution.py:501
  5.5 11.4 %copy-start.23 = (s32[8,512]{1,0:T(8,128)S(1)}, s32[8,512]{1,0:T(8,128)}, u32[]{:S(2)}) copy-start(s32[8,512]{1,0:T(8,128)} %ids.3) | copy-start | bytes 49156
  5.5 11.7 %copy-start.25 = (s32[32]{0:T(128)S(1)}, s32[32]{0:T(128)}, u32[]{:S(2)}) copy-start(s32[32]{0:T(128)} %param.19) | copy-start | bytes 388
  5.5 4.5 %collective-permute-start.2 = (bf16[64,2048]{1,0:T(8,128)(2,1)}, bf16[64,2048]{1,0:T(8,128)(2,1)S(1)}, u32[]{:S(2)}, u32[]{:S(2)}) collective-permute-start(bf16[64,2048]{1,0:T(8,128)(2,1)} %get-tuple-element.82), channel_id=1, source_target_pairs={{0,1},{1,0},{2,3},{3,2},{4,5},{5,4},{6,7},{7,6},{8,9},{9,8},{10,11... | collective-permute-start | bytes 786440 | tf_op jit(solution)/shard_map/ppermute | solution.py:495
  5.7 4.4 %collective-permute-start.1 = (bf16[64,2048]{1,0:T(8,128)(2,1)S(1)}, bf16[64,2048]{1,0:T(8,128)(2,1)S(1)}, u32[]{:S(2)}, u32[]{:S(2)}) collective-permute-start(bf16[64,2048]{1,0:T(8,128)(2,1)S(1)} %get-tuple-element.83), channel_id=1, source_target_pairs={{0,1},{1,0},{2,3},{3,2},{4,5},{5,4},{6,7},{7,6},{8,9},{9,8},{10,11... | collective-permute-start | bytes 786440 | tf_op jit(solution)/shard_map/ppermute | solution.py:495
  10.0 0.7 copy-start.12
  10.0 0.8 copy-start.13
  17.8 6.0 %copy-start.5 = (bf16[128,2048]{1,0:T(8,128)(2,1)}, bf16[128,2048]{1,0:T(8,128)(2,1)S(1)}, u32[]{:S(2)}) copy-start(bf16[128,2048]{1,0:T(8,128)(2,1)S(1)} %collective-permute-done.mine_far) | copy-start | bytes 1572868
  17.9 2.0 %collective-permute-start.4 = (bf16[128,2048]{1,0:T(8,128)(2,1)S(1)}, bf16[128,2048]{1,0:T(8,128)(2,1)S(1)}, u32[]{:S(2)}, u32[]{:S(2)}) collective-permute-start(bf16[128,2048]{1,0:T(8,128)(2,1)S(1)} %collective-permute-done.mine_far), channel_id=1, source_target_pairs={{0,1},{1,0},{2,3},{3,2},{4,5},{5,4},{6,7},{7,6},{8,9},{9,8},{10,11... | collective-permute-start | bytes 1572872 | tf_op jit(solution)/shard_map/ppermute | solution.py:495
  19.8 0.8 copy-start.6
  20.6 13.6 %collective-permute-start.8 = (bf16[768,2048]{1,0:T(8,128)(2,1)}, bf16[768,2048]{1,0:T(8,128)(2,1)S(1)}, u32[]{:S(2)}, u32[]{:S(2)}) collective-permute-start(bf16[768,2048]{1,0:T(8,128)(2,1)} %param.31), channel_id=1, source_target_pairs={{0,1},{1,0},{2,3},{3,2},{4,5},{5,4},{6,7},{7,6},{8,9},{9,8},{10,11... | collective-permute-start | bytes 9437192 | tf_op jit(solution)/shard_map/ppermute | solution.py:495
  20.8 10.6 %collective-permute-start.5 = (bf16[256,2,256]{2,1,0:T(2,128)(2,1)}, bf16[256,2,256]{2,1,0:T(2,128)(2,1)S(1)}, u32[]{:S(2)}, u32[]{:S(2)}) collective-permute-start(bf16[256,2,256]{2,1,0:T(2,128)(2,1)} %get-tuple-element.50.refs_2_), channel_id=1, source_target_pairs={{0,8},{4,12},{8,16},{12,20},{16,24},{20,28},{24,0},{28,4},{1,9},{5... | collective-permute-start | bytes 786440 | tf_op jit(solution)/shard_map/ppermute | solution.py:504
  22.4 9.1 %collective-permute-start.6 = (bf16[256,2,256]{2,1,0:T(2,128)(2,1)}, bf16[256,2,256]{2,1,0:T(2,128)(2,1)}, u32[]{:S(2)}, u32[]{:S(2)}) collective-permute-start(bf16[256,2,256]{2,1,0:T(2,128)(2,1)} %get-tuple-element.50.refs_2_), channel_id=1, source_target_pairs={{0,4},{4,0},{8,12},{12,8},{16,20},{20,16},{24,28},{28,24},{1,5},{5... | collective-permute-start | bytes 786440 | tf_op jit(solution)/shard_map/ppermute | solution.py:507
  31.3 2.4 %copy-start.3 = (bf16[512,2048]{1,0:T(8,128)(2,1)S(1)}, bf16[512,2048]{1,0:T(8,128)(2,1)}, u32[]{:S(2)}) copy-start(bf16[512,2048]{1,0:T(8,128)(2,1)} %param.27) | copy-start | bytes 6291460
  31.3 2.4 %copy-start.22 = (bf16[256,512]{1,0:T(8,128)(2,1)S(1)}, bf16[256,512]{1,0:T(8,128)(2,1)}, u32[]{:S(2)}) copy-start(bf16[256,512]{1,0:T(8,128)(2,1)} %get-tuple-element.55) | copy-start | bytes 786436
  31.4 4.4 %copy-start.14 = (bf16[256,2,256]{2,1,0:T(2,128)(2,1)}, bf16[256,2,256]{2,1,0:T(2,128)(2,1)S(1)}, u32[]{:S(2)}) copy-start(bf16[256,2,256]{2,1,0:T(2,128)(2,1)S(1)} %collective-permute-done.5.refs_4_) | copy-start | bytes 786436
  31.4 5.4 %copy-start.15 = (bf16[256,2,256]{2,1,0:T(2,128)(2,1)S(1)}, bf16[256,2,256]{2,1,0:T(2,128)(2,1)}, u32[]{:S(2)}) copy-start(bf16[256,2,256]{2,1,0:T(2,128)(2,1)} %get-tuple-element.60.refs_3_) | copy-start | bytes 786436
  31.4 1.8 %collective-permute-start.7 = (bf16[256,512]{1,0:T(8,128)(2,1)}, bf16[256,512]{1,0:T(8,128)(2,1)S(1)}, u32[]{:S(2)}, u32[]{:S(2)}) collective-permute-start(bf16[256,512]{1,0:T(8,128)(2,1)} %get-tuple-element.52), channel_id=1, source_target_pairs={{0,1},{1,0},{2,3},{3,2},{4,5},{5,4},{6,7},{7,6},{8,9},{9,8},{10,11... | collective-permute-start | bytes 786440 | tf_op jit(solution)/shard_map/ppermute | solution.py:495
  34.2 18.3 %collective-permute-start.12 = (bf16[256,2,256]{2,1,0:T(2,128)(2,1)S(1)}, bf16[256,2,256]{2,1,0:T(2,128)(2,1)S(1)}, u32[]{:S(2)}, u32[]{:S(2)}) collective-permute-start(bf16[256,2,256]{2,1,0:T(2,128)(2,1)S(1)} %collective-permute-done.5.refs_4_), channel_id=1, source_target_pairs={{0,4},{4,0},{8,12},{12,8},{16,20},{20,16},{24,28},{28,24},{1,5},{5... | collective-permute-start | bytes 786440 | tf_op jit(solution)/shard_map/ppermute | solution.py:507
  35.8 16.7 %collective-permute-start.10 = (bf16[256,2,256]{2,1,0:T(2,128)(2,1)S(1)}, bf16[256,2,256]{2,1,0:T(2,128)(2,1)S(1)}, u32[]{:S(2)}, u32[]{:S(2)}) collective-permute-start(bf16[256,2,256]{2,1,0:T(2,128)(2,1)S(1)} %collective-permute-done.5.refs_4_), channel_id=1, source_target_pairs={{0,8},{4,12},{8,16},{12,20},{16,24},{20,28},{24,0},{28,4},{1,9},{5... | collective-permute-start | bytes 786440 | tf_op jit(solution)/shard_map/ppermute | solution.py:504
  36.8 15.4 %copy-start.4 = (bf16[128,2048]{1,0:T(8,128)(2,1)S(1)}, bf16[128,2048]{1,0:T(8,128)(2,1)}, u32[]{:S(2)}) copy-start(bf16[128,2048]{1,0:T(8,128)(2,1)} %refs_0_.1) | copy-start | bytes 1572868
  36.8 15.7 %collective-permute-start.13 = (bf16[256,2,256]{2,1,0:T(2,128)(2,1)S(1)}, bf16[256,2,256]{2,1,0:T(2,128)(2,1)S(1)}, u32[]{:S(2)}, u32[]{:S(2)}) collective-permute-start(bf16[256,2,256]{2,1,0:T(2,128)(2,1)S(1)} %copy-done.15), channel_id=1, source_target_pairs={{0,4},{4,0},{8,12},{12,8},{16,20},{20,16},{24,28},{28,24},{1,5},{5... | collective-permute-start | bytes 786440 | tf_op jit(solution)/shard_map/ppermute | solution.py:507
  37.8 14.7 %collective-permute-start.11 = (bf16[256,2,256]{2,1,0:T(2,128)(2,1)S(1)}, bf16[256,2,256]{2,1,0:T(2,128)(2,1)S(1)}, u32[]{:S(2)}, u32[]{:S(2)}) collective-permute-start(bf16[256,2,256]{2,1,0:T(2,128)(2,1)S(1)} %copy-done.15), channel_id=1, source_target_pairs={{0,8},{4,12},{8,16},{12,20},{16,24},{20,28},{24,0},{28,4},{1,9},{5... | collective-permute-start | bytes 786440 | tf_op jit(solution)/shard_map/ppermute | solution.py:504
  39.4 12.8 %collective-permute-start.9 = (bf16[128,2048]{1,0:T(8,128)(2,1)S(1)}, bf16[128,2048]{1,0:T(8,128)(2,1)S(1)}, u32[]{:S(2)}, u32[]{:S(2)}) collective-permute-start(bf16[128,2048]{1,0:T(8,128)(2,1)S(1)} %fusion), channel_id=1, source_target_pairs={{0,2},{1,3},{2,0},{3,1},{4,6},{5,7},{6,4},{7,5},{8,10},{9,11},{10,... | collective-permute-start | bytes 1572872 | tf_op jit(solution)/shard_map/ppermute | solution.py:501
  40.4 16.7 %copy-start.24 = (bf16[2048]{0:T(1024)(128)(2,1)S(1)}, bf16[2048]{0:T(1024)(128)(2,1)}, u32[]{:S(2)}) copy-start(bf16[2048]{0:T(1024)(128)(2,1)} %param.28) | copy-start | bytes 12292
  40.4 16.7 %copy-start = (bf16[2048,768]{1,0:T(8,128)(2,1)S(1)}, bf16[2048,768]{1,0:T(8,128)(2,1)}, u32[]{:S(2)}) copy-start(bf16[2048,768]{1,0:T(8,128)(2,1)} %refs_3_.3) | copy-start | bytes 9437188
  40.4 16.7 %copy-start.1 = (bf16[2048,768]{1,0:T(8,128)(2,1)S(1)}, bf16[2048,768]{1,0:T(8,128)(2,1)}, u32[]{:S(2)}) copy-start(bf16[2048,768]{1,0:T(8,128)(2,1)} %refs_4_.5) | copy-start | bytes 9437188
  52.5 4.1 %copy-start.16 = (bf16[256,2,256]{2,1,0:T(2,128)(2,1)}, bf16[256,2,256]{2,1,0:T(2,128)(2,1)S(1)}, u32[]{:S(2)}) copy-start(bf16[256,2,256]{2,1,0:T(2,128)(2,1)S(1)} %collective-permute-done.12.refs_10_) | copy-start | bytes 786436
  52.5 6.7 %copy-start.17 = (bf16[256,2,256]{2,1,0:T(2,128)(2,1)}, bf16[256,2,256]{2,1,0:T(2,128)(2,1)S(1)}, u32[]{:S(2)}) copy-start(bf16[256,2,256]{2,1,0:T(2,128)(2,1)S(1)} %collective-permute-done.10.refs_6_) | copy-start | bytes 786436
  52.5 4.6 %copy-start.18 = (bf16[256,2,256]{2,1,0:T(2,128)(2,1)}, bf16[256,2,256]{2,1,0:T(2,128)(2,1)S(1)}, u32[]{:S(2)}) copy-start(bf16[256,2,256]{2,1,0:T(2,128)(2,1)S(1)} %collective-permute-done.13.refs_9_) | copy-start | bytes 786436
  52.5 6.7 %copy-start.19 = (bf16[256,2,256]{2,1,0:T(2,128)(2,1)}, bf16[256,2,256]{2,1,0:T(2,128)(2,1)S(1)}, u32[]{:S(2)}) copy-start(bf16[256,2,256]{2,1,0:T(2,128)(2,1)S(1)} %collective-permute-done.11.refs_5_) | copy-start | bytes 786436
  52.5 4.0 %collective-permute-start.14 = (bf16[128,2048]{1,0:T(8,128)(2,1)S(1)}, bf16[128,2048]{1,0:T(8,128)(2,1)S(1)}, u32[]{:S(2)}, u32[]{:S(2)}) collective-permute-start(bf16[128,2048]{1,0:T(8,128)(2,1)S(1)} %add_convert_fusion.1.refs_0_), channel_id=1, source_target_pairs={{0,1},{1,0},{2,3},{3,2},{4,5},{5,4},{6,7},{7,6},{8,9},{9,8},{10,11... | collective-permute-start | bytes 1572872 | tf_op jit(solution)/shard_map/ppermute | solution.py:495
  52.6 14.3 %collective-permute-start.16 = (bf16[128,2048]{1,0:T(8,128)(2,1)S(1)}, bf16[128,2048]{1,0:T(8,128)(2,1)S(1)}, u32[]{:S(2)}, u32[]{:S(2)}) collective-permute-start(bf16[128,2048]{1,0:T(8,128)(2,1)S(1)} %add_convert_fusion.1.refs_0_), channel_id=1, source_target_pairs={{0,2},{1,3},{2,0},{3,1},{4,6},{5,7},{6,4},{7,5},{8,10},{9,11},{10,... | collective-permute-start | bytes 1572872 | tf_op jit(solution)/shard_map/ppermute | solution.py:501
  53.2 13.7 %collective-permute-start.17 = (bf16[256,2,256]{2,1,0:T(2,128)(2,1)S(1)}, bf16[256,2,256]{2,1,0:T(2,128)(2,1)S(1)}, u32[]{:S(2)}, u32[]{:S(2)}) collective-permute-start(bf16[256,2,256]{2,1,0:T(2,128)(2,1)S(1)} %collective-permute-done.11.refs_5_), channel_id=1, source_target_pairs={{0,8},{4,12},{8,16},{12,20},{16,24},{20,28},{24,0},{28,4},{1,9},{5... | collective-permute-start | bytes 786440 | tf_op jit(solution)/shard_map/ppermute | solution.py:504
  53.6 15.4 %collective-permute-start.18 = (bf16[256,2,256]{2,1,0:T(2,128)(2,1)S(1)}, bf16[256,2,256]{2,1,0:T(2,128)(2,1)S(1)}, u32[]{:S(2)}, u32[]{:S(2)}) collective-permute-start(bf16[256,2,256]{2,1,0:T(2,128)(2,1)S(1)} %collective-permute-done.10.refs_6_), channel_id=1, source_target_pairs={{0,8},{4,12},{8,16},{12,20},{16,24},{20,28},{24,0},{28,4},{1,9},{5... | collective-permute-start | bytes 786440 | tf_op jit(solution)/shard_map/ppermute | solution.py:504
  55.1 14.0 %collective-permute-start.19 = (bf16[256,2,256]{2,1,0:T(2,128)(2,1)S(1)}, bf16[256,2,256]{2,1,0:T(2,128)(2,1)S(1)}, u32[]{:S(2)}, u32[]{:S(2)}) collective-permute-start(bf16[256,2,256]{2,1,0:T(2,128)(2,1)S(1)} %collective-permute-done.11.refs_5_), channel_id=1, source_target_pairs={{0,4},{4,0},{8,12},{12,8},{16,20},{20,16},{24,28},{28,24},{1,5},{5... | collective-permute-start | bytes 786440 | tf_op jit(solution)/shard_map/ppermute | solution.py:507
  56.6 12.4 %collective-permute-start.20 = (bf16[256,2,256]{2,1,0:T(2,128)(2,1)S(1)}, bf16[256,2,256]{2,1,0:T(2,128)(2,1)S(1)}, u32[]{:S(2)}, u32[]{:S(2)}) collective-permute-start(bf16[256,2,256]{2,1,0:T(2,128)(2,1)S(1)} %collective-permute-done.10.refs_6_), channel_id=1, source_target_pairs={{0,4},{4,0},{8,12},{12,8},{16,20},{20,16},{24,28},{28,24},{1,5},{5... | collective-permute-start | bytes 786440 | tf_op jit(solution)/shard_map/ppermute | solution.py:507
  59.2 12.5 %copy-start.2 = (bf16[768,2048]{1,0:T(8,128)(2,1)S(1)}, bf16[768,2048]{1,0:T(8,128)(2,1)}, u32[]{:S(2)}) copy-start(bf16[768,2048]{1,0:T(8,128)(2,1)} %param.31) | copy-start | bytes 9437188
  67.0 4.1 %collective-permute-start.15 = (bf16[128,768]{1,0:T(8,128)(2,1)S(1)}, bf16[128,768]{1,0:T(8,128)(2,1)S(1)}, u32[]{:S(2)}, u32[]{:S(2)}) collective-permute-start(bf16[128,768]{1,0:T(8,128)(2,1)S(1)} %get-tuple-element.63), channel_id=1, source_target_pairs={{0,1},{1,0},{2,3},{3,2},{4,5},{5,4},{6,7},{7,6},{8,9},{9,8},{10,11... | collective-permute-start | bytes 589832 | tf_op jit(solution)/shard_map/ppermute | solution.py:495
  67.0 5.3 %copy-start.20 = (bf16[256,2,256]{2,1,0:T(2,128)(2,1)}, bf16[256,2,256]{2,1,0:T(2,128)(2,1)S(1)}, u32[]{:S(2)}) copy-start(bf16[256,2,256]{2,1,0:T(2,128)(2,1)S(1)} %collective-permute-done.17.refs_7_) | copy-start | bytes 786436
  69.0 3.3 %copy-start.7 = (bf16[256,2,256]{2,1,0:T(2,128)(2,1)}, bf16[256,2,256]{2,1,0:T(2,128)(2,1)S(1)}, u32[]{:S(2)}) copy-start(bf16[256,2,256]{2,1,0:T(2,128)(2,1)S(1)} %collective-permute-done.18.refs_2_) | copy-start | bytes 786436
  69.0 2.1 %copy-start.21 = (bf16[256,2,256]{2,1,0:T(2,128)(2,1)}, bf16[256,2,256]{2,1,0:T(2,128)(2,1)S(1)}, u32[]{:S(2)}) copy-start(bf16[256,2,256]{2,1,0:T(2,128)(2,1)S(1)} %collective-permute-done.19.refs_11_) | copy-start | bytes 786436
  69.0 9.7 %copy-start.8 = (bf16[256,2,256]{2,1,0:T(2,128)(2,1)}, bf16[256,2,256]{2,1,0:T(2,128)(2,1)S(1)}, u32[]{:S(2)}) copy-start(bf16[256,2,256]{2,1,0:T(2,128)(2,1)S(1)} %collective-permute-done.20.refs_4_) | copy-start | bytes 786436
  69.0 11.3 %collective-permute-start.25 = (bf16[256,2,256]{2,1,0:T(2,128)(2,1)S(1)}, bf16[256,2,256]{2,1,0:T(2,128)(2,1)S(1)}, u32[]{:S(2)}, u32[]{:S(2)}) collective-permute-start(bf16[256,2,256]{2,1,0:T(2,128)(2,1)S(1)} %collective-permute-done.17.refs_7_), channel_id=1, source_target_pairs={{0,4},{4,0},{8,12},{12,8},{16,20},{20,16},{24,28},{28,24},{1,5},{5... | collective-permute-start | bytes 786440 | tf_op jit(solution)/shard_map/ppermute | solution.py:507
  70.1 10.2 %collective-permute-start.24 = (bf16[256,2,256]{2,1,0:T(2,128)(2,1)S(1)}, bf16[256,2,256]{2,1,0:T(2,128)(2,1)}, u32[]{:S(2)}, u32[]{:S(2)}) collective-permute-start(bf16[256,2,256]{2,1,0:T(2,128)(2,1)S(1)} %collective-permute-done.17.refs_7_), channel_id=1, source_target_pairs={{0,8},{4,12},{8,16},{12,20},{16,24},{20,28},{24,0},{28,4},{1,9},{5... | collective-permute-start | bytes 786440 | tf_op jit(solution)/shard_map/ppermute | solution.py:504
  71.1 1.9 %collective-permute-start.21 = (bf16[128,2048]{1,0:T(8,128)(2,1)S(1)}, bf16[128,2048]{1,0:T(8,128)(2,1)S(1)}, u32[]{:S(2)}, u32[]{:S(2)}) collective-permute-start(bf16[128,2048]{1,0:T(8,128)(2,1)S(1)} %collective-permute-done.16.refs_0_), channel_id=1, source_target_pairs={{0,1},{1,0},{2,3},{3,2},{4,5},{5,4},{6,7},{7,6},{8,9},{9,8},{10,11... | collective-permute-start | bytes 1572872 | tf_op jit(solution)/shard_map/ppermute | solution.py:495
  75.0 1.5 %collective-permute-start.22 = (bf16[128,768]{1,0:T(8,128)(2,1)S(1)}, bf16[128,768]{1,0:T(8,128)(2,1)S(1)}, u32[]{:S(2)}, u32[]{:S(2)}) collective-permute-start(bf16[128,768]{1,0:T(8,128)(2,1)S(1)} %get-tuple-element.73), channel_id=1, source_target_pairs={{0,1},{1,0},{2,3},{3,2},{4,5},{5,4},{6,7},{7,6},{8,9},{9,8},{10,11... | collective-permute-start | bytes 589832 | tf_op jit(solution)/shard_map/ppermute | solution.py:495
  77.2 19.3 %collective-permute-start.23 = (bf16[128,2048]{1,0:T(8,128)(2,1)S(1)}, bf16[128,2048]{1,0:T(8,128)(2,1)S(1)}, u32[]{:S(2)}, u32[]{:S(2)}) collective-permute-start(bf16[128,2048]{1,0:T(8,128)(2,1)S(1)} %fusion.1), channel_id=1, source_target_pairs={{0,2},{1,3},{2,0},{3,1},{4,6},{5,7},{6,4},{7,5},{8,10},{9,11},{10,... | collective-permute-start | bytes 1572872 | tf_op jit(solution)/shard_map/ppermute | solution.py:501
  78.7 10.2 %collective-permute-start.26 = (bf16[256,2,256]{2,1,0:T(2,128)(2,1)S(1)}, bf16[256,2,256]{2,1,0:T(2,128)(2,1)S(1)}, u32[]{:S(2)}, u32[]{:S(2)}) collective-permute-start(bf16[256,2,256]{2,1,0:T(2,128)(2,1)S(1)} %collective-permute-done.20.refs_4_), channel_id=1, source_target_pairs={{0,8},{4,12},{8,16},{12,20},{16,24},{20,28},{24,0},{28,4},{1,9},{5... | collective-permute-start | bytes 786440 | tf_op jit(solution)/shard_map/ppermute | solution.py:504
  80.3 8.6 %copy-start.9 = (bf16[256,2,256]{2,1,0:T(2,128)(2,1)}, bf16[256,2,256]{2,1,0:T(2,128)(2,1)S(1)}, u32[]{:S(2)}) copy-start(bf16[256,2,256]{2,1,0:T(2,128)(2,1)S(1)} %collective-permute-done.25.refs_5_) | copy-start | bytes 786436
  80.3 8.7 %collective-permute-start.27 = (bf16[256,2,256]{2,1,0:T(2,128)(2,1)}, bf16[256,2,256]{2,1,0:T(2,128)(2,1)S(1)}, u32[]{:S(2)}, u32[]{:S(2)}) collective-permute-start(bf16[256,2,256]{2,1,0:T(2,128)(2,1)} %collective-permute-done.24.refs_3_), channel_id=1, source_target_pairs={{0,4},{4,0},{8,12},{12,8},{16,20},{20,16},{24,28},{28,24},{1,5},{5... | collective-permute-start | bytes 786440 | tf_op jit(solution)/shard_map/ppermute | solution.py:507
  89.0 0.7 copy-start.10
  89.7 0.7 copy-start.11
